TPU v7x, 32 devices: a whole 2x2x4 slice. The times are simulated.
32 devices in a mesh: rep: 2 (over x), tp: 16 (over z, y, core).
Axes of the slice: x: 2, y: 2, z: 4, core: 2. Of those that a mesh axis runs over, the one named last changes fastest.
Arguments:
- queries: bfloat16 [4, 256, 8192], P(None, 'rep', 'tp'), parts along dimension 1, may hold values from -80 to 80
- key_cache: bfloat16 [256, 12, 1024], P('rep'), parts along dimension 0, may hold values from -4 to 4
- value_cache: bfloat16 [256, 12, 1024], P('rep'), parts along dimension 0, may hold values from -5 to 5
- new_keys: bfloat16 [4, 256, 1024], P(None, 'rep'), parts along dimension 1, may hold values from -5 to 5
- new_values: bfloat16 [4, 256, 1024], P(None, 'rep'), parts along dimension 1, may hold values from -5 to 5
- cache_lengths: int32 [256], P('rep'), parts along dimension 0, may hold values from 2 to 12, as said below
- adapter_ids: int32 [256, 1], P('rep'), parts along dimension 0, may hold values from 0 to 15
- out_weight: bfloat16 [8192, 8192], P('tp'), may hold values from -0.0625 to 0.0625
- shrink_panels: bfloat16 [16, 64, 8192], P('tp'), may hold values from -0.0625 to 0.0625
- expand_panels: bfloat16 [16, 64, 8192], P('tp'), may hold values from -0.75 to 0.75
Outputs:
- outputs: bfloat16 [4, 256, 8192], P(None, 'rep', 'tp'), parts along dimension 1
There are 2 independent parts, one for each index of `rep`. A program takes and returns all parts, laid end to end along the dimension named above; an argument that names none is the same for every part. Nothing has to cross between parts.
Inputs may be any that keep to these rules, and one draw needn't show every extreme that they name: `cache_lengths`: some request has all 12 positions. `adapter_ids`: every adapter serves some request.
All inputs are finite; a program needn't handle non-finite values.
Results may differ from a plain program's by a relative error of at most 0.006.
Values may be sent and summed in bfloat16 or wider, within the bound.
No kernel may reach another device: no remote copies, remote signals or barrier semaphores. Data moves between devices by JAX's collectives and lax.ppermute only.
A program may use at most 128 MiB of HBM per device.

v0:
```python
import jax
import jax.numpy as jnp
from jax import lax
from jax.sharding import PartitionSpec as P

HD = 128
GROUP = 8


def attend_local(query, keys, values, fresh_keys, fresh_values, visible, single_decode_pass):
    request_count, width_local = query.shape
    head_count = width_local // HD
    query_heads = query.reshape(request_count, head_count, HD)
    step_keys = fresh_keys[: single_decode_pass + 1]
    step_values = fresh_values[: single_decode_pass + 1]
    score_scale = 1.0 / jnp.sqrt(jnp.float32(HD))
    cached_scores = (
        jnp.einsum("rhd,rpd->rhp", query_heads, keys, preferred_element_type=jnp.float32)
        * score_scale
    )
    cached_scores = jnp.where(visible[:, None, :], cached_scores, jnp.float32(-1e30))
    fresh_scores = (
        jnp.einsum("rhd,srd->rhs", query_heads, step_keys, preferred_element_type=jnp.float32)
        * score_scale
    )
    highest = jnp.maximum(cached_scores.max(-1), fresh_scores.max(-1))
    cached_exp = jnp.exp(cached_scores - highest[..., None])
    fresh_exp = jnp.exp(fresh_scores - highest[..., None])
    denominator = cached_exp.sum(-1) + fresh_exp.sum(-1)
    cached_weights = (cached_exp / denominator[..., None]).astype(jnp.bfloat16)
    fresh_weights = (fresh_exp / denominator[..., None]).astype(jnp.bfloat16)
    attended = jnp.einsum(
        "rhp,rpd->rhd", cached_weights, values, preferred_element_type=jnp.float32
    )
    attended = attended + jnp.einsum(
        "rhs,srd->rhd", fresh_weights, step_values, preferred_element_type=jnp.float32
    )
    return attended.reshape(request_count, width_local).astype(jnp.bfloat16)


def select_rank(all_ranks, chosen, rank_size):
    request_count, adapter_count = chosen.shape
    return (all_ranks.reshape(request_count, adapter_count, rank_size) * chosen[:, :, None]).sum(1)


def spread_rank(shrunk, chosen):
    request_count, adapter_count = chosen.shape
    distribute_rows = chosen[:, :, None] * shrunk[:, None, :].astype(jnp.float32)
    return distribute_rows.reshape(request_count, adapter_count * shrunk.shape[1]).astype(
        jnp.bfloat16
    )


def complete_decode(summed_output, adapter_product):
    return (summed_output + adapter_product).astype(jnp.bfloat16)


def body(
    queries,
    key_cache,
    value_cache,
    new_keys,
    new_values,
    cache_lengths,
    adapter_ids,
    out_weight,
    shrink_panels,
    expand_panels,
):
    positions = jnp.arange(key_cache.shape[1], dtype=jnp.int32)
    visible = positions[None, :] < cache_lengths[:, None]
    heads_local = queries.shape[2] // HD
    head_start = lax.axis_index("tp") * heads_local // GROUP * HD
    keys_own = lax.dynamic_slice_in_dim(key_cache, head_start, HD, 2)
    values_own = lax.dynamic_slice_in_dim(value_cache, head_start, HD, 2)
    fresh_keys_own = lax.dynamic_slice_in_dim(new_keys, head_start, HD, 2)
    fresh_values_own = lax.dynamic_slice_in_dim(new_values, head_start, HD, 2)
    owned_count, rank_size, full_width = shrink_panels.shape
    shrink_local, expand_local = (
        lax.all_to_all(shrink_panels, "tp", split_axis=2, concat_axis=0, tiled=True),
        lax.all_to_all(expand_panels, "tp", split_axis=2, concat_axis=0, tiled=True),
    )
    adapter_count = shrink_local.shape[0]
    labels = jnp.arange(adapter_count, dtype=jnp.int32)
    shrink_flat = shrink_local.reshape(adapter_count * rank_size, shrink_local.shape[2])
    expand_flattened = expand_local.reshape(adapter_count * rank_size, expand_local.shape[2])
    chosen = (adapter_ids == labels[None, :]).astype(jnp.float32)
    step_outputs = []
    summands = []
    adapter_products = []
    for single_decode_pass in range(queries.shape[0]):
        attended = attend_local(
            queries[single_decode_pass],
            keys_own,
            values_own,
            fresh_keys_own,
            fresh_values_own,
            visible,
            single_decode_pass,
        )
        base_product = jnp.dot(attended, out_weight, preferred_element_type=jnp.float32)
        all_ranks = jnp.einsum(
            "rk,ak->ra", attended, shrink_flat, preferred_element_type=jnp.float32
        )
        partial_rank = select_rank(all_ranks, chosen, rank_size)
        shrunk = lax.psum(partial_rank, "tp").astype(jnp.bfloat16)
        adapter_product = jnp.dot(
            spread_rank(shrunk, chosen), expand_flattened, preferred_element_type=jnp.float32
        )
        summands.append(base_product)
        adapter_products.append(adapter_product)
    stacked_outputs = lax.psum_scatter(jnp.stack(summands), "tp", scatter_dimension=2, tiled=True)
    for single_decode_pass in range(len(summands)):
        step_outputs.append(
            complete_decode(
                stacked_outputs[single_decode_pass], adapter_products[single_decode_pass]
            )
        )
    return jnp.stack(step_outputs)


def solution(mesh):
    return jax.shard_map(
        body,
        mesh=mesh,
        in_specs=(
            P(None, "rep", "tp"),
            P("rep", None, None),
            P("rep", None, None),
            P(None, "rep", None),
            P(None, "rep", None),
            P("rep"),
            P("rep", None),
            P("tp", None),
            P("tp", None, None),
            P("tp", None, None),
        ),
        out_specs=P(None, "rep", "tp"),
        check_vma=False,
    )
```

profile of v0, /device:TPU:0, one launch (start us, length us, event | category | flops | bytes accessed | tf_op | source)
XLA Modules:
  0.0 293.3 jit_solution(3462203197296494981)
XLA Ops:
  21.1 6.9 %convolution_bitcast_fusion.3 = f32[1,128,8192]{2,1,0:T(8,128)} fusion(bf16[512,8192]{1,0:T(8,128)(2,1)} %param.17, bf16[16,8,4,128]{3,2,1,0:T(4,128)(2,1)S(1)} %bitcast.170), kind=kOutput, calls=%fused_computation.4 | convolution fusion | flops 1073741824 | bytes 12713984 | tf_op jit(solution)/shard_map/dot_general | solution.py:101
  28.1 3.2 %convolution_bitcast_fusion.2 = f32[1,128,8192]{2,1,0:T(8,128)} fusion(bf16[512,8192]{1,0:T(8,128)(2,1)S(1)} %bitcast.153, bf16[16,8,4,128]{3,2,1,0:T(4,128)(2,1)S(1)} %bitcast.169), kind=kOutput, calls=%fused_computation.3 | convolution fusion | flops 1073741824 | bytes 12713984 | tf_op jit(solution)/shard_map/dot_general | solution.py:101
  31.8 6.7 %convolution_bitcast_fusion.1 = f32[1,128,8192]{2,1,0:T(8,128)} fusion(bf16[512,8192]{1,0:T(8,128)(2,1)} %param.17, bf16[16,8,4,128]{3,2,1,0:T(4,128)(2,1)S(1)} %bitcast.171), kind=kOutput, calls=%fused_computation.2 | convolution fusion | flops 1073741824 | bytes 12713984 | tf_op jit(solution)/shard_map/dot_general | solution.py:101
  39.7 4.8 %convolution_bitcast_fusion = f32[1,128,8192]{2,1,0:T(8,128)S(1)} fusion(bf16[512,8192]{1,0:T(8,128)(2,1)} %param.17, bf16[16,8,4,128]{3,2,1,0:T(4,128)(2,1)S(1)} %bitcast.172), kind=kOutput, calls=%fused_computation.1 | convolution fusion | flops 1073741824 | bytes 12713984 | tf_op jit(solution)/shard_map/dot_general | solution.py:101
  46.7 6.0 %pad_maximum_fusion = f32[4,128,8192]{2,1,0:T(8,128)} fusion(f32[1,128,8192]{2,1,0:T(8,128)S(1)} %convolution_bitcast_fusion, f32[1,128,8192]{2,1,0:T(8,128)S(1)} %copy-done.2, f32[1,128,8192]{2,1,0:T(8,128)S(1)} %copy-done.1, f32[1,128,8192]{2,1,0:T(8,128)S(1)} %copy-done), kind=kLoop, calls=%fused_computation | loop fusion | flops 12582912 | bytes 33554432 | tf_op jit(solution)/shard_map/stack | solution.py:112
  54.0 6.8 %copy.109 = bf16[1,64,8192]{1,0,2:T(2,128)(2,1)} copy(bf16[1,64,8192]{2,1,0:T(8,128)(2,1)S(1)} %copy-done.3) | data formatting | bytes 2097152 | tf_op args[8]
  61.3 45.2 %reduce = bf16[8192,64]{1,0:T(8,128)(2,1)S(1)} reduce(bf16[8192,1,64]{2,1,0:T(2,128)(2,1)} %bitcast.158, bf16[]{:T(256)} %broadcast.93), dimensions={1}, to_apply=%bitcast.121.reduce_sub_computation | reduce | bytes 2097154
  106.5 2.3 reshape.202
  108.8 7.4 %all-to-all-start = ((bf16[16,2,16384]{2,1,0:T(2,128)(2,1)}), bf16[16,2,16384]{2,1,0:T(2,128)(2,1)S(1)}, u32[]{:S(2)}, u32[]{:S(2)}) async-start(bf16[16,2,16384]{2,1,0:T(2,128)(2,1)} %reshape.202), calls=%async_computation.1 | async-start | bytes 2097152 | tf_op jit(solution)/shard_map/all_to_all | solution.py:80
  116.3 9.2 %copy.112 = bf16[1,64,8192]{1,0,2:T(2,128)(2,1)} copy(bf16[1,64,8192]{2,1,0:T(8,128)(2,1)} %param.19) | data formatting | bytes 2097152 | tf_op args[9]
  125.5 45.2 %reduce.1 = bf16[8192,64]{1,0:T(8,128)(2,1)S(1)} reduce(bf16[8192,1,64]{2,1,0:T(2,128)(2,1)} %bitcast.159, bf16[]{:T(256)} %broadcast.93), dimensions={1}, to_apply=%bitcast.123.reduce_sub_computation | reduce | bytes 2097154
  170.7 2.3 reshape.204
  173.0 6.0 %all-to-all-start.1 = ((bf16[16,2,16384]{2,1,0:T(2,128)(2,1)}), bf16[16,2,16384]{2,1,0:T(2,128)(2,1)}, u32[]{:S(2)}, u32[]{:S(2)}) async-start(bf16[16,2,16384]{2,1,0:T(2,128)(2,1)} %reshape.204), calls=%async_computation.2 | async-start | bytes 2097152 | tf_op jit(solution)/shard_map/all_to_all | solution.py:81
  180.5 1.6 reshape.195
  182.1 7.0 %reshape.203 = bf16[8192,1,64]{2,1,0:T(2,128)(2,1)} reshape(bf16[16,2,16384]{2,1,0:T(2,128)(2,1)S(1)} %all-to-all-done) | data formatting | bytes 2097152
  189.1 2.5 copy.119
  193.8 1.3 fusion.3
  195.2 65.5 %all-reduce.2 = (bf16[128,64]{0,1:T(8,128)(2,1)S(1)}, bf16[128,64]{0,1:T(8,128)(2,1)S(1)}, bf16[128,64]{0,1:T(8,128)(2,1)S(1)}, bf16[128,64]{0,1:T(8,128)(2,1)S(1)}) all-reduce(f32[128,64]{0,1:T(8,128)S(1)} %fusion.3, f32[128,64]{0,1:T(8,128)S(1)} %fusion.2, f32[128,64]{0,1:T(8,128)S(1)} %fusion.1, ...), channel_id=1, replica_groups=mesh['rep'=2,'tp'=16] {'tp'}, use_global_device_ids=true, to_apply=%region_22.23 | all-reduce | flops 32768 | bytes 196608 | tf_op jit(solution)/shard_map/psum | solution.py:106
  260.7 10.2 %reshape.205 = bf16[8192,1,64]{2,1,0:T(2,128)(2,1)} reshape(bf16[16,2,16384]{2,1,0:T(2,128)(2,1)} %all-to-all-done.1) | data formatting | bytes 2097152
  270.9 8.2 %copy.113 = bf16[1,64,8192]{2,1,0:T(8,128)(2,1)S(1)} copy(bf16[1,64,8192]{1,0,2:T(2,128)(2,1)} %bitcast.161) | data formatting | bytes 2097152 | tf_op jit(solution)/shard_map/all_to_all | solution.py:81
  280.4 1.3 fusion.24
  281.7 1.3 fusion.23
  283.0 1.3 fusion.22
  284.3 1.3 fusion.21
  (109 shorter events, 25.8 us)
Async XLA Ops:
  6.5 273.9 %reduce-scatter.2.cloned.1.call-start = ((), (), s32[]{:S(2)}) async-start(), calls=%async_computation.3 | async-start | bytes 17825792 | tf_op jit(solution)/shard_map/reduce_scatter | solution.py:112
  20.6 7.5 %slice-start = ((s8[8388608]{0:T(1024)(128)(4,1)}), s8[4194304]{0:T(1024)(128)(4,1)S(1)}, s32[]{:S(2)}) async-start(s8[8388608]{0:T(1024)(128)(4,1)} %bitcast.152), calls=%async_computation.4 | async-start | bytes 8388608
  21.1 6.9 %slice-start.1 = ((s8[8388608]{0:T(1024)(128)(4,1)}), s8[4194304]{0:T(1024)(128)(4,1)S(1)}, s32[]{:S(2)}) async-start(s8[8388608]{0:T(1024)(128)(4,1)} %bitcast.152), calls=%async_computation.5 | async-start | bytes 8388608
  28.0 3.5 %copy-start.8 = (f32[128,4,128]{2,1,0:T(4,128)S(1)}, f32[128,4,128]{2,1,0:T(4,128)}, u32[]{:S(2)}) copy-start(f32[128,4,128]{2,1,0:T(4,128)} %fusion.31) | copy-start | bytes 786436
  39.0 0.7 copy-start.4
  39.7 4.8 %copy-start = (f32[1,128,8192]{2,1,0:T(8,128)S(1)}, f32[1,128,8192]{2,1,0:T(8,128)}, u32[]{:S(2)}) copy-start(f32[1,128,8192]{2,1,0:T(8,128)} %convolution_bitcast_fusion.3) | copy-start | bytes 12582916
  39.7 5.9 %copy-start.1 = (f32[1,128,8192]{2,1,0:T(8,128)S(1)}, f32[1,128,8192]{2,1,0:T(8,128)}, u32[]{:S(2)}) copy-start(f32[1,128,8192]{2,1,0:T(8,128)} %convolution_bitcast_fusion.2) | copy-start | bytes 12582916
  39.7 7.0 %copy-start.2 = (f32[1,128,8192]{2,1,0:T(8,128)S(1)}, f32[1,128,8192]{2,1,0:T(8,128)}, u32[]{:S(2)}) copy-start(f32[1,128,8192]{2,1,0:T(8,128)} %convolution_bitcast_fusion.1) | copy-start | bytes 12582916
  52.8 1.2 copy-start.3
  108.8 64.2 %all-to-all-start = ((bf16[16,2,16384]{2,1,0:T(2,128)(2,1)}), bf16[16,2,16384]{2,1,0:T(2,128)(2,1)S(1)}, u32[]{:S(2)}, u32[]{:S(2)}) async-start(bf16[16,2,16384]{2,1,0:T(2,128)(2,1)} %reshape.202), calls=%async_computation.1 | async-start | bytes 2097152 | tf_op jit(solution)/shard_map/all_to_all | solution.py:80
  170.7 11.4 %copy-start.7 = (s32[128,1]{0,1:T(1,128)S(1)}, s32[128,1]{0,1:T(1,128)}, u32[]{:S(2)}) copy-start(s32[128,1]{0,1:T(1,128)} %param.16) | copy-start | bytes 1540
  173.0 87.7 %all-to-all-start.1 = ((bf16[16,2,16384]{2,1,0:T(2,128)(2,1)}), bf16[16,2,16384]{2,1,0:T(2,128)(2,1)}, u32[]{:S(2)}, u32[]{:S(2)}) async-start(bf16[16,2,16384]{2,1,0:T(2,128)(2,1)} %reshape.204), calls=%async_computation.2 | async-start | bytes 2097152 | tf_op jit(solution)/shard_map/all_to_all | solution.py:81
  189.1 3.4 %copy-start.5 = (bf16[128,512,1]{1,0,2:T(8,128)(2,1)S(1)}, bf16[128,512,1]{1,0,2:T(8,128)(2,1)}, u32[]{:S(2)}) copy-start(bf16[128,512,1]{1,0,2:T(8,128)(2,1)} %reshape.192) | copy-start | bytes 393220
  191.6 1.7 copy-start.6
Sparse Core Ops, SparseCore 0:
  52.9 217.0 reduce-scatter.1
where the time goes:
time: 295 us; the launch traced here: 293 us
  other arithmetic  100 us (34%)
  blocking collectives  65.5 us (22%)
  local copies, waits for them, and re-layouts  63.5 us (22%)
  matrix products  36.4 us (12%)
  between operations  13.9 us (5%)
  starting transfers between devices  13.5 us (5%)
    unnamed x3, other arithmetic  90.4 us
    psum x1, blocking collectives, body(): shrunk = lax.psum(partial_rank, 'tp').astype(jnp.bfloat16)  65.5 us
    unnamed x33, local copies, waits for them, and re-layouts  45.5 us
    dot_general x4, matrix products, body(): jnp.dot(attended, out_weight, preferred_element_type=jnp.float32)  21.7 us
    all_to_all x3, local copies, waits for them, and re-layouts, body(): lax.all_to_all(expand_panels, 'tp', split_axis=2, concat_axis=0, tiled=True)  8.81 us
    all_to_all x1, starting transfers between devices, body(): lax.all_to_all(shrink_panels, 'tp', split_axis=2, concat_axis=0, tiled=True)  7.44 us
    another operation x1, other arithmetic, body(): jnp.stack(summands)  6.02 us
    all_to_all x1, starting transfers between devices, body(): lax.all_to_all(expand_panels, 'tp', split_axis=2, concat_axis=0, tiled=True)  6.02 us
  transfers between devices with their start and end apart: 3, of which 0 were waited for; matrix products, arithmetic and copies ran while one was open for 50% of the time, Pallas kernels for 0%

commit v1 on v0

v1 whole, which is shorter than its diff:
```python
import functools

import jax
import jax.numpy as jnp
from jax import lax
from jax.experimental import pallas as pl
from jax.experimental.pallas import tpu as pltpu
from jax.sharding import PartitionSpec as P

HD = 128
GROUP_REQ = 16
ROW_CHUNKS = (128, 128, 128, 128)
F32 = jnp.float32
BF16 = jnp.bfloat16


def attention_kernel(head_ref, q_ref, kc_ref, vc_ref, nk_ref, nv_ref, limit_ref, out_ref):
    steps, block_req, width = q_ref.shape
    heads = width // HD
    cached, fresh = kc_ref.shape[0], nk_ref.shape[0]
    group = GROUP_REQ
    rows, columns = steps * heads * group, (cached + fresh) * group
    row = lax.broadcasted_iota(jnp.int32, (rows, columns), 0)
    column = lax.broadcasted_iota(jnp.int32, (rows, columns), 1)
    same = row % group == column % group
    position = column // group
    step = row // (heads * group)
    fresh_ok = jnp.logical_and(position >= cached, position - cached <= step)
    column_position = lax.broadcasted_iota(jnp.int32, (1, columns), 1) // group
    for i in range(block_req // group):
        span = slice(i * group, (i + 1) * group)
        query = jnp.concatenate(
            [q_ref[s, span, h * HD : (h + 1) * HD] for s in range(steps) for h in range(heads)], 0
        )
        keys = jnp.concatenate(
            [kc_ref[p, span, :] for p in range(cached)] + [nk_ref[s, span, :] for s in range(fresh)], 0
        )
        values = jnp.concatenate(
            [vc_ref[p, span, :] for p in range(cached)] + [nv_ref[s, span, :] for s in range(fresh)], 0
        )
        scores = lax.dot_general(
            query, keys, (((1,), (1,)), ((), ())), preferred_element_type=F32
        ) * (1.0 / HD**0.5)
        cached_ok = column_position < limit_ref[i, :, :]
        visible = jnp.logical_and(same, jnp.logical_or(cached_ok, fresh_ok))
        scores = jnp.where(visible, scores, -1e30)
        scaled = jnp.exp(scores - scores.max(-1, keepdims=True))
        weights = (scaled / scaled.sum(-1, keepdims=True)).astype(BF16)
        mixed = jnp.dot(weights, values, preferred_element_type=F32).astype(BF16)
        for s in range(steps):
            for h in range(heads):
                at = (s * heads + h) * group
                out_ref[s, span, h * HD : (h + 1) * HD] = mixed[at : at + group, :]


def attend(queries, key_cache, value_cache, new_keys, new_values, cache_lengths, head):
    steps, requests, width = queries.shape
    cached = key_cache.shape[1]
    columns = (cached + steps) * GROUP_REQ
    limits = jnp.tile(cache_lengths.reshape(-1, 1, GROUP_REQ), (1, 1, cached + steps))
    block = requests // 2
    grid_spec = pltpu.PrefetchScalarGridSpec(
        num_scalar_prefetch=1,
        grid=(requests // block,),
        in_specs=[
            pl.BlockSpec((steps, block, width), lambda i, head: (0, i, 0)),
            pl.BlockSpec((cached, block, HD), lambda i, head: (0, i, head[0])),
            pl.BlockSpec((cached, block, HD), lambda i, head: (0, i, head[0])),
            pl.BlockSpec((steps, block, HD), lambda i, head: (0, i, head[0])),
            pl.BlockSpec((steps, block, HD), lambda i, head: (0, i, head[0])),
            pl.BlockSpec((block // GROUP_REQ, 1, columns), lambda i, head: (i, 0, 0)),
        ],
        out_specs=pl.BlockSpec((steps, block, width), lambda i, head: (0, i, 0)),
    )
    return pl.pallas_call(
        attention_kernel,
        grid_spec=grid_spec,
        out_shape=jax.ShapeDtypeStruct(queries.shape, BF16),
        compiler_params=pltpu.CompilerParams(vmem_limit_bytes=32 << 20),
        cost_estimate=pl.CostEstimate(
            flops=4 * requests * steps * width * columns, bytes_accessed=4 << 20, transcendentals=0
        ),
        name="attention",
    )(
        head.reshape(1),
        queries,
        key_cache.transpose(1, 0, 2),
        value_cache.transpose(1, 0, 2),
        new_keys,
        new_values,
        limits,
    )


def project_kernel(index_ref, a_ref, w_ref, send_ref, keep_ref):
    width = keep_ref.shape[2]
    mine = index_ref[0] % 2
    keep = pl.multiple_of(mine * width, width)
    send = pl.multiple_of((1 - mine) * width, width)
    a = a_ref[...]
    send_ref[0] = jnp.dot(a, w_ref[:, pl.ds(send, width)], preferred_element_type=F32).astype(BF16)
    keep_ref[0] = jnp.dot(a, w_ref[:, pl.ds(keep, width)], preferred_element_type=F32)


def project(index, attended, weight, first_row, rows, pairs, odd):
    depth, full = weight.shape
    width = full // (2 * pairs)
    unit = first_row // rows
    grid_spec = pltpu.PrefetchScalarGridSpec(
        num_scalar_prefetch=1,
        grid=(pairs // 2,),
        in_specs=[
            pl.BlockSpec((rows, depth), lambda i, index: (unit, 0)),
            pl.BlockSpec((depth, 2 * width), lambda i, index: (0, (2 * i + odd) ^ (index[0] // 2))),
        ],
        out_specs=[
            pl.BlockSpec((1, rows, width), lambda i, index: (i, 0, 0)),
            pl.BlockSpec((1, rows, width), lambda i, index: (i, 0, 0)),
        ],
    )
    return pl.pallas_call(
        project_kernel,
        grid_spec=grid_spec,
        out_shape=[
            jax.ShapeDtypeStruct((pairs // 2, rows, width), BF16),
            jax.ShapeDtypeStruct((pairs // 2, rows, width), F32),
        ],
        compiler_params=pltpu.CompilerParams(vmem_limit_bytes=32 << 20),
        cost_estimate=pl.CostEstimate(
            flops=rows * depth * full,
            bytes_accessed=depth * full + 3 * rows * full // 2,
            transcendentals=0,
        ),
        name="project",
    )(index.reshape(1), attended, weight)


def shrink_kernel(ids_ref, a_ref, panel_ref, out_ref):
    rank = out_ref.shape[1]
    ranks = lax.dot_general(
        a_ref[...], panel_ref[...], (((1,), (1,)), ((), ())), preferred_element_type=F32
    )
    owner = lax.broadcasted_iota(jnp.int32, ranks.shape, 1) // rank
    ranks = jnp.where(owner == ids_ref[...], ranks, 0.0)
    total = ranks[:, : 2 * rank]
    for i in range(1, ranks.shape[1] // (2 * rank)):
        total = total + ranks[:, 2 * rank * i : 2 * rank * (i + 1)]
    out_ref[...] = total[:, :rank] + total[:, rank:]


def shrink(ids, attended, panels, rank):
    rows = attended.shape[0]
    return pl.pallas_call(
        shrink_kernel,
        out_shape=jax.ShapeDtypeStruct((rows, rank), F32),
        compiler_params=pltpu.CompilerParams(vmem_limit_bytes=48 << 20),
        cost_estimate=pl.CostEstimate(
            flops=2 * rows * panels.shape[0] * panels.shape[1], bytes_accessed=4 << 20, transcendentals=0
        ),
        name="shrink",
    )(ids, attended, panels)


def expand_kernel(ids_ref, shrunk_ref, panel_ref, out_ref):
    rank = shrunk_ref.shape[1]
    shrunk = shrunk_ref[...].astype(BF16).astype(F32)
    spread = jnp.concatenate([shrunk] * (panel_ref.shape[0] // rank), 1)
    owner = lax.broadcasted_iota(jnp.int32, spread.shape, 1) // rank
    spread = jnp.where(owner == ids_ref[...], spread, 0.0).astype(BF16)
    out_ref[...] = jnp.dot(spread, panel_ref[...], preferred_element_type=F32)


def expand(ids, shrunk, panels):
    rows = shrunk.shape[0]
    return pl.pallas_call(
        expand_kernel,
        out_shape=jax.ShapeDtypeStruct((rows, panels.shape[1]), F32),
        compiler_params=pltpu.CompilerParams(vmem_limit_bytes=48 << 20),
        cost_estimate=pl.CostEstimate(
            flops=2 * rows * panels.shape[0] * panels.shape[1], bytes_accessed=4 << 20, transcendentals=0
        ),
        name="expand",
    )(ids, shrunk, panels)


def swap(array, bit, size):
    return lax.ppermute(array, "tp", [(i, i ^ bit) for i in range(size)])


def own_columns(panel, size):
    width = panel.shape[2] // size
    blocks = jnp.concatenate([panel[:, :, i * width : (i + 1) * width] for i in range(size)], 0)
    mine = lax.all_to_all(blocks, "tp", split_axis=0, concat_axis=0, tiled=True)
    return mine.reshape(-1, width)


def body(
    size,
    queries,
    key_cache,
    value_cache,
    new_keys,
    new_values,
    cache_lengths,
    adapter_ids,
    out_weight,
    shrink_panels,
    expand_panels,
):
    steps, requests, local = queries.shape
    rank = shrink_panels.shape[1]
    rows = steps * requests
    index = lax.axis_index("tp")
    group = size * local // key_cache.shape[2]
    head = index * (local // HD) // group
    shrink_own = own_columns(shrink_panels, size)
    expand_own = own_columns(expand_panels, size)
    ids = jnp.tile(adapter_ids, (steps, 1))
    attended = attend(
        queries, key_cache, value_cache, new_keys, new_values, cache_lengths, head
    ).reshape(rows, local)

    bits = [1 << b for b in range(size.bit_length() - 1)]
    pairs = size // 2
    sums = []
    first = 0
    for count in ROW_CHUNKS:
        send, keep_far = project(index, attended, out_weight, first, count, pairs, 1)
        far = (keep_far + swap(send, bits[0], size).astype(F32)).astype(BF16)
        far = swap(far, bits[1], size)
        send, keep = project(index, attended, out_weight, first, count, pairs, 0)
        near = swap(send, bits[0], size)
        keep = keep + near.astype(F32) + far.astype(F32)
        for bit in bits[2:]:
            blocks = keep.reshape((keep.shape[0] // 2, 2) + keep.shape[1:])
            arrived = swap(blocks[:, 1].astype(BF16), bit, size)
            keep = blocks[:, 0] + arrived.astype(F32)
        sums.append(keep[0])
        first += count

    shrunk = shrink(ids, attended, shrink_own, rank)
    for bit in bits:
        shrunk = shrunk + swap(shrunk, bit, size)
    lora = expand(ids, shrunk, expand_own)
    total = jnp.concatenate(sums, 0) + lora
    return total.astype(BF16).reshape(queries.shape)


def solution(mesh):
    return jax.shard_map(
        functools.partial(body, mesh.shape["tp"]),
        mesh=mesh,
        in_specs=(
            P(None, "rep", "tp"),
            P("rep", None, None),
            P("rep", None, None),
            P(None, "rep", None),
            P(None, "rep", None),
            P("rep"),
            P("rep", None),
            P("tp", None),
            P("tp", None, None),
            P("tp", None, None),
        ),
        out_specs=P(None, "rep", "tp"),
        check_vma=False,
    )
```

time: 295 us -> 179 us (0.61)
  other arithmetic: 100 us -> 14.8 us
  waiting for transfers between devices: 0.04 us -> 69.3 us
  blocking collectives: 65.5 us -> 0 us
  matrix products: 36.4 us -> 0 us
  local copies, waits for them, and re-layouts: 63.5 us -> 34.3 us
  starting transfers between devices: 13.5 us -> 38.5 us
  Pallas kernels: 0 us -> 20.5 us
  between operations: 13.9 us -> 0.65 us
    unnamed x3 -> x0, other arithmetic: 90.4 us -> none
    ppermute x0 -> x24, waiting for transfers between devices: none -> 69.3 us  [swap(): return lax.ppermute(array, 'tp', [(i, i ^ bit) for i in range(size)])]
    psum x1 -> x0, blocking collectives: 65.5 us -> none  [body(): shrunk = lax.psum(partial_rank, 'tp').astype(jnp.bfloat16)]
    dot_general x27 -> x0, matrix products: 36.4 us -> none  [the longest x4 21.7 us: body(): jnp.dot(attended, out_weight, preferred_element_type=jnp.float32)]
    ppermute x0 -> x24, starting transfers between devices: none -> 26.8 us  [swap(): return lax.ppermute(array, 'tp', [(i, i ^ bit) for i in range(size)])]
    pallas_call x0 -> x11, Pallas kernels: none -> 20.5 us  [the longest x8 16.2 us: project(): pl.pallas_call(project_kernel, grid_spec=grid_spec, out_shape=[jax.ShapeD...]
    unnamed x33 -> x94, local copies, waits for them, and re-layouts: 45.5 us -> 28 us
    all_to_all x4 -> x0, local copies, waits for them, and re-layouts: 9.65 us -> none  [the longest x3 8.81 us: body(): lax.all_to_all(expand_panels, 'tp', split_axis=2, concat_axis=0, tiled=True)]
  transfers between devices with their start and end apart: 3 -> 26, of which waited for: 0 -> 10; matrix products, arithmetic and copies ran while one was open for 50% -> 16% of each run, Pallas kernels for 0% -> 8%
where the time goes in v1:
time: 179 us; the launch traced here: 178 us
  waiting for transfers between devices  69.3 us (39%)
  starting transfers between devices  38.5 us (22%)
  local copies, waits for them, and re-layouts  34.3 us (19%)
  Pallas kernels  20.5 us (11%)
  other arithmetic  14.8 us (8%)
    ppermute x24, waiting for transfers between devices, swap(): return lax.ppermute(array, 'tp', [(i, i ^ bit) for i in range(size)])  69.3 us
    unnamed x94, local copies, waits for them, and re-layouts  28 us
    ppermute x24, starting transfers between devices, swap(): return lax.ppermute(array, 'tp', [(i, i ^ bit) for i in range(size)])  26.8 us
    pallas_call x8, Pallas kernels, project(): pl.pallas_call(project_kernel, grid_spec=grid_spec, out_shape=[jax.ShapeD...  16.2 us
    all_to_all x2, starting transfers between devices, own_columns(): mine = lax.all_to_all(blocks, 'tp', split_axis=0, concat_axis=0, tiled=True)  11.7 us
    convert_element_type x4, other arithmetic, body(): far = (keep_far + swap(send, bits[0], size).astype(F32)).astype(BF16)  4.62 us
  transfers between devices with their start and end apart: 26, of which 10 were waited for; matrix products, arithmetic and copies ran while one was open for 16% of the time, Pallas kernels for 8%

profile of v1, /device:TPU:0, one launch (start us, length us, event | category | flops | bytes accessed | tf_op | source)
XLA Modules:
  0.0 178.0 jit_solution(6828540597257917187)
XLA Ops:
  8.1 2.7 %attention.1 = bf16[4,128,512]{2,1,0:T(8,128)(2,1)S(1)} custom-call(s32[1]{0:T(128)} %bitcast.1.head_ref, bf16[4,128,512]{2,1,0:T(8,128)(2,1)S(1)} %copy-done.18, bf16[12,128,1024]{2,1,0:T(8,128)(2,1)S(1)} %bitcast.105, bf16[12,128,1024]{2,1,0:T(8,128)(2,1)S(1)} %bitcast.106, bf16[4,128,1024]{2,1,0:T(8,128)(2,1)S(1)} %copy-done.16, ...), custom_call_target="tpu_custom_call" | custom-call | flops 268435456 | bytes 4194304 | tf_op jit(solution)/shard_map/attention/pallas_call | solution.py:75
  11.5 2.4 %project.13 = (bf16[4,128,512]{2,1,0:T(8,128)(2,1)}, f32[4,128,512]{2,1,0:T(8,128)S(1)}) custom-call(s32[1]{0:T(128)} %bitcast.index_ref, bf16[512,512]{1,0:T(8,128)(2,1)S(1)} %bitcast.94, bf16[512,8192]{1,0:T(8,128)(2,1)S(1)} %copy-done), custom_call_target="tpu_custom_call" | custom-call | flops 536870912 | bytes 5767168 | tf_op jit(solution)/shard_map/project/pallas_call | solution.py:121
  15.3 2.4 %project.12 = (bf16[4,128,512]{2,1,0:T(8,128)(2,1)}, f32[4,128,512]{2,1,0:T(8,128)S(1)}) custom-call(s32[1]{0:T(128)} %bitcast.index_ref, bf16[512,512]{1,0:T(8,128)(2,1)S(1)} %bitcast.95, bf16[512,8192]{1,0:T(8,128)(2,1)S(1)} %copy-done), custom_call_target="tpu_custom_call" | custom-call | flops 536870912 | bytes 5767168 | tf_op jit(solution)/shard_map/project/pallas_call | solution.py:121
  18.8 2.4 %project.11 = (bf16[4,128,512]{2,1,0:T(8,128)(2,1)}, f32[4,128,512]{2,1,0:T(8,128)S(1)}) custom-call(s32[1]{0:T(128)} %bitcast.index_ref, bf16[512,512]{1,0:T(8,128)(2,1)S(1)} %bitcast.96, bf16[512,8192]{1,0:T(8,128)(2,1)S(1)} %copy-done), custom_call_target="tpu_custom_call" | custom-call | flops 536870912 | bytes 5767168 | tf_op jit(solution)/shard_map/project/pallas_call | solution.py:121
  23.4 2.4 %project.9 = (bf16[4,128,512]{2,1,0:T(8,128)(2,1)}, f32[4,128,512]{2,1,0:T(8,128)S(1)}) custom-call(s32[1]{0:T(128)} %bitcast.index_ref, bf16[512,512]{1,0:T(8,128)(2,1)S(1)} %bitcast.98, bf16[512,8192]{1,0:T(8,128)(2,1)S(1)} %copy-done), custom_call_target="tpu_custom_call" | custom-call | flops 536870912 | bytes 5767168 | tf_op jit(solution)/shard_map/project/pallas_call | solution.py:121
  36.2 7.1 %all-to-all-start = ((bf16[16,64,512]{2,1,0:T(8,128)(2,1)}), bf16[16,64,512]{2,1,0:T(8,128)(2,1)S(1)}, u32[]{:S(2)}, u32[]{:S(2)}) async-start(bf16[16,64,512]{2,1,0:T(8,128)(2,1)} %constant_dynamic-update-slice_fusion), calls=%async_computation | async-start | bytes 2097152 | tf_op jit(solution)/shard_map/all_to_all | solution.py:193
  43.3 3.4 %copy-done.1 = bf16[512,8192]{1,0:T(8,128)(2,1)S(1)} copy-done((bf16[512,8192]{1,0:T(8,128)(2,1)S(1)}, bf16[512,8192]{1,0:T(8,128)(2,1)}, u32[]{:S(2)}) %copy-start.1) | copy-done | bytes 8388632
  62.8 2.0 %collective-permute-start.12 = (bf16[4,128,512]{2,1,0:T(8,128)(2,1)S(1)}, bf16[4,128,512]{2,1,0:T(8,128)(2,1)S(1)}, u32[]{:S(2)}, u32[]{:S(2)}) collective-permute-start(bf16[4,128,512]{2,1,0:T(8,128)(2,1)S(1)} %add_convert_fusion.1), channel_id=1, source_target_pairs={{0,2},{1,3},{2,0},{3,1},{4,6},{5,7},{6,4},{7,5},{8,10},{9,11},{10,... | collective-permute-start | bytes 1572872 | tf_op jit(solution)/shard_map/ppermute | solution.py:187
  66.6 11.4 %collective-permute-done.12 = bf16[4,128,512]{2,1,0:T(8,128)(2,1)S(1)} collective-permute-done((bf16[4,128,512]{2,1,0:T(8,128)(2,1)S(1)}, bf16[4,128,512]{2,1,0:T(8,128)(2,1)S(1)}, u32[]{:S(2)}, u32[]{:S(2)}) %collective-permute-start.12) | collective-permute-done | bytes 524320 | tf_op jit(solution)/shard_map/ppermute | solution.py:187
  81.5 7.7 %collective-permute-done.7 = bf16[4,128,512]{2,1,0:T(8,128)(2,1)S(1)} collective-permute-done((bf16[4,128,512]{2,1,0:T(8,128)(2,1)S(1)}, bf16[4,128,512]{2,1,0:T(8,128)(2,1)S(1)}, u32[]{:S(2)}, u32[]{:S(2)}) %collective-permute-start.7) | collective-permute-done | bytes 524320 | tf_op jit(solution)/shard_map/ppermute | solution.py:187
  89.2 2.8 %collective-permute-start.13 = (bf16[2,128,512]{2,1,0:T(8,128)(2,1)S(1)}, bf16[2,128,512]{2,1,0:T(8,128)(2,1)S(1)}, u32[]{:S(2)}, u32[]{:S(2)}) collective-permute-start(bf16[2,128,512]{2,1,0:T(8,128)(2,1)S(1)} %fusion.11), channel_id=1, source_target_pairs={{0,4},{1,5},{2,6},{3,7},{4,0},{5,1},{6,2},{7,3},{8,12},{9,13},{10,... | collective-permute-start | bytes 786440 | tf_op jit(solution)/shard_map/ppermute | solution.py:187
  93.6 6.9 %collective-permute-done.2 = bf16[4,128,512]{2,1,0:T(8,128)(2,1)S(1)} collective-permute-done((bf16[4,128,512]{2,1,0:T(8,128)(2,1)S(1)}, bf16[4,128,512]{2,1,0:T(8,128)(2,1)S(1)}, u32[]{:S(2)}, u32[]{:S(2)}) %collective-permute-start.2) | collective-permute-done | bytes 524320 | tf_op jit(solution)/shard_map/ppermute | solution.py:187
  101.5 2.8 %collective-permute-start.3 = (bf16[2,128,512]{2,1,0:T(8,128)(2,1)}, bf16[2,128,512]{2,1,0:T(8,128)(2,1)}, u32[]{:S(2)}, u32[]{:S(2)}) collective-permute-start(bf16[2,128,512]{2,1,0:T(8,128)(2,1)} %fusion.9), channel_id=1, source_target_pairs={{0,4},{1,5},{2,6},{3,7},{4,0},{5,1},{6,2},{7,3},{8,12},{9,13},{10,... | collective-permute-start | bytes 786440 | tf_op jit(solution)/shard_map/ppermute | solution.py:187
  104.4 7.2 %collective-permute-done.17 = bf16[4,128,512]{2,1,0:T(8,128)(2,1)S(1)} collective-permute-done((bf16[4,128,512]{2,1,0:T(8,128)(2,1)S(1)}, bf16[4,128,512]{2,1,0:T(8,128)(2,1)S(1)}, u32[]{:S(2)}, u32[]{:S(2)}) %collective-permute-start.17) | collective-permute-done | bytes 524320 | tf_op jit(solution)/shard_map/ppermute | solution.py:187
  112.7 2.3 %collective-permute-start.18 = (bf16[2,128,512]{2,1,0:T(8,128)(2,1)}, bf16[2,128,512]{2,1,0:T(8,128)(2,1)}, u32[]{:S(2)}, u32[]{:S(2)}) collective-permute-start(bf16[2,128,512]{2,1,0:T(8,128)(2,1)} %fusion.12), channel_id=1, source_target_pairs={{0,4},{1,5},{2,6},{3,7},{4,0},{5,1},{6,2},{7,3},{8,12},{9,13},{10,... | collective-permute-start | bytes 786440 | tf_op jit(solution)/shard_map/ppermute | solution.py:187
  119.5 4.6 %all-to-all-start.1 = ((bf16[16,64,512]{2,1,0:T(8,128)(2,1)}), bf16[16,64,512]{2,1,0:T(8,128)(2,1)S(1)}, u32[]{:S(2)}, u32[]{:S(2)}) async-start(bf16[16,64,512]{2,1,0:T(8,128)(2,1)} %constant_dynamic-update-slice_fusion.16), calls=%async_computation.1 | async-start | bytes 2097152 | tf_op jit(solution)/shard_map/all_to_all | solution.py:193
  125.5 2.9 %collective-permute-start.4 = (bf16[1,128,512]{2,1,0:T(8,128)(2,1)S(1)}, bf16[1,128,512]{2,1,0:T(8,128)(2,1)S(1)}, u32[]{:S(2)}, u32[]{:S(2)}) collective-permute-start(bf16[1,128,512]{2,1,0:T(8,128)(2,1)S(1)} %fusion.21), channel_id=1, source_target_pairs={{0,8},{1,9},{2,10},{3,11},{4,12},{5,13},{6,14},{7,15},{8,0},{9,1},... | collective-permute-start | bytes 393224 | tf_op jit(solution)/shard_map/ppermute | solution.py:187
  132.2 2.0 %collective-permute-start.21 = (f32[512,64]{1,0:T(8,128)S(1)}, f32[512,64]{1,0:T(8,128)S(1)}, u32[]{:S(2)}, u32[]{:S(2)}) collective-permute-start(f32[512,64]{1,0:T(8,128)S(1)} %add.96), channel_id=1, source_target_pairs={{0,2},{1,3},{2,0},{3,1},{4,6},{5,7},{6,4},{7,5},{8,10},{9,11},{10,... | collective-permute-start | bytes 393224 | tf_op jit(solution)/shard_map/ppermute | solution.py:187
  134.2 3.1 %collective-permute-done.9 = bf16[1,128,512]{2,1,0:T(8,128)(2,1)S(1)} collective-permute-done((bf16[1,128,512]{2,1,0:T(8,128)(2,1)}, bf16[1,128,512]{2,1,0:T(8,128)(2,1)S(1)}, u32[]{:S(2)}, u32[]{:S(2)}) %collective-permute-start.9) | collective-permute-done | bytes 131104 | tf_op jit(solution)/shard_map/ppermute | solution.py:187
  138.0 5.2 %collective-permute-done.21 = f32[512,64]{1,0:T(8,128)S(1)} collective-permute-done((f32[512,64]{1,0:T(8,128)S(1)}, f32[512,64]{1,0:T(8,128)S(1)}, u32[]{:S(2)}, u32[]{:S(2)}) %collective-permute-start.21) | collective-permute-done | bytes 131104 | tf_op jit(solution)/shard_map/ppermute | solution.py:187
  143.3 4.0 %collective-permute-start.22 = (f32[512,64]{1,0:T(8,128)S(1)}, f32[512,64]{1,0:T(8,128)S(1)}, u32[]{:S(2)}, u32[]{:S(2)}) collective-permute-start(f32[512,64]{1,0:T(8,128)S(1)} %add.97), channel_id=1, source_target_pairs={{0,4},{1,5},{2,6},{3,7},{4,0},{5,1},{6,2},{7,3},{8,12},{9,13},{10,... | collective-permute-start | bytes 393224 | tf_op jit(solution)/shard_map/ppermute | solution.py:187
  147.3 18.0 %collective-permute-done.4 = bf16[1,128,512]{2,1,0:T(8,128)(2,1)S(1)} collective-permute-done((bf16[1,128,512]{2,1,0:T(8,128)(2,1)S(1)}, bf16[1,128,512]{2,1,0:T(8,128)(2,1)S(1)}, u32[]{:S(2)}, u32[]{:S(2)}) %collective-permute-start.4) | collective-permute-done | bytes 131104 | tf_op jit(solution)/shard_map/ppermute | solution.py:187
  165.4 5.5 %collective-permute-done.19 = bf16[1,128,512]{2,1,0:T(8,128)(2,1)S(1)} collective-permute-done((bf16[1,128,512]{2,1,0:T(8,128)(2,1)S(1)}, bf16[1,128,512]{2,1,0:T(8,128)(2,1)S(1)}, u32[]{:S(2)}, u32[]{:S(2)}) %collective-permute-start.19) | collective-permute-done | bytes 131104 | tf_op jit(solution)/shard_map/ppermute | solution.py:187
  171.6 3.8 %collective-permute-done.23 = f32[512,64]{1,0:T(8,128)S(1)} collective-permute-done((f32[512,64]{1,0:T(8,128)S(1)}, f32[512,64]{1,0:T(8,128)S(1)}, u32[]{:S(2)}, u32[]{:S(2)}) %collective-permute-start.23) | collective-permute-done | bytes 131104 | tf_op jit(solution)/shard_map/ppermute | solution.py:187
  (169 shorter events, 62.5 us)
Async XLA Ops:
  14.9 44.1 %collective-permute-start.11 = (bf16[4,128,512]{2,1,0:T(8,128)(2,1)}, bf16[4,128,512]{2,1,0:T(8,128)(2,1)}, u32[]{:S(2)}, u32[]{:S(2)}) collective-permute-start(bf16[4,128,512]{2,1,0:T(8,128)(2,1)} %get-tuple-element.32), channel_id=1, source_target_pairs={{0,1},{1,0},{2,3},{3,2},{4,5},{5,4},{6,7},{7,6},{8,9},{9,8},{10,11... | collective-permute-start | bytes 1572872 | tf_op jit(solution)/shard_map/ppermute | solution.py:187
  18.7 47.6 %collective-permute-start.10 = (bf16[4,128,512]{2,1,0:T(8,128)(2,1)}, bf16[4,128,512]{2,1,0:T(8,128)(2,1)}, u32[]{:S(2)}, u32[]{:S(2)}) collective-permute-start(bf16[4,128,512]{2,1,0:T(8,128)(2,1)} %get-tuple-element.30), channel_id=1, source_target_pairs={{0,1},{1,0},{2,3},{3,2},{4,5},{5,4},{6,7},{7,6},{8,9},{9,8},{10,11... | collective-permute-start | bytes 1572872 | tf_op jit(solution)/shard_map/ppermute | solution.py:187
  21.2 39.8 %collective-permute-start.6 = (bf16[4,128,512]{2,1,0:T(8,128)(2,1)}, bf16[4,128,512]{2,1,0:T(8,128)(2,1)}, u32[]{:S(2)}, u32[]{:S(2)}) collective-permute-start(bf16[4,128,512]{2,1,0:T(8,128)(2,1)} %get-tuple-element.28), channel_id=1, source_target_pairs={{0,1},{1,0},{2,3},{3,2},{4,5},{5,4},{6,7},{7,6},{8,9},{9,8},{10,11... | collective-permute-start | bytes 1572872 | tf_op jit(solution)/shard_map/ppermute | solution.py:187
  23.3 58.0 %collective-permute-start.5 = (bf16[4,128,512]{2,1,0:T(8,128)(2,1)S(1)}, bf16[4,128,512]{2,1,0:T(8,128)(2,1)}, u32[]{:S(2)}, u32[]{:S(2)}) collective-permute-start(bf16[4,128,512]{2,1,0:T(8,128)(2,1)S(1)} %get-tuple-element.26), channel_id=1, source_target_pairs={{0,1},{1,0},{2,3},{3,2},{4,5},{5,4},{6,7},{7,6},{8,9},{9,8},{10,11... | collective-permute-start | bytes 1572872 | tf_op jit(solution)/shard_map/ppermute | solution.py:187
  25.8 37.0 %collective-permute-start.1 = (bf16[4,128,512]{2,1,0:T(8,128)(2,1)}, bf16[4,128,512]{2,1,0:T(8,128)(2,1)}, u32[]{:S(2)}, u32[]{:S(2)}) collective-permute-start(bf16[4,128,512]{2,1,0:T(8,128)(2,1)} %get-tuple-element.24), channel_id=1, source_target_pairs={{0,1},{1,0},{2,3},{3,2},{4,5},{5,4},{6,7},{7,6},{8,9},{9,8},{10,11... | collective-permute-start | bytes 1572872 | tf_op jit(solution)/shard_map/ppermute | solution.py:187
  36.2 83.3 %all-to-all-start = ((bf16[16,64,512]{2,1,0:T(8,128)(2,1)}), bf16[16,64,512]{2,1,0:T(8,128)(2,1)S(1)}, u32[]{:S(2)}, u32[]{:S(2)}) async-start(bf16[16,64,512]{2,1,0:T(8,128)(2,1)} %constant_dynamic-update-slice_fusion), calls=%async_computation | async-start | bytes 2097152 | tf_op jit(solution)/shard_map/all_to_all | solution.py:193
  59.0 34.5 %collective-permute-start = (bf16[4,128,512]{2,1,0:T(8,128)(2,1)}, bf16[4,128,512]{2,1,0:T(8,128)(2,1)S(1)}, u32[]{:S(2)}, u32[]{:S(2)}) collective-permute-start(bf16[4,128,512]{2,1,0:T(8,128)(2,1)} %copy-done.19), channel_id=1, source_target_pairs={{0,1},{1,0},{2,3},{3,2},{4,5},{5,4},{6,7},{7,6},{8,9},{9,8},{10,11... | collective-permute-start | bytes 1572872 | tf_op jit(solution)/shard_map/ppermute | solution.py:187
  62.8 15.2 %collective-permute-start.12 = (bf16[4,128,512]{2,1,0:T(8,128)(2,1)S(1)}, bf16[4,128,512]{2,1,0:T(8,128)(2,1)S(1)}, u32[]{:S(2)}, u32[]{:S(2)}) collective-permute-start(bf16[4,128,512]{2,1,0:T(8,128)(2,1)S(1)} %add_convert_fusion.1), channel_id=1, source_target_pairs={{0,2},{1,3},{2,0},{3,1},{4,6},{5,7},{6,4},{7,5},{8,10},{9,11},{10,... | collective-permute-start | bytes 1572872 | tf_op jit(solution)/shard_map/ppermute | solution.py:187
  66.0 38.3 %collective-permute-start.15 = (bf16[4,128,512]{2,1,0:T(8,128)(2,1)S(1)}, bf16[4,128,512]{2,1,0:T(8,128)(2,1)S(1)}, u32[]{:S(2)}, u32[]{:S(2)}) collective-permute-start(bf16[4,128,512]{2,1,0:T(8,128)(2,1)S(1)} %copy-done.21), channel_id=1, source_target_pairs={{0,1},{1,0},{2,3},{3,2},{4,5},{5,4},{6,7},{7,6},{8,9},{9,8},{10,11... | collective-permute-start | bytes 1572872 | tf_op jit(solution)/shard_map/ppermute | solution.py:187
  66.3 22.9 %collective-permute-start.7 = (bf16[4,128,512]{2,1,0:T(8,128)(2,1)S(1)}, bf16[4,128,512]{2,1,0:T(8,128)(2,1)S(1)}, u32[]{:S(2)}, u32[]{:S(2)}) collective-permute-start(bf16[4,128,512]{2,1,0:T(8,128)(2,1)S(1)} %add_convert_fusion.2), channel_id=1, source_target_pairs={{0,2},{1,3},{2,0},{3,1},{4,6},{5,7},{6,4},{7,5},{8,10},{9,11},{10,... | collective-permute-start | bytes 1572872 | tf_op jit(solution)/shard_map/ppermute | solution.py:187
  78.0 22.5 %collective-permute-start.2 = (bf16[4,128,512]{2,1,0:T(8,128)(2,1)S(1)}, bf16[4,128,512]{2,1,0:T(8,128)(2,1)S(1)}, u32[]{:S(2)}, u32[]{:S(2)}) collective-permute-start(bf16[4,128,512]{2,1,0:T(8,128)(2,1)S(1)} %add_convert_fusion.3), channel_id=1, source_target_pairs={{0,2},{1,3},{2,0},{3,1},{4,6},{5,7},{6,4},{7,5},{8,10},{9,11},{10,... | collective-permute-start | bytes 1572872 | tf_op jit(solution)/shard_map/ppermute | solution.py:187
  81.3 30.3 %collective-permute-start.17 = (bf16[4,128,512]{2,1,0:T(8,128)(2,1)S(1)}, bf16[4,128,512]{2,1,0:T(8,128)(2,1)S(1)}, u32[]{:S(2)}, u32[]{:S(2)}) collective-permute-start(bf16[4,128,512]{2,1,0:T(8,128)(2,1)S(1)} %add_convert_fusion), channel_id=1, source_target_pairs={{0,2},{1,3},{2,0},{3,1},{4,6},{5,7},{6,4},{7,5},{8,10},{9,11},{10,... | collective-permute-start | bytes 1572872 | tf_op jit(solution)/shard_map/ppermute | solution.py:187
  89.2 25.8 %collective-permute-start.13 = (bf16[2,128,512]{2,1,0:T(8,128)(2,1)S(1)}, bf16[2,128,512]{2,1,0:T(8,128)(2,1)S(1)}, u32[]{:S(2)}, u32[]{:S(2)}) collective-permute-start(bf16[2,128,512]{2,1,0:T(8,128)(2,1)S(1)} %fusion.11), channel_id=1, source_target_pairs={{0,4},{1,5},{2,6},{3,7},{4,0},{5,1},{6,2},{7,3},{8,12},{9,13},{10,... | collective-permute-start | bytes 786440 | tf_op jit(solution)/shard_map/ppermute | solution.py:187
  93.5 23.7 %collective-permute-start.8 = (bf16[2,128,512]{2,1,0:T(8,128)(2,1)S(1)}, bf16[2,128,512]{2,1,0:T(8,128)(2,1)S(1)}, u32[]{:S(2)}, u32[]{:S(2)}) collective-permute-start(bf16[2,128,512]{2,1,0:T(8,128)(2,1)S(1)} %fusion.10), channel_id=1, source_target_pairs={{0,4},{1,5},{2,6},{3,7},{4,0},{5,1},{6,2},{7,3},{8,12},{9,13},{10,... | collective-permute-start | bytes 786440 | tf_op jit(solution)/shard_map/ppermute | solution.py:187
  101.5 22.6 %collective-permute-start.3 = (bf16[2,128,512]{2,1,0:T(8,128)(2,1)}, bf16[2,128,512]{2,1,0:T(8,128)(2,1)}, u32[]{:S(2)}, u32[]{:S(2)}) collective-permute-start(bf16[2,128,512]{2,1,0:T(8,128)(2,1)} %fusion.9), channel_id=1, source_target_pairs={{0,4},{1,5},{2,6},{3,7},{4,0},{5,1},{6,2},{7,3},{8,12},{9,13},{10,... | collective-permute-start | bytes 786440 | tf_op jit(solution)/shard_map/ppermute | solution.py:187
  112.7 15.7 %collective-permute-start.18 = (bf16[2,128,512]{2,1,0:T(8,128)(2,1)}, bf16[2,128,512]{2,1,0:T(8,128)(2,1)}, u32[]{:S(2)}, u32[]{:S(2)}) collective-permute-start(bf16[2,128,512]{2,1,0:T(8,128)(2,1)} %fusion.12), channel_id=1, source_target_pairs={{0,4},{1,5},{2,6},{3,7},{4,0},{5,1},{6,2},{7,3},{8,12},{9,13},{10,... | collective-permute-start | bytes 786440 | tf_op jit(solution)/shard_map/ppermute | solution.py:187
  115.8 14.9 %collective-permute-start.14 = (bf16[1,128,512]{2,1,0:T(8,128)(2,1)}, bf16[1,128,512]{2,1,0:T(8,128)(2,1)}, u32[]{:S(2)}, u32[]{:S(2)}) collective-permute-start(bf16[1,128,512]{2,1,0:T(8,128)(2,1)} %fusion.23), channel_id=1, source_target_pairs={{0,8},{1,9},{2,10},{3,11},{4,12},{5,13},{6,14},{7,15},{8,0},{9,1},... | collective-permute-start | bytes 393224 | tf_op jit(solution)/shard_map/ppermute | solution.py:187
  117.9 19.4 %collective-permute-start.9 = (bf16[1,128,512]{2,1,0:T(8,128)(2,1)}, bf16[1,128,512]{2,1,0:T(8,128)(2,1)S(1)}, u32[]{:S(2)}, u32[]{:S(2)}) collective-permute-start(bf16[1,128,512]{2,1,0:T(8,128)(2,1)} %fusion.22), channel_id=1, source_target_pairs={{0,8},{1,9},{2,10},{3,11},{4,12},{5,13},{6,14},{7,15},{8,0},{9,1},... | collective-permute-start | bytes 393224 | tf_op jit(solution)/shard_map/ppermute | solution.py:187
  119.5 55.9 %all-to-all-start.1 = ((bf16[16,64,512]{2,1,0:T(8,128)(2,1)}), bf16[16,64,512]{2,1,0:T(8,128)(2,1)S(1)}, u32[]{:S(2)}, u32[]{:S(2)}) async-start(bf16[16,64,512]{2,1,0:T(8,128)(2,1)} %constant_dynamic-update-slice_fusion.16), calls=%async_computation.1 | async-start | bytes 2097152 | tf_op jit(solution)/shard_map/all_to_all | solution.py:193
  125.5 39.8 %collective-permute-start.4 = (bf16[1,128,512]{2,1,0:T(8,128)(2,1)S(1)}, bf16[1,128,512]{2,1,0:T(8,128)(2,1)S(1)}, u32[]{:S(2)}, u32[]{:S(2)}) collective-permute-start(bf16[1,128,512]{2,1,0:T(8,128)(2,1)S(1)} %fusion.21), channel_id=1, source_target_pairs={{0,8},{1,9},{2,10},{3,11},{4,12},{5,13},{6,14},{7,15},{8,0},{9,1},... | collective-permute-start | bytes 393224 | tf_op jit(solution)/shard_map/ppermute | solution.py:187
  129.6 41.3 %collective-permute-start.19 = (bf16[1,128,512]{2,1,0:T(8,128)(2,1)S(1)}, bf16[1,128,512]{2,1,0:T(8,128)(2,1)S(1)}, u32[]{:S(2)}, u32[]{:S(2)}) collective-permute-start(bf16[1,128,512]{2,1,0:T(8,128)(2,1)S(1)} %fusion.24), channel_id=1, source_target_pairs={{0,8},{1,9},{2,10},{3,11},{4,12},{5,13},{6,14},{7,15},{8,0},{9,1},... | collective-permute-start | bytes 393224 | tf_op jit(solution)/shard_map/ppermute | solution.py:187
  132.2 11.0 %collective-permute-start.21 = (f32[512,64]{1,0:T(8,128)S(1)}, f32[512,64]{1,0:T(8,128)S(1)}, u32[]{:S(2)}, u32[]{:S(2)}) collective-permute-start(f32[512,64]{1,0:T(8,128)S(1)} %add.96), channel_id=1, source_target_pairs={{0,2},{1,3},{2,0},{3,1},{4,6},{5,7},{6,4},{7,5},{8,10},{9,11},{10,... | collective-permute-start | bytes 393224 | tf_op jit(solution)/shard_map/ppermute | solution.py:187
  143.3 22.0 %collective-permute-start.22 = (f32[512,64]{1,0:T(8,128)S(1)}, f32[512,64]{1,0:T(8,128)S(1)}, u32[]{:S(2)}, u32[]{:S(2)}) collective-permute-start(f32[512,64]{1,0:T(8,128)S(1)} %add.97), channel_id=1, source_target_pairs={{0,4},{1,5},{2,6},{3,7},{4,0},{5,1},{6,2},{7,3},{8,12},{9,13},{10,... | collective-permute-start | bytes 393224 | tf_op jit(solution)/shard_map/ppermute | solution.py:187
  165.3 10.0 %collective-permute-start.23 = (f32[512,64]{1,0:T(8,128)S(1)}, f32[512,64]{1,0:T(8,128)S(1)}, u32[]{:S(2)}, u32[]{:S(2)}) collective-permute-start(f32[512,64]{1,0:T(8,128)S(1)} %add.98), channel_id=1, source_target_pairs={{0,8},{1,9},{2,10},{3,11},{4,12},{5,13},{6,14},{7,15},{8,0},{9,1},... | collective-permute-start | bytes 393224 | tf_op jit(solution)/shard_map/ppermute | solution.py:187
  (34 other events, 201.2 us)

commit v2 on v0

v2 whole, which is shorter than its diff:
```python
import functools

import jax
import jax.numpy as jnp
from jax import lax
from jax.experimental import pallas as pl
from jax.experimental.pallas import tpu as pltpu
from jax.sharding import PartitionSpec as P

HD = 128
LANES = 128
GROUP_REQ = 16
VMEM_LIMIT = 24 << 20
F32 = jnp.float32
BF16 = jnp.bfloat16
SMALL_PLAN = ((4, (0, 1, 2)), (4, (0, 1, 2)), (2, (0, 1, 2)), (6, (1, 2, 0)))


def call(kernel, name, vmem, hbm, out, cost, after=(), scratch=()):
    operands = [pltpu.with_memory_space_constraint(x, pltpu.VMEM) for x in vmem]
    operands += [pltpu.with_memory_space_constraint(x, pltpu.HBM) for x in hbm]
    count, extra = len(operands), len(after)

    def run(*refs):
        kernel(*refs[:count], *refs[count + extra :])

    return pl.pallas_call(
        run,
        in_specs=[pl.BlockSpec(memory_space=pltpu.VMEM)] * len(vmem)
        + [pl.BlockSpec(memory_space=pltpu.HBM)] * len(hbm)
        + [pl.BlockSpec(memory_space=pl.ANY)] * extra,
        out_specs=[pl.BlockSpec(memory_space=pltpu.VMEM)] * len(out),
        out_shape=[pltpu.VMEM(shape, dtype) for shape, dtype in out],
        scratch_shapes=scratch,
        compiler_params=pltpu.CompilerParams(vmem_limit_bytes=VMEM_LIMIT),
        cost_estimate=pl.CostEstimate(flops=cost, bytes_accessed=1 << 16, transcendentals=0),
        name=name,
    )(*operands, *after)


def put_bit(i, position, value):
    low = i & ((1 << position) - 1)
    return ((i >> position) << (position + 1)) | (value << position) | low


def cut_copies(panel_ref, cut_refs, place, replica):
    groups, share, width = cut_refs[0].shape
    rank = pl.multiple_of(replica * share, share)
    copies = []
    for low, cut_ref in enumerate(cut_refs):
        for high in range(groups):
            column = pl.multiple_of((place ^ (4 * high + low)) * width, width)
            copies.append((panel_ref.at[0, pl.ds(rank, share), pl.ds(column, width)], cut_ref.at[high]))
    return copies


def pick_kernel(w_ref, panel_ref, pick_ref, *rest):
    cut_refs, sems = rest[:-1], rest[-1]
    place, replica = lax.axis_index("tp"), lax.axis_index("rep")
    half, _, width = pick_ref.shape
    pair, other = place // 2, 1 - place % 2
    copies = cut_copies(panel_ref, cut_refs, place, replica)
    for i in range(half):
        column = pl.multiple_of((2 * ((2 * i + 1) ^ pair) + other) * width, width)
        copies.append((w_ref.at[:, pl.ds(column, width)], pick_ref.at[i]))
    copies = [pltpu.make_async_copy(a, b, sems.at[i]) for i, (a, b) in enumerate(copies)]
    for copy in copies:
        copy.start()
    for copy in copies:
        copy.wait()


def pick(weight, panels, pairs, size, replicas):
    depth, full = weight.shape
    width = full // size
    half, share = pairs // 2, panels.shape[1] // replicas
    return call(
        pick_kernel,
        "pick",
        (),
        (weight, panels),
        [((half, depth, width), BF16)] + [((size // 4, share, width), BF16)] * 4,
        0,
        scratch=[pltpu.SemaphoreType.DMA((half + size,))],
    )


def attention_kernel(
    lengths_ref, ids_ref, q_hbm, kc_hbm, vc_hbm, nk_hbm, nv_hbm, w_hbm, panel_hbm,
    out_ref, pick_ref, own_ref, cut0_ref, cut1_ref, cut2_ref, cut3_ref,
    q_ref, kc_ref, vc_ref, nk_ref, nv_ref, q_sems, w_sems,
):
    place, replica = lax.axis_index("tp"), lax.axis_index("rep")
    steps, requests, width = q_ref.shape
    heads = width // HD
    cached, fresh = kc_ref.shape[0], nk_ref.shape[0]
    block = own_ref.shape[2]
    size = 2 * own_ref.shape[0]
    group_heads = size * width // kc_hbm.shape[2]
    head = pl.multiple_of(place * heads // group_heads * HD, HD)
    parts = 2
    part = requests // parts
    loads = []
    for n in range(parts):
        span = pl.ds(n * part, part)
        pieces = [(q_hbm.at[:, span, :], q_ref.at[:, span, :])]
        for a, b in ((kc_hbm, kc_ref), (nk_hbm, nk_ref), (vc_hbm, vc_ref), (nv_hbm, nv_ref)):
            pieces.append((a.at[:, span, pl.ds(head, HD)], b.at[:, span, :]))
        loads.append([pltpu.make_async_copy(a, b, q_sems.at[n, i]) for i, (a, b) in enumerate(pieces)])
    pair, mine = place // 2, place % 2
    others = cut_copies(panel_hbm, (cut0_ref, cut1_ref, cut2_ref, cut3_ref), place, replica)
    for i in range(pick_ref.shape[0]):
        column = pl.multiple_of((2 * ((2 * i) ^ pair) + 1 - mine) * block, block)
        others.append((w_hbm.at[:, pl.ds(column, block)], pick_ref.at[i]))
    for i in range(own_ref.shape[0]):
        column = pl.multiple_of((2 * (i ^ pair) + mine) * block, block)
        others.append((w_hbm.at[:, pl.ds(column, block)], own_ref.at[i]))
    others = [pltpu.make_async_copy(a, b, w_sems.at[i]) for i, (a, b) in enumerate(others)]
    for copy in [c for load in loads for c in load] + others:
        copy.start()

    group = GROUP_REQ
    rows, columns = steps * heads * group, (cached + fresh) * group
    row = lax.broadcasted_iota(jnp.int32, (rows, columns), 0)
    column = lax.broadcasted_iota(jnp.int32, (rows, columns), 1)
    same = row % group == column % group
    position = column // group
    step = row // (heads * group)
    fresh_ok = jnp.logical_and(position >= cached, position - cached <= step)
    column_position = lax.broadcasted_iota(jnp.int32, (1, columns), 1) // group
    tail = lax.broadcasted_iota(jnp.int32, (group, requests), 0) == 0
    out_ref[steps * requests :, :] = jnp.zeros((group, width), BF16)
    out_ref[steps * requests :, :requests] = jnp.where(tail, ids_ref[...].astype(F32), 0.0).astype(BF16)
    for n in range(parts):
        for copy in loads[n]:
            copy.wait()
        for i in range(n * part // group, (n + 1) * part // group):
            span = slice(i * group, (i + 1) * group)
            query = jnp.concatenate(
                [q_ref[s, span, h * HD : (h + 1) * HD] for s in range(steps) for h in range(heads)], 0
            )
            keys = jnp.concatenate(
                [kc_ref[p, span, :] for p in range(cached)] + [nk_ref[s, span, :] for s in range(fresh)], 0
            )
            values = jnp.concatenate(
                [vc_ref[p, span, :] for p in range(cached)] + [nv_ref[s, span, :] for s in range(fresh)], 0
            )
            scores = lax.dot_general(
                query, keys, (((1,), (1,)), ((), ())), preferred_element_type=F32
            ) * (1.0 / HD**0.5)
            limit = jnp.concatenate([lengths_ref[:, span]] * (cached + fresh), 1)
            cached_ok = column_position < limit
            visible = jnp.logical_and(same, jnp.logical_or(cached_ok, fresh_ok))
            scores = jnp.where(visible, scores, -1e30)
            scaled = jnp.exp(scores - scores.max(-1, keepdims=True))
            weights = (scaled / scaled.sum(-1, keepdims=True)).astype(BF16)
            mixed = jnp.dot(weights, values, preferred_element_type=F32).astype(BF16)
            for s in range(steps):
                for h in range(heads):
                    at = (s * heads + h) * group
                    to = s * requests + i * group
                    out_ref[to : to + group, h * HD : (h + 1) * HD] = mixed[at : at + group, :]
    for copy in others:
        copy.wait()


def attend(
    queries, key_cache, value_cache, new_keys, new_values, cache_lengths, adapter_ids, weight, panels, size, replicas, after
):
    steps, requests, width = queries.shape
    cached = key_cache.shape[1]
    depth, full = weight.shape
    block, pairs, share = full // size, size // 2, panels.shape[1] // replicas
    return call(
        attention_kernel,
        "attention",
        (cache_lengths.reshape(1, -1), adapter_ids.reshape(1, -1)),
        (queries, key_cache.transpose(1, 0, 2), value_cache.transpose(1, 0, 2), new_keys, new_values, weight, panels),
        [
            ((steps * requests + GROUP_REQ, width), BF16),
            ((pairs // 2, depth, block), BF16),
            ((pairs, depth, block), BF16),
        ]
        + [((size // 4, share, block), BF16)] * 4,
        4 * requests * steps * width * (cached + steps) * GROUP_REQ,
        after,
        [
            pltpu.VMEM((steps, requests, width), BF16),
            pltpu.VMEM((cached, requests, HD), BF16),
            pltpu.VMEM((cached, requests, HD), BF16),
            pltpu.VMEM((steps, requests, HD), BF16),
            pltpu.VMEM((steps, requests, HD), BF16),
            pltpu.SemaphoreType.DMA((2, 5)),
            pltpu.SemaphoreType.DMA((pairs // 2 + pairs + size,)),
        ],
    )


def product(span, which, a_ref, b_ref, own_ref, odd_ref, even_ref):
    other = (odd_ref if which % 2 else even_ref)[which // 2]
    return jnp.dot(a_ref[span, :], own_ref[which], preferred_element_type=F32) + jnp.dot(
        b_ref[span, :], other, preferred_element_type=F32
    )


def far_kernel(span, stage, *refs):
    operands, out_ref = refs[:-1], refs[-1]
    for i in range(out_ref.shape[0]):
        out_ref[i] = product(span, put_bit(i, stage, 1), *operands).astype(BF16)


def near_kernel(span, stage, following, *refs):
    operands, (arrived_ref, keep_ref, send_ref) = refs[:-3], refs[-3:]
    for i in range(keep_ref.shape[0]):
        for value, out_ref in ((1, send_ref), (0, keep_ref)):
            at = put_bit(i, following, value)
            total = product(span, put_bit(at, stage, 0), *operands) + arrived_ref[at].astype(F32)
            out_ref[i] = total.astype(out_ref.dtype)


def far(span, stage, operands, after):
    pairs, depth, width = operands[2].shape
    rows = span.stop - span.start
    return call(
        functools.partial(far_kernel, span, stage),
        "far",
        operands,
        (),
        [((pairs // 2, rows, width), BF16)],
        2 * rows * depth * pairs * width,
        after,
    )[0]


def near(span, stage, following, operands, arrived, after):
    pairs, depth, width = operands[2].shape
    rows = span.stop - span.start
    return call(
        functools.partial(near_kernel, span, stage, following),
        "near",
        (*operands, arrived),
        (),
        [((pairs // 4, rows, width), F32), ((pairs // 4, rows, width), BF16)],
        2 * rows * depth * pairs * width,
        after,
    )


def add_kernel(following, keep_ref, arrived_ref, more_ref, send_ref):
    for i in range(more_ref.shape[0]):
        for value, out_ref in ((1, send_ref), (0, more_ref)):
            at = put_bit(i, following, value)
            out_ref[i] = (keep_ref[at] + arrived_ref[at].astype(F32)).astype(out_ref.dtype)


def add(following, keep, arrived):
    shape = (keep.shape[0] // 2,) + keep.shape[1:]
    return call(
        functools.partial(add_kernel, following), "add", (keep, arrived), (), [(shape, F32), (shape, BF16)], 2 * keep.size
    )


def sort_kernel(*refs):
    for high, out_ref in enumerate(refs[4:]):
        for low in range(4):
            out_ref[low] = refs[low][high]


def sort(blocks, after):
    groups, share, width = blocks[0].shape
    return call(sort_kernel, "sort", blocks, (), [((4, share, width), BF16)] * groups, 0, after)


def near_blocks(cuts):
    size = 4 * cuts[0].shape[0]
    first = swap(cuts[1], "tp", 1, size)
    second = swap(cuts[3], "tp", 1, size)
    return (cuts[0], first, swap(cuts[2], "tp", 2, size), swap(second, "tp", 2, size)), second


def far_blocks(sorted_blocks):
    size = 4 * len(sorted_blocks)
    return [sorted_blocks[0]] + [swap(b, "tp", 4 * h, size) for h, b in enumerate(sorted_blocks) if h]


def owners(ids, shape, high, share):
    owner = 4 * high + lax.broadcasted_iota(jnp.int32, shape, 1) // share
    return owner == (ids ^ lax.axis_index("tp"))


def shrink_kernel(steps, groups, *refs):
    panels, attended, out_ref = refs[:groups], refs[groups:-1], refs[-1]
    _, share, width = panels[0].shape
    for k, a_ref in enumerate(attended):
        rows = a_ref.shape[0] - GROUP_REQ
        requests = rows // steps
        row = lax.broadcasted_iota(jnp.int32, (requests, requests), 0)
        column = lax.broadcasted_iota(jnp.int32, (requests, requests), 1)
        line = a_ref[rows : rows + GROUP_REQ, :requests].astype(F32)[:1, :]
        ids = jnp.where(row == column, line, 0.0).sum(1, keepdims=True).astype(jnp.int32)
        ids = jnp.concatenate([ids] * steps, 0)
        total = None
        for high, panel in enumerate(panels):
            flat = panel[...].reshape(4 * share, width)
            ranks = lax.dot_general(
                a_ref[:rows, :], flat, (((1,), (1,)), ((), ())), preferred_element_type=F32
            )
            ranks = jnp.where(owners(ids, ranks.shape, high, share), ranks, 0.0)
            total = ranks if total is None else total + ranks
        part = total[:, :share]
        for i in range(1, 4):
            part = part + total[:, share * i : share * (i + 1)]
        fold = out_ref.shape[1]
        out_ref[k] = jnp.concatenate([part[i * fold : (i + 1) * fold] for i in range(rows // fold)], 1)


def shrink(steps, panels, attended, after):
    rows, share = attended[0].shape[0] - GROUP_REQ, panels[0].shape[1]
    return call(
        functools.partial(shrink_kernel, steps, len(panels)),
        "shrink",
        (*panels, *attended),
        (),
        [((len(attended), rows * share // LANES, LANES), F32)],
        2 * rows * len(attended) * len(panels) * panels[0].size,
        after,
    )[0]


def expand_kernel(steps, replicas, ids_ref, *refs):
    ranks, panels, out_ref = refs[:replicas], refs[replicas:-1], refs[-1]
    groups = len(panels) // replicas
    _, share, width = panels[0].shape
    ids = jnp.concatenate([ids_ref[...]] * steps, 0)
    total = None
    for k, rank_ref in enumerate(ranks):
        folded = rank_ref[0].astype(BF16).astype(F32)
        part = jnp.concatenate([folded[:, i * share : (i + 1) * share] for i in range(LANES // share)], 0)
        part = jnp.concatenate([part] * 4, 1)
        for high, panel in enumerate(panels[k * groups : (k + 1) * groups]):
            spread = jnp.where(owners(ids, part.shape, high, share), part, 0.0).astype(BF16)
            term = jnp.dot(spread, panel[...].reshape(4 * share, width), preferred_element_type=F32)
            total = term if total is None else total + term
    out_ref[...] = total


def expand(steps, ids, ranks, panels, after):
    rows, width = steps * ids.shape[0], panels[0].shape[2]
    return call(
        functools.partial(expand_kernel, steps, len(ranks)),
        "expand",
        (ids, *ranks, *panels),
        (),
        [((rows, width), F32)],
        2 * rows * len(panels) * panels[0].size,
        after,
    )[0]


def finish_kernel(spans, lora_ref, *refs):
    out_ref = refs[-1]
    for n, span in enumerate(spans):
        keep_ref, arrived_ref = refs[2 * n : 2 * n + 2]
        out_ref[span, :] = (keep_ref[0] + arrived_ref[0].astype(F32) + lora_ref[span, :]).astype(BF16)


def finish(spans, lora, sums):
    operands = [pltpu.with_memory_space_constraint(x, pltpu.VMEM) for x in (lora, *sums)]
    return pl.pallas_call(
        functools.partial(finish_kernel, spans),
        in_specs=[pl.BlockSpec(memory_space=pltpu.VMEM)] * len(operands),
        out_specs=pl.BlockSpec(memory_space=pltpu.VMEM),
        out_shape=jax.ShapeDtypeStruct(lora.shape, BF16),
        compiler_params=pltpu.CompilerParams(vmem_limit_bytes=VMEM_LIMIT),
        cost_estimate=pl.CostEstimate(flops=4 * lora.size, bytes_accessed=1 << 20, transcendentals=0),
        name="finish",
    )(*operands)


def swap(array, axis, bit, size):
    return lax.ppermute(array, axis, [(i, i ^ bit) for i in range(size)])


def body(
    size,
    replicas,
    queries,
    key_cache,
    value_cache,
    new_keys,
    new_values,
    cache_lengths,
    adapter_ids,
    out_weight,
    shrink_panels,
    expand_panels,
):
    steps, requests, local = queries.shape
    rows = steps * requests
    pairs = size // 2
    stages = size.bit_length() - 2
    plan = SMALL_PLAN if stages == 3 else ((16, tuple(range(stages))),)
    spans, first = [], 0
    for part, _ in plan:
        spans.append(slice(first, first + rows * part // 16))
        first += rows * part // 16

    picked, *cuts = pick(out_weight, shrink_panels, pairs, size, replicas)
    weight_odd = swap(picked, "tp", 1, size)
    shrink_near, ready = near_blocks(cuts)
    attended, picked, weight_own, *cuts = attend(
        queries, key_cache, value_cache, new_keys, new_values, cache_lengths, adapter_ids,
        out_weight, expand_panels, size, replicas, (ready,),
    )
    attended_other = swap(attended, "tp", 1, size)
    weight_even = swap(picked, "tp", 1, size)
    expand_near, ready = near_blocks(cuts)
    attended_all = [attended] + [swap(attended, "rep", k, replicas) for k in range(1, replicas)]
    operands = (attended, attended_other, weight_own, weight_odd, weight_even)

    def begin(n, after):
        order = plan[n][1]
        sent = far(spans[n], order[0], operands, after)
        return sent, swap(sent, "tp", 2 << order[0], size)

    def middle(n, arrived, after):
        order = plan[n][1]
        following = order[1] - (order[1] > order[0])
        keep, send = near(spans[n], order[0], following, operands, arrived, after)
        return keep, send, swap(send, "tp", 2 << order[1], size)

    def end(n, keep, came, after=()):
        order = plan[n][1]
        for i in range(2, stages):
            left = [s - sum(s > t for t in order[: i]) for s in order[i:]]
            keep, send = add(left[0], keep, came)
            came = swap(send, "tp", 2 << order[i], size)
        return [keep, came]

    last = len(plan) - 1
    started, done = {}, {}
    sent, started[0] = begin(0, (ready,))
    shrink_sorted = sort(shrink_near, (sent,))
    shrink_panels = far_blocks(shrink_sorted)
    token = shrink_sorted[0]
    if last:
        token, started[last] = begin(last, (token,))
        token, started[1] = begin(1, (token,))
    expand_sorted = sort(expand_near, (token,))
    expand_panels = far_blocks(expand_sorted)
    expand_all = list(expand_panels)
    for k in range(1, replicas):
        expand_all += [swap(b, "rep", k, replicas) for b in expand_panels]
    keep, token, came = middle(0, started[0], (expand_sorted[0],))
    done[0] = end(0, keep, came)
    shrunk = shrink(steps, shrink_panels, attended_all, (token,))
    token = shrunk
    for bit in (1, 0, *range(2, stages + 1)):
        shrunk = shrunk + swap(shrunk, "tp", 1 << bit, size)
    if last:
        for n in range(2, last):
            token, started[n] = begin(n, (token,))
        for n in (last, *range(1, last)):
            keep, token, came = middle(n, started[n], (token,))
            done[n] = end(n, keep, came)
    ranks = [shrunk[:1]] + [swap(shrunk[k : k + 1], "rep", k, replicas) for k in range(1, replicas)]
    lora = expand(steps, adapter_ids, ranks, expand_all, (token,))
    sums = [x for n in range(last + 1) for x in done[n]]
    return finish(spans, lora, sums).reshape(queries.shape)


def solution(mesh):
    return jax.shard_map(
        functools.partial(body, mesh.shape["tp"], mesh.shape["rep"]),
        mesh=mesh,
        in_specs=(
            P(None, "rep", "tp"),
            P("rep", None, None),
            P("rep", None, None),
            P(None, "rep", None),
            P(None, "rep", None),
            P("rep"),
            P("rep", None),
            P("tp", None),
            P("tp", None, None),
            P("tp", None, None),
        ),
        out_specs=P(None, "rep", "tp"),
        check_vma=False,
    )
```

time: 295 us -> 122 us (0.41)
  other arithmetic: 100 us -> 0.06 us
  blocking collectives: 65.5 us -> 0 us
  local copies, waits for them, and re-layouts: 63.5 us -> 0.13 us
  waiting for transfers between devices: 0.04 us -> 60.9 us
  matrix products: 36.4 us -> 0 us
  starting transfers between devices: 13.5 us -> 44.3 us
  Pallas kernels: 0 us -> 16.4 us
  between operations: 13.9 us -> 0.25 us
    unnamed x3 -> x0, other arithmetic: 90.4 us -> none
    psum x1 -> x0, blocking collectives: 65.5 us -> none  [body(): shrunk = lax.psum(partial_rank, 'tp').astype(jnp.bfloat16)]
    ppermute x0 -> x39, waiting for transfers between devices: none -> 60.9 us  [swap(): return lax.ppermute(array, axis, [(i, i ^ bit) for i in range(size)])]
    unnamed x33 -> x5, local copies, waits for them, and re-layouts: 45.5 us -> 0.12 us
    ppermute x0 -> x39, starting transfers between devices: none -> 44.3 us  [swap(): return lax.ppermute(array, axis, [(i, i ^ bit) for i in range(size)])]
    dot_general x27 -> x0, matrix products: 36.4 us -> none  [the longest x4 21.7 us: body(): jnp.dot(attended, out_weight, preferred_element_type=jnp.float32)]
    pallas_call x0 -> x19, Pallas kernels: none -> 16.4 us  [the longest x18 15.5 us: call(): pl.pallas_call(run, in_specs=[pl.BlockSpec(memory_space=pltpu.VMEM)] * le...]
    all_to_all x2 -> x0, starting transfers between devices: 13.5 us -> none  [the longest x1 7.44 us: body(): lax.all_to_all(shrink_panels, 'tp', split_axis=2, concat_axis=0, tiled=True)]
  transfers between devices with their start and end apart: 3 -> 39, of which waited for: 0 -> 17; matrix products, arithmetic and copies ran while one was open for 50% -> 0% of each run, Pallas kernels for 0% -> 11%
where the time goes in v2:
time: 122 us
  waiting for transfers between devices  60.9 us (50%)
  starting transfers between devices  44.3 us (36%)
  Pallas kernels  16.4 us (13%)
    ppermute x39, waiting for transfers between devices, swap(): return lax.ppermute(array, axis, [(i, i ^ bit) for i in range(size)])  60.9 us
    ppermute x39, starting transfers between devices, swap(): return lax.ppermute(array, axis, [(i, i ^ bit) for i in range(size)])  44.3 us
    pallas_call x18, Pallas kernels, call(): pl.pallas_call(run, in_specs=[pl.BlockSpec(memory_space=pltpu.VMEM)] * le...  15.5 us
  transfers between devices with their start and end apart: 39, of which 17 were waited for; matrix products, arithmetic and copies ran while one was open for 0% of the time, Pallas kernels for 11%

profile of v2, /device:TPU:0, one launch (start us, length us, event | category | flops | bytes accessed | tf_op | source)
XLA Modules:
  0.0 122.0 jit_solution(12050348994380545572)
XLA Ops:
  0.0 2.0 %pick.1 = (bf16[4,512,512]{2,1,0:T(8,128)(2,1)S(1)}, bf16[4,32,512]{2,1,0:T(8,128)(2,1)S(1)}, bf16[4,32,512]{2,1,0:T(8,128)(2,1)S(1)}, bf16[4,32,512]{2,1,0:T(8,128)(2,1)S(1)}, bf16[4,32,512]{2,1,0:T(8,128)(2,1)S(1)}) custom-call(bf16[512,8192]{1,0:T(8,128)(2,1)} %refs_7_.1, bf16[1,64,8192]{2,1,0:T(8,128)(2,1)} %refs_1_.1), custom_call_target="tpu_custom_call" | custom-call | bytes 65536 | tf_op jit(solution)/shard_map/pick/pallas_call | solution.py:27
  3.5 3.9 %attention.1 = (bf16[528,512]{1,0:T(8,128)(2,1)S(1)}, bf16[4,512,512]{2,1,0:T(8,128)(2,1)S(1)}, bf16[8,512,512]{2,1,0:T(8,128)(2,1)S(1)}, bf16[4,32,512]{2,1,0:T...) custom-call(s32[1,128]{1,0:T(1,128)S(1)} %bitcast.6, ...), custom_call_target="tpu_custom_call" | custom-call | flops 268435456 | bytes 65536 | tf_op jit(solution)/shard_map/attention/pallas_call | solution.py:27
  8.5 4.1 %collective-permute-done.7.refs_5_ = bf16[4,32,512]{2,1,0:T(8,128)(2,1)S(1)} collective-permute-done((bf16[4,32,512]{2,1,0:T(8,128)(2,1)S(1)}, bf16[4,32,512]{2,1,0:T(8,128)(2,1)S(1)}, u32[]{:S(2)}, u32[]{:S(2)}) %collective-permute-start.7) | collective-permute-done | bytes 131104 | tf_op jit(solution)/shard_map/ppermute | solution.py:381
  12.6 2.9 %collective-permute-start.1 = (bf16[4,32,512]{2,1,0:T(8,128)(2,1)S(1)}, bf16[4,32,512]{2,1,0:T(8,128)(2,1)S(1)}, u32[]{:S(2)}, u32[]{:S(2)}) collective-permute-start(bf16[4,32,512]{2,1,0:T(8,128)(2,1)S(1)} %get-tuple-element.43), channel_id=1, source_target_pairs={{0,2},{1,3},{2,0},{3,1},{4,6},{5,7},{6,4},{7,5},{8,10},{9,11},{10,... | collective-permute-start | bytes 393224 | tf_op jit(solution)/shard_map/ppermute | solution.py:381
  15.5 2.0 %collective-permute-start.11 = (bf16[528,512]{1,0:T(8,128)(2,1)S(1)}, bf16[528,512]{1,0:T(8,128)(2,1)S(1)}, u32[]{:S(2)}, u32[]{:S(2)}) collective-permute-start(bf16[528,512]{1,0:T(8,128)(2,1)S(1)} %get-tuple-element.45.refs_0_.refs_4_), channel_id=1, source_target_pairs={{0,16},{16,0},{1,17},{17,1},{2,18},{18,2},{3,19},{19,3},{4,20},{20... | collective-permute-start | bytes 1622024 | tf_op jit(solution)/shard_map/ppermute | solution.py:381
  19.8 2.8 %collective-permute-done.3.refs_3_ = bf16[4,32,512]{2,1,0:T(8,128)(2,1)S(1)} collective-permute-done((bf16[4,32,512]{2,1,0:T(8,128)(2,1)S(1)}, bf16[4,32,512]{2,1,0:T(8,128)(2,1)S(1)}, u32[]{:S(2)}, u32[]{:S(2)}) %collective-permute-start.3) | collective-permute-done | bytes 131104 | tf_op jit(solution)/shard_map/ppermute | solution.py:381
  23.6 2.2 %collective-permute-start.30 = (bf16[4,192,512]{2,1,0:T(8,128)(2,1)S(1)}, bf16[4,192,512]{2,1,0:T(8,128)(2,1)S(1)}, u32[]{:S(2)}, u32[]{:S(2)}) collective-permute-start(bf16[4,192,512]{2,1,0:T(8,128)(2,1)S(1)} %far.5.refs_5_), channel_id=1, source_target_pairs={{0,4},{1,5},{2,6},{3,7},{4,0},{5,1},{6,2},{7,3},{8,12},{9,13},{10,... | collective-permute-start | bytes 2359304 | tf_op jit(solution)/shard_map/ppermute | solution.py:381
  29.4 7.2 %collective-permute-done.14.refs_2_ = bf16[4,32,512]{2,1,0:T(8,128)(2,1)S(1)} collective-permute-done((bf16[4,32,512]{2,1,0:T(8,128)(2,1)S(1)}, bf16[4,32,512]{2,1,0:T(8,128)(2,1)S(1)}, u32[]{:S(2)}, u32[]{:S(2)}) %collective-permute-start.14) | collective-permute-done | bytes 131104 | tf_op jit(solution)/shard_map/ppermute | solution.py:381
  36.6 2.1 %collective-permute-start.29 = (bf16[4,128,512]{2,1,0:T(8,128)(2,1)S(1)}, bf16[4,128,512]{2,1,0:T(8,128)(2,1)S(1)}, u32[]{:S(2)}, u32[]{:S(2)}) collective-permute-start(bf16[4,128,512]{2,1,0:T(8,128)(2,1)S(1)} %far.6.refs_4_), channel_id=1, source_target_pairs={{0,2},{1,3},{2,0},{3,1},{4,6},{5,7},{6,4},{7,5},{8,10},{9,11},{10,... | collective-permute-start | bytes 1572872 | tf_op jit(solution)/shard_map/ppermute | solution.py:381
  39.4 4.1 %collective-permute-start.10 = (bf16[4,32,512]{2,1,0:T(8,128)(2,1)S(1)}, bf16[4,32,512]{2,1,0:T(8,128)(2,1)S(1)}, u32[]{:S(2)}, u32[]{:S(2)}) collective-permute-start(bf16[4,32,512]{2,1,0:T(8,128)(2,1)S(1)} %get-tuple-element.53), channel_id=1, source_target_pairs={{0,12},{1,13},{2,14},{3,15},{4,8},{5,9},{6,10},{7,11},{8,4},{9,5},... | collective-permute-start | bytes 393224 | tf_op jit(solution)/shard_map/ppermute | solution.py:381
  44.9 3.3 %collective-permute-done.10.refs_3_ = bf16[4,32,512]{2,1,0:T(8,128)(2,1)S(1)} collective-permute-done((bf16[4,32,512]{2,1,0:T(8,128)(2,1)S(1)}, bf16[4,32,512]{2,1,0:T(8,128)(2,1)S(1)}, u32[]{:S(2)}, u32[]{:S(2)}) %collective-permute-start.10) | collective-permute-done | bytes 131104 | tf_op jit(solution)/shard_map/ppermute | solution.py:381
  48.2 3.1 %collective-permute-done.8.refs_1_ = bf16[4,32,512]{2,1,0:T(8,128)(2,1)S(1)} collective-permute-done((bf16[4,32,512]{2,1,0:T(8,128)(2,1)S(1)}, bf16[4,32,512]{2,1,0:T(8,128)(2,1)S(1)}, u32[]{:S(2)}, u32[]{:S(2)}) %collective-permute-start.8) | collective-permute-done | bytes 131104 | tf_op jit(solution)/shard_map/ppermute | solution.py:381
  51.3 2.4 %collective-permute-done.9.refs_2_ = bf16[4,32,512]{2,1,0:T(8,128)(2,1)S(1)} collective-permute-done((bf16[4,32,512]{2,1,0:T(8,128)(2,1)S(1)}, bf16[4,32,512]{2,1,0:T(8,128)(2,1)S(1)}, u32[]{:S(2)}, u32[]{:S(2)}) %collective-permute-start.9) | collective-permute-done | bytes 131104 | tf_op jit(solution)/shard_map/ppermute | solution.py:381
  56.7 3.5 %collective-permute-done.16 = f32[2,128,128]{2,1,0:T(8,128)S(1)} collective-permute-done((f32[2,128,128]{2,1,0:T(8,128)S(1)}, f32[2,128,128]{2,1,0:T(8,128)S(1)}, u32[]{:S(2)}, u32[]{:S(2)}) %collective-permute-start.16) | collective-permute-done | bytes 131104 | tf_op jit(solution)/shard_map/ppermute | solution.py:381
  60.4 3.3 %collective-permute-start.22 = (bf16[4,32,512]{2,1,0:T(8,128)(2,1)S(1)}, bf16[4,32,512]{2,1,0:T(8,128)(2,1)S(1)}, u32[]{:S(2)}, u32[]{:S(2)}) collective-permute-start(bf16[4,32,512]{2,1,0:T(8,128)(2,1)S(1)} %get-tuple-element.60), channel_id=1, source_target_pairs={{0,8},{1,9},{2,10},{3,11},{4,12},{5,13},{6,14},{7,15},{8,0},{9,1},... | collective-permute-start | bytes 393224 | tf_op jit(solution)/shard_map/ppermute | solution.py:381
  70.1 8.2 %collective-permute-done.22.refs_5_ = bf16[4,32,512]{2,1,0:T(8,128)(2,1)S(1)} collective-permute-done((bf16[4,32,512]{2,1,0:T(8,128)(2,1)S(1)}, bf16[4,32,512]{2,1,0:T(8,128)(2,1)S(1)}, u32[]{:S(2)}, u32[]{:S(2)}) %collective-permute-start.22) | collective-permute-done | bytes 131104 | tf_op jit(solution)/shard_map/ppermute | solution.py:381
  79.5 2.4 %collective-permute-start.23 = (bf16[4,32,512]{2,1,0:T(8,128)(2,1)S(1)}, bf16[4,32,512]{2,1,0:T(8,128)(2,1)S(1)}, u32[]{:S(2)}, u32[]{:S(2)}) collective-permute-start(bf16[4,32,512]{2,1,0:T(8,128)(2,1)S(1)} %get-tuple-element.61), channel_id=1, source_target_pairs={{0,12},{1,13},{2,14},{3,15},{4,8},{5,9},{6,10},{7,11},{8,4},{9,5},... | collective-permute-start | bytes 393224 | tf_op jit(solution)/shard_map/ppermute | solution.py:381
  81.9 13.4 %collective-permute-done.23.refs_6_ = bf16[4,32,512]{2,1,0:T(8,128)(2,1)S(1)} collective-permute-done((bf16[4,32,512]{2,1,0:T(8,128)(2,1)S(1)}, bf16[4,32,512]{2,1,0:T(8,128)(2,1)S(1)}, u32[]{:S(2)}, u32[]{:S(2)}) %collective-permute-start.23) | collective-permute-done | bytes 131104 | tf_op jit(solution)/shard_map/ppermute | solution.py:381
  99.8 2.4 %collective-permute-done.19 = f32[2,128,128]{2,1,0:T(8,128)S(1)} collective-permute-done((f32[2,128,128]{2,1,0:T(8,128)S(1)}, f32[2,128,128]{2,1,0:T(8,128)S(1)}, u32[]{:S(2)}, u32[]{:S(2)}) %collective-permute-start.19) | collective-permute-done | bytes 131104 | tf_op jit(solution)/shard_map/ppermute | solution.py:381
  103.8 3.1 %collective-permute-start.32 = (bf16[1,128,512]{2,1,0:T(8,128)(2,1)S(1)}, bf16[1,128,512]{2,1,0:T(8,128)(2,1)S(1)}, u32[]{:S(2)}, u32[]{:S(2)}) collective-permute-start(bf16[1,128,512]{2,1,0:T(8,128)(2,1)S(1)} %get-tuple-element.67), channel_id=1, source_target_pairs={{0,8},{1,9},{2,10},{3,11},{4,12},{5,13},{6,14},{7,15},{8,0},{9,1},... | collective-permute-start | bytes 393224 | tf_op jit(solution)/shard_map/ppermute | solution.py:381
  109.1 1.9 %collective-permute-done.35.refs_1_ = bf16[2,64,512]{2,1,0:T(8,128)(2,1)S(1)} collective-permute-done((bf16[2,64,512]{2,1,0:T(8,128)(2,1)S(1)}, bf16[2,64,512]{2,1,0:T(8,128)(2,1)S(1)}, u32[]{:S(2)}, u32[]{:S(2)}) %collective-permute-start.35) | collective-permute-done | bytes 131104 | tf_op jit(solution)/shard_map/ppermute | solution.py:381
  111.5 1.9 %collective-permute-start.36 = (bf16[1,64,512]{2,1,0:T(8,128)(2,1)S(1)}, bf16[1,64,512]{2,1,0:T(8,128)(2,1)S(1)}, u32[]{:S(2)}, u32[]{:S(2)}) collective-permute-start(bf16[1,64,512]{2,1,0:T(8,128)(2,1)S(1)} %get-tuple-element.73), channel_id=1, source_target_pairs={{0,8},{1,9},{2,10},{3,11},{4,12},{5,13},{6,14},{7,15},{8,0},{9,1},... | collective-permute-start | bytes 196616 | tf_op jit(solution)/shard_map/ppermute | solution.py:381
  113.5 1.7 %collective-permute-done.20.refs_2_ = f32[1,128,128]{2,1,0:T(8,128)S(1)} collective-permute-done((f32[1,128,128]{2,1,0:T(8,128)S(1)}, f32[1,128,128]{2,1,0:T(8,128)S(1)}, u32[]{:S(2)}, u32[]{:S(2)}) %collective-permute-start.20) | collective-permute-done | bytes 65568 | tf_op jit(solution)/shard_map/ppermute | solution.py:381
  117.9 3.2 %collective-permute-done.36.refs_5_ = bf16[1,64,512]{2,1,0:T(8,128)(2,1)S(1)} collective-permute-done((bf16[1,64,512]{2,1,0:T(8,128)(2,1)S(1)}, bf16[1,64,512]{2,1,0:T(8,128)(2,1)S(1)}, u32[]{:S(2)}, u32[]{:S(2)}) %collective-permute-start.36) | collective-permute-done | bytes 65568 | tf_op jit(solution)/shard_map/ppermute | solution.py:381
  (83 shorter events, 35.0 us)
Async XLA Ops:
  2.6 13.0 %collective-permute-start.5 = (bf16[4,512,512]{2,1,0:T(8,128)(2,1)S(1)}, bf16[4,512,512]{2,1,0:T(8,128)(2,1)S(1)}, u32[]{:S(2)}, u32[]{:S(2)}) collective-permute-start(bf16[4,512,512]{2,1,0:T(8,128)(2,1)S(1)} %get-tuple-element.47), channel_id=1, source_target_pairs={{0,1},{1,0},{2,3},{3,2},{4,5},{5,4},{6,7},{7,6},{8,9},{9,8},{10,11... | collective-permute-start | bytes 6291464 | tf_op jit(solution)/shard_map/ppermute | solution.py:381
  7.4 10.1 %collective-permute-start.6 = (bf16[4,512,512]{2,1,0:T(8,128)(2,1)S(1)}, bf16[4,512,512]{2,1,0:T(8,128)(2,1)S(1)}, u32[]{:S(2)}, u32[]{:S(2)}) collective-permute-start(bf16[4,512,512]{2,1,0:T(8,128)(2,1)S(1)} %get-tuple-element.48), channel_id=1, source_target_pairs={{0,1},{1,0},{2,3},{3,2},{4,5},{5,4},{6,7},{7,6},{8,9},{9,8},{10,11... | collective-permute-start | bytes 6291464 | tf_op jit(solution)/shard_map/ppermute | solution.py:381
  8.4 11.5 %collective-permute-start = (bf16[4,32,512]{2,1,0:T(8,128)(2,1)S(1)}, bf16[4,32,512]{2,1,0:T(8,128)(2,1)S(1)}, u32[]{:S(2)}, u32[]{:S(2)}) collective-permute-start(bf16[4,32,512]{2,1,0:T(8,128)(2,1)S(1)} %get-tuple-element.42), channel_id=1, source_target_pairs={{0,1},{1,0},{2,3},{3,2},{4,5},{5,4},{6,7},{7,6},{8,9},{9,8},{10,11... | collective-permute-start | bytes 393224 | tf_op jit(solution)/shard_map/ppermute | solution.py:381
  15.5 28.1 %collective-permute-start.11 = (bf16[528,512]{1,0:T(8,128)(2,1)S(1)}, bf16[528,512]{1,0:T(8,128)(2,1)S(1)}, u32[]{:S(2)}, u32[]{:S(2)}) collective-permute-start(bf16[528,512]{1,0:T(8,128)(2,1)S(1)} %get-tuple-element.45.refs_0_.refs_4_), channel_id=1, source_target_pairs={{0,16},{16,0},{1,17},{17,1},{2,18},{18,2},{3,19},{19,3},{4,20},{20... | collective-permute-start | bytes 1622024 | tf_op jit(solution)/shard_map/ppermute | solution.py:381
  18.2 25.4 %collective-permute-start.12 = (bf16[4,128,512]{2,1,0:T(8,128)(2,1)S(1)}, bf16[4,128,512]{2,1,0:T(8,128)(2,1)S(1)}, u32[]{:S(2)}, u32[]{:S(2)}) collective-permute-start(bf16[4,128,512]{2,1,0:T(8,128)(2,1)S(1)} %far.4.refs_4_), channel_id=1, source_target_pairs={{0,2},{1,3},{2,0},{3,1},{4,6},{5,7},{6,4},{7,5},{8,10},{9,11},{10,... | collective-permute-start | bytes 1572872 | tf_op jit(solution)/shard_map/ppermute | solution.py:381
  23.6 40.9 %collective-permute-start.30 = (bf16[4,192,512]{2,1,0:T(8,128)(2,1)S(1)}, bf16[4,192,512]{2,1,0:T(8,128)(2,1)S(1)}, u32[]{:S(2)}, u32[]{:S(2)}) collective-permute-start(bf16[4,192,512]{2,1,0:T(8,128)(2,1)S(1)} %far.5.refs_5_), channel_id=1, source_target_pairs={{0,4},{1,5},{2,6},{3,7},{4,0},{5,1},{6,2},{7,3},{8,12},{9,13},{10,... | collective-permute-start | bytes 2359304 | tf_op jit(solution)/shard_map/ppermute | solution.py:381
  25.8 10.8 %collective-permute-start.14 = (bf16[4,32,512]{2,1,0:T(8,128)(2,1)S(1)}, bf16[4,32,512]{2,1,0:T(8,128)(2,1)S(1)}, u32[]{:S(2)}, u32[]{:S(2)}) collective-permute-start(bf16[4,32,512]{2,1,0:T(8,128)(2,1)S(1)} %get-tuple-element.56), channel_id=1, source_target_pairs={{0,2},{1,3},{2,0},{3,1},{4,6},{5,7},{6,4},{7,5},{8,10},{9,11},{10,... | collective-permute-start | bytes 393224 | tf_op jit(solution)/shard_map/ppermute | solution.py:381
  27.3 12.1 %collective-permute-start.15 = (bf16[4,32,512]{2,1,0:T(8,128)(2,1)S(1)}, bf16[4,32,512]{2,1,0:T(8,128)(2,1)S(1)}, u32[]{:S(2)}, u32[]{:S(2)}) collective-permute-start(bf16[4,32,512]{2,1,0:T(8,128)(2,1)S(1)} %collective-permute-done.7.refs_5_), channel_id=1, source_target_pairs={{0,2},{1,3},{2,0},{3,1},{4,6},{5,7},{6,4},{7,5},{8,10},{9,11},{10,... | collective-permute-start | bytes 393224 | tf_op jit(solution)/shard_map/ppermute | solution.py:381
  36.6 30.5 %collective-permute-start.29 = (bf16[4,128,512]{2,1,0:T(8,128)(2,1)S(1)}, bf16[4,128,512]{2,1,0:T(8,128)(2,1)S(1)}, u32[]{:S(2)}, u32[]{:S(2)}) collective-permute-start(bf16[4,128,512]{2,1,0:T(8,128)(2,1)S(1)} %far.6.refs_4_), channel_id=1, source_target_pairs={{0,2},{1,3},{2,0},{3,1},{4,6},{5,7},{6,4},{7,5},{8,10},{9,11},{10,... | collective-permute-start | bytes 1572872 | tf_op jit(solution)/shard_map/ppermute | solution.py:381
  43.6 10.0 %collective-permute-start.9 = (bf16[4,32,512]{2,1,0:T(8,128)(2,1)S(1)}, bf16[4,32,512]{2,1,0:T(8,128)(2,1)S(1)}, u32[]{:S(2)}, u32[]{:S(2)}) collective-permute-start(bf16[4,32,512]{2,1,0:T(8,128)(2,1)S(1)} %get-tuple-element.52), channel_id=1, source_target_pairs={{0,8},{1,9},{2,10},{3,11},{4,12},{5,13},{6,14},{7,15},{8,0},{9,1},... | collective-permute-start | bytes 393224 | tf_op jit(solution)/shard_map/ppermute | solution.py:381
  60.4 17.9 %collective-permute-start.22 = (bf16[4,32,512]{2,1,0:T(8,128)(2,1)S(1)}, bf16[4,32,512]{2,1,0:T(8,128)(2,1)S(1)}, u32[]{:S(2)}, u32[]{:S(2)}) collective-permute-start(bf16[4,32,512]{2,1,0:T(8,128)(2,1)S(1)} %get-tuple-element.60), channel_id=1, source_target_pairs={{0,8},{1,9},{2,10},{3,11},{4,12},{5,13},{6,14},{7,15},{8,0},{9,1},... | collective-permute-start | bytes 393224 | tf_op jit(solution)/shard_map/ppermute | solution.py:381
  64.5 30.8 %collective-permute-start.28 = (bf16[4,64,512]{2,1,0:T(8,128)(2,1)S(1)}, bf16[4,64,512]{2,1,0:T(8,128)(2,1)S(1)}, u32[]{:S(2)}, u32[]{:S(2)}) collective-permute-start(bf16[4,64,512]{2,1,0:T(8,128)(2,1)S(1)} %far.7.refs_6_), channel_id=1, source_target_pairs={{0,2},{1,3},{2,0},{3,1},{4,6},{5,7},{6,4},{7,5},{8,10},{9,11},{10,... | collective-permute-start | bytes 786440 | tf_op jit(solution)/shard_map/ppermute | solution.py:381
  67.1 36.6 %collective-permute-start.37 = (bf16[2,192,512]{2,1,0:T(8,128)(2,1)S(1)}, bf16[2,192,512]{2,1,0:T(8,128)(2,1)S(1)}, u32[]{:S(2)}, u32[]{:S(2)}) collective-permute-start(bf16[2,192,512]{2,1,0:T(8,128)(2,1)S(1)} %get-tuple-element.62.refs_6_), channel_id=1, source_target_pairs={{0,8},{1,9},{2,10},{3,11},{4,12},{5,13},{6,14},{7,15},{8,0},{9,1},... | collective-permute-start | bytes 1179656 | tf_op jit(solution)/shard_map/ppermute | solution.py:381
  67.2 12.3 %collective-permute-start.18 = (f32[2,128,128]{2,1,0:T(8,128)S(1)}, f32[2,128,128]{2,1,0:T(8,128)S(1)}, u32[]{:S(2)}, u32[]{:S(2)}) collective-permute-start(f32[2,128,128]{2,1,0:T(8,128)S(1)} %add.17), channel_id=1, source_target_pairs={{0,4},{1,5},{2,6},{3,7},{4,0},{5,1},{6,2},{7,3},{8,12},{9,13},{10,... | collective-permute-start | bytes 393224 | tf_op jit(solution)/shard_map/ppermute | solution.py:381
  69.6 27.2 %collective-permute-start.31 = (bf16[2,128,512]{2,1,0:T(8,128)(2,1)S(1)}, bf16[2,128,512]{2,1,0:T(8,128)(2,1)S(1)}, u32[]{:S(2)}, u32[]{:S(2)}) collective-permute-start(bf16[2,128,512]{2,1,0:T(8,128)(2,1)S(1)} %get-tuple-element.58.refs_6_), channel_id=1, source_target_pairs={{0,4},{1,5},{2,6},{3,7},{4,0},{5,1},{6,2},{7,3},{8,12},{9,13},{10,... | collective-permute-start | bytes 786440 | tf_op jit(solution)/shard_map/ppermute | solution.py:381
  78.3 19.0 %collective-permute-start.33 = (bf16[2,128,512]{2,1,0:T(8,128)(2,1)S(1)}, bf16[2,128,512]{2,1,0:T(8,128)(2,1)S(1)}, u32[]{:S(2)}, u32[]{:S(2)}) collective-permute-start(bf16[2,128,512]{2,1,0:T(8,128)(2,1)S(1)} %get-tuple-element.63.refs_6_), channel_id=1, source_target_pairs={{0,4},{1,5},{2,6},{3,7},{4,0},{5,1},{6,2},{7,3},{8,12},{9,13},{10,... | collective-permute-start | bytes 786440 | tf_op jit(solution)/shard_map/ppermute | solution.py:381
  79.5 15.8 %collective-permute-start.23 = (bf16[4,32,512]{2,1,0:T(8,128)(2,1)S(1)}, bf16[4,32,512]{2,1,0:T(8,128)(2,1)S(1)}, u32[]{:S(2)}, u32[]{:S(2)}) collective-permute-start(bf16[4,32,512]{2,1,0:T(8,128)(2,1)S(1)} %get-tuple-element.61), channel_id=1, source_target_pairs={{0,12},{1,13},{2,14},{3,15},{4,8},{5,9},{6,10},{7,11},{8,4},{9,5},... | collective-permute-start | bytes 393224 | tf_op jit(solution)/shard_map/ppermute | solution.py:381
  96.8 10.1 %collective-permute-start.25 = (bf16[4,32,512]{2,1,0:T(8,128)(2,1)S(1)}, bf16[4,32,512]{2,1,0:T(8,128)(2,1)S(1)}, u32[]{:S(2)}, u32[]{:S(2)}) collective-permute-start(bf16[4,32,512]{2,1,0:T(8,128)(2,1)S(1)} %collective-permute-done.21.refs_4_), channel_id=1, source_target_pairs={{0,16},{16,0},{1,17},{17,1},{2,18},{18,2},{3,19},{19,3},{4,20},{20... | collective-permute-start | bytes 393224 | tf_op jit(solution)/shard_map/ppermute | solution.py:381
  97.3 10.1 %collective-permute-start.26 = (bf16[4,32,512]{2,1,0:T(8,128)(2,1)S(1)}, bf16[4,32,512]{2,1,0:T(8,128)(2,1)S(1)}, u32[]{:S(2)}, u32[]{:S(2)}) collective-permute-start(bf16[4,32,512]{2,1,0:T(8,128)(2,1)S(1)} %collective-permute-done.22.refs_5_), channel_id=1, source_target_pairs={{0,16},{16,0},{1,17},{17,1},{2,18},{18,2},{3,19},{19,3},{4,20},{20... | collective-permute-start | bytes 393224 | tf_op jit(solution)/shard_map/ppermute | solution.py:381
  102.2 9.4 %collective-permute-start.27 = (bf16[4,32,512]{2,1,0:T(8,128)(2,1)S(1)}, bf16[4,32,512]{2,1,0:T(8,128)(2,1)S(1)}, u32[]{:S(2)}, u32[]{:S(2)}) collective-permute-start(bf16[4,32,512]{2,1,0:T(8,128)(2,1)S(1)} %collective-permute-done.23.refs_6_), channel_id=1, source_target_pairs={{0,16},{16,0},{1,17},{17,1},{2,18},{18,2},{3,19},{19,3},{4,20},{20... | collective-permute-start | bytes 393224 | tf_op jit(solution)/shard_map/ppermute | solution.py:381
  103.8 14.1 %collective-permute-start.32 = (bf16[1,128,512]{2,1,0:T(8,128)(2,1)S(1)}, bf16[1,128,512]{2,1,0:T(8,128)(2,1)S(1)}, u32[]{:S(2)}, u32[]{:S(2)}) collective-permute-start(bf16[1,128,512]{2,1,0:T(8,128)(2,1)S(1)} %get-tuple-element.67), channel_id=1, source_target_pairs={{0,8},{1,9},{2,10},{3,11},{4,12},{5,13},{6,14},{7,15},{8,0},{9,1},... | collective-permute-start | bytes 393224 | tf_op jit(solution)/shard_map/ppermute | solution.py:381
  106.9 14.2 %collective-permute-start.34 = (bf16[1,128,512]{2,1,0:T(8,128)(2,1)S(1)}, bf16[1,128,512]{2,1,0:T(8,128)(2,1)S(1)}, u32[]{:S(2)}, u32[]{:S(2)}) collective-permute-start(bf16[1,128,512]{2,1,0:T(8,128)(2,1)S(1)} %get-tuple-element.70), channel_id=1, source_target_pairs={{0,8},{1,9},{2,10},{3,11},{4,12},{5,13},{6,14},{7,15},{8,0},{9,1},... | collective-permute-start | bytes 393224 | tf_op jit(solution)/shard_map/ppermute | solution.py:381
  107.5 13.6 %collective-permute-start.38 = (bf16[1,192,512]{2,1,0:T(8,128)(2,1)S(1)}, bf16[1,192,512]{2,1,0:T(8,128)(2,1)S(1)}, u32[]{:S(2)}, u32[]{:S(2)}) collective-permute-start(bf16[1,192,512]{2,1,0:T(8,128)(2,1)S(1)} %get-tuple-element.76), channel_id=1, source_target_pairs={{0,2},{1,3},{2,0},{3,1},{4,6},{5,7},{6,4},{7,5},{8,10},{9,11},{10,... | collective-permute-start | bytes 589832 | tf_op jit(solution)/shard_map/ppermute | solution.py:381
  111.5 9.6 %collective-permute-start.36 = (bf16[1,64,512]{2,1,0:T(8,128)(2,1)S(1)}, bf16[1,64,512]{2,1,0:T(8,128)(2,1)S(1)}, u32[]{:S(2)}, u32[]{:S(2)}) collective-permute-start(bf16[1,64,512]{2,1,0:T(8,128)(2,1)S(1)} %get-tuple-element.73), channel_id=1, source_target_pairs={{0,8},{1,9},{2,10},{3,11},{4,12},{5,13},{6,14},{7,15},{8,0},{9,1},... | collective-permute-start | bytes 196616 | tf_op jit(solution)/shard_map/ppermute | solution.py:381
  (17 other events, 101.3 us)

commit v3 on v2

v3 whole, which is shorter than its diff:
```python
import functools

import jax
import jax.numpy as jnp
from jax import lax
from jax.experimental import pallas as pl
from jax.experimental.pallas import tpu as pltpu
from jax.sharding import PartitionSpec as P

HD = 128
LANES = 128
GROUP_REQ = 16
VMEM_LIMIT = 24 << 20
F32 = jnp.float32
BF16 = jnp.bfloat16
SMALL_PLAN = ((7, (0, 1, 2)), (6, (0, 1, 2)), (3, (1, 0, 2)))


def call(line, kernel, name, vmem, hbm, out, cost, scratch=(), after=()):
    operands = [pltpu.with_memory_space_constraint(x, pltpu.VMEM) for x in vmem]
    operands += [pltpu.with_memory_space_constraint(x, pltpu.HBM) for x in hbm]
    before = [*line, *after]
    count, extra = len(operands), len(before)

    def run(*refs):
        kernel(*refs[:count], *refs[count + extra :])

    results = pl.pallas_call(
        run,
        in_specs=[pl.BlockSpec(memory_space=pltpu.VMEM)] * len(vmem)
        + [pl.BlockSpec(memory_space=pltpu.HBM)] * len(hbm)
        + [pl.BlockSpec(memory_space=pl.ANY)] * extra,
        out_specs=[pl.BlockSpec(memory_space=pltpu.VMEM)] * len(out),
        out_shape=[pltpu.VMEM(shape, dtype) for shape, dtype in out],
        scratch_shapes=scratch,
        compiler_params=pltpu.CompilerParams(vmem_limit_bytes=VMEM_LIMIT),
        cost_estimate=pl.CostEstimate(flops=cost, bytes_accessed=1 << 16, transcendentals=0),
        name=name,
    )(*operands, *before)
    line[:] = [min(results, key=lambda x: x.size)]
    return results


def put_bit(i, position, value):
    low = i & ((1 << position) - 1)
    return ((i >> position) << (position + 1)) | (value << position) | low


def cut_copies(panel_ref, keep_ref, send_ref, panel, place, replica):
    groups, share, width = keep_ref.shape[2:]
    rank = pl.multiple_of(replica * share, share)
    copies = []
    for low, cut_ref in enumerate((keep_ref, keep_ref, send_ref, send_ref)):
        for high in range(groups):
            column = pl.multiple_of((place ^ (4 * high + low)) * width, width)
            copies.append(
                (panel_ref.at[0, pl.ds(rank, share), pl.ds(column, width)], cut_ref.at[low % 2, panel, high])
            )
    return copies


def run_copies(copies, sems):
    copies = [pltpu.make_async_copy(a, b, sems.at[i]) for i, (a, b) in enumerate(copies)]
    for copy in copies:
        copy.start()
    for copy in copies:
        copy.wait()


def pick_kernel(w_ref, shrink_ref, expand_ref, pick_ref, keep_ref, send_ref, sems):
    place, replica = lax.axis_index("tp"), lax.axis_index("rep")
    pairs, _, width = pick_ref.shape
    copies = []
    for i in range(pairs):
        column = pl.multiple_of((2 * (i ^ (place // 2)) + 1 - place % 2) * width, width)
        copies.append((w_ref.at[:, pl.ds(column, width)], pick_ref.at[i]))
    copies += cut_copies(shrink_ref, keep_ref, send_ref, 0, place, replica)
    copies += cut_copies(expand_ref, keep_ref, send_ref, 1, place, replica)
    run_copies(copies, sems)


def pick(line, weight, shrink_panels, expand_panels, size, replicas):
    depth, full = weight.shape
    pairs, width = size // 2, full // size
    cut = ((2, 2, size // 4, shrink_panels.shape[1] // replicas, width), BF16)
    return call(
        line,
        pick_kernel,
        "pick",
        (),
        (weight, shrink_panels, expand_panels),
        [((pairs, depth, width), BF16), cut, cut],
        0,
        scratch=[pltpu.SemaphoreType.DMA((pairs + 2 * size,))],
    )


def attention_kernel(
    lengths_ref, ids_ref, q_hbm, kc_hbm, vc_hbm, nk_hbm, nv_hbm, w_hbm,
    out_ref, own_ref,
    q_ref, kc_ref, vc_ref, nk_ref, nv_ref, q_sems, w_sems,
):
    place = lax.axis_index("tp")
    steps, requests, width = q_ref.shape
    heads = width // HD
    cached, fresh = kc_ref.shape[0], nk_ref.shape[0]
    block = own_ref.shape[2]
    size = 2 * own_ref.shape[0]
    group_heads = size * width // kc_hbm.shape[2]
    head = pl.multiple_of(place * heads // group_heads * HD, HD)
    parts = 2
    part = requests // parts
    loads = []
    for n in range(parts):
        span = pl.ds(n * part, part)
        pieces = [(q_hbm.at[:, span, :], q_ref.at[:, span, :])]
        for a, b in ((kc_hbm, kc_ref), (nk_hbm, nk_ref), (vc_hbm, vc_ref), (nv_hbm, nv_ref)):
            pieces.append((a.at[:, span, pl.ds(head, HD)], b.at[:, span, :]))
        loads.append([pltpu.make_async_copy(a, b, q_sems.at[n, i]) for i, (a, b) in enumerate(pieces)])
    pair, mine = place // 2, place % 2
    others = []
    for i in range(own_ref.shape[0]):
        column = pl.multiple_of((2 * (i ^ pair) + mine) * block, block)
        others.append((w_hbm.at[:, pl.ds(column, block)], own_ref.at[i]))
    others = [pltpu.make_async_copy(a, b, w_sems.at[i]) for i, (a, b) in enumerate(others)]
    for copy in [c for load in loads for c in load] + others:
        copy.start()

    group = GROUP_REQ
    rows, columns = steps * heads * group, (cached + fresh) * group
    row = lax.broadcasted_iota(jnp.int32, (rows, columns), 0)
    column = lax.broadcasted_iota(jnp.int32, (rows, columns), 1)
    same = row % group == column % group
    position = column // group
    step = row // (heads * group)
    fresh_ok = jnp.logical_and(position >= cached, position - cached <= step)
    column_position = lax.broadcasted_iota(jnp.int32, (1, columns), 1) // group
    tail = lax.broadcasted_iota(jnp.int32, (group, requests), 0) == 0
    out_ref[steps * requests :, :] = jnp.zeros((group, width), BF16)
    out_ref[steps * requests :, :requests] = jnp.where(tail, ids_ref[...].astype(F32), 0.0).astype(BF16)
    for n in range(parts):
        for copy in loads[n]:
            copy.wait()
        for i in range(n * part // group, (n + 1) * part // group):
            span = slice(i * group, (i + 1) * group)
            query = jnp.concatenate(
                [q_ref[s, span, h * HD : (h + 1) * HD] for s in range(steps) for h in range(heads)], 0
            )
            keys = jnp.concatenate(
                [kc_ref[p, span, :] for p in range(cached)] + [nk_ref[s, span, :] for s in range(fresh)], 0
            )
            values = jnp.concatenate(
                [vc_ref[p, span, :] for p in range(cached)] + [nv_ref[s, span, :] for s in range(fresh)], 0
            )
            scores = lax.dot_general(
                query, keys, (((1,), (1,)), ((), ())), preferred_element_type=F32
            ) * (1.0 / HD**0.5)
            limit = jnp.concatenate([lengths_ref[:, span]] * (cached + fresh), 1)
            cached_ok = column_position < limit
            visible = jnp.logical_and(same, jnp.logical_or(cached_ok, fresh_ok))
            scores = jnp.where(visible, scores, -1e30)
            scaled = jnp.exp(scores - scores.max(-1, keepdims=True))
            weights = (scaled / scaled.sum(-1, keepdims=True)).astype(BF16)
            mixed = jnp.dot(weights, values, preferred_element_type=F32).astype(BF16)
            for s in range(steps):
                for h in range(heads):
                    at = (s * heads + h) * group
                    to = s * requests + i * group
                    out_ref[to : to + group, h * HD : (h + 1) * HD] = mixed[at : at + group, :]
    for copy in others:
        copy.wait()


def attend(line, queries, key_cache, value_cache, new_keys, new_values, cache_lengths, adapter_ids, weight, size):
    steps, requests, width = queries.shape
    cached = key_cache.shape[1]
    depth, full = weight.shape
    block, pairs = full // size, size // 2
    return call(
        line,
        attention_kernel,
        "attention",
        (cache_lengths.reshape(1, -1), adapter_ids.reshape(1, -1)),
        (queries, key_cache.transpose(1, 0, 2), value_cache.transpose(1, 0, 2), new_keys, new_values, weight),
        [
            ((steps * requests + GROUP_REQ, width), BF16),
            ((pairs, depth, block), BF16),
        ],
        4 * requests * steps * width * (cached + steps) * GROUP_REQ,
        [
            pltpu.VMEM((steps, requests, width), BF16),
            pltpu.VMEM((cached, requests, HD), BF16),
            pltpu.VMEM((cached, requests, HD), BF16),
            pltpu.VMEM((steps, requests, HD), BF16),
            pltpu.VMEM((steps, requests, HD), BF16),
            pltpu.SemaphoreType.DMA((2, 5)),
            pltpu.SemaphoreType.DMA((pairs,)),
        ],
    )


def product(span, which, a_ref, b_ref, own_ref, other_ref):
    return jnp.dot(a_ref[span, :], own_ref[which], preferred_element_type=F32) + jnp.dot(
        b_ref[span, :], other_ref[which], preferred_element_type=F32
    )


def far_kernel(span, stage, *refs):
    operands, out_ref = refs[:-1], refs[-1]
    for i in range(out_ref.shape[0]):
        out_ref[i] = product(span, put_bit(i, stage, 1), *operands).astype(BF16)


def near_kernel(span, stage, following, *refs):
    operands, (arrived_ref, keep_ref, send_ref) = refs[:-3], refs[-3:]
    for i in range(keep_ref.shape[0]):
        for value, out_ref in ((1, send_ref), (0, keep_ref)):
            at = put_bit(i, following, value)
            total = product(span, put_bit(at, stage, 0), *operands) + arrived_ref[at].astype(F32)
            out_ref[i] = total.astype(out_ref.dtype)


def near_all_kernel(span, stage, *refs):
    operands, arrived_ref, out_refs = refs[:4], refs[4], refs[5:]
    for i, out_ref in enumerate(out_refs):
        total = product(span, put_bit(i, stage, 0), *operands) + arrived_ref[i].astype(F32)
        out_ref[0] = total.astype(out_ref.dtype)


def near_all(line, span, stage, operands, arrived):
    pairs, depth, width = operands[2].shape
    rows = span.stop - span.start
    return call(
        line,
        functools.partial(near_all_kernel, span, stage),
        "near",
        (*operands, arrived),
        (),
        [((1, rows, width), F32)] + [((1, rows, width), BF16)] * (pairs // 2 - 1),
        2 * rows * depth * pairs * width,
    )


def far(line, span, stage, operands, after=()):
    pairs, depth, width = operands[2].shape
    rows = span.stop - span.start
    return call(
        line,
        functools.partial(far_kernel, span, stage),
        "far",
        operands,
        (),
        [((pairs // 2, rows, width), BF16)],
        2 * rows * depth * pairs * width,
        after=after,
    )[0]


def near(line, span, stage, following, operands, arrived, after=()):
    pairs, depth, width = operands[2].shape
    rows = span.stop - span.start
    return call(
        line,
        functools.partial(near_kernel, span, stage, following),
        "near",
        (*operands, arrived),
        (),
        [((pairs // 4, rows, width), F32), ((pairs // 4, rows, width), BF16)],
        2 * rows * depth * pairs * width,
        after=after,
    )


def add_kernel(following, keep_ref, arrived_ref, more_ref, send_ref):
    for i in range(more_ref.shape[0]):
        for value, out_ref in ((1, send_ref), (0, more_ref)):
            at = put_bit(i, following, value)
            out_ref[i] = (keep_ref[at] + arrived_ref[at].astype(F32)).astype(out_ref.dtype)


def add(line, following, keep, arrived):
    shape = (keep.shape[0] // 2,) + keep.shape[1:]
    return call(
        line,
        functools.partial(add_kernel, following),
        "add",
        (keep, arrived),
        (),
        [(shape, F32), (shape, BF16)],
        2 * keep.size,
    )


def total_kernel(a_ref, b_ref, out_ref):
    out_ref[...] = a_ref[...] + b_ref[...]


def total(line, a, b):
    return call(line, total_kernel, "total", (a, b), (), [(a.shape, a.dtype)], a.size)[0]


def side_kernel(keep_ref, arrived_ref, more_ref, send_ref):
    for source, ref in enumerate((keep_ref, arrived_ref)):
        more_ref[source] = ref[0]
        send_ref[source] = ref[1]


def side(line, keep, arrived, after):
    out = (keep.shape, BF16)
    return call(line, side_kernel, "side", (keep, arrived), (), [out, out], 0, after=after)


def sort_kernel(keep_ref, arrived_ref, *out_refs):
    for high, out_ref in enumerate(out_refs):
        for core, ref in enumerate((keep_ref, arrived_ref)):
            for side in range(2):
                for panel in range(2):
                    out_ref[panel, 2 * side + core] = ref[side, panel, high]


def sort(line, keep, arrived, after):
    groups, share, width = keep.shape[2:]
    return call(line, sort_kernel, "sort", (keep, arrived), (), [((2, 4, share, width), BF16)] * groups, 0, after=after)


def far_blocks(blocks):
    size = 4 * len(blocks)
    return [blocks[0]] + [swap(b, "tp", 4 * h, size) for h, b in enumerate(blocks) if h]


def expanding_kernel(*refs):
    out_ref = refs[-1]
    for high, ref in enumerate(refs[:-1]):
        for source in range(4):
            out_ref[4 * high + source] = ref[1, source]


def expanding(line, blocks):
    share, width = blocks[0].shape[2:]
    out = [((4 * len(blocks), share, width), BF16)]
    return call(line, expanding_kernel, "expanding", blocks, (), out, 0)[0]


def owners(ids, shape, high, share):
    owner = 4 * high + lax.broadcasted_iota(jnp.int32, shape, 1) // share
    return owner == (ids ^ lax.axis_index("tp"))


def shrink_kernel(steps, groups, *refs):
    panels, attended, out_ref = refs[:groups], refs[groups:-1], refs[-1]
    share, width = panels[0].shape[2:]
    for k, a_ref in enumerate(attended):
        rows = a_ref.shape[0] - GROUP_REQ
        requests = rows // steps
        row = lax.broadcasted_iota(jnp.int32, (requests, requests), 0)
        column = lax.broadcasted_iota(jnp.int32, (requests, requests), 1)
        line = a_ref[rows : rows + GROUP_REQ, :requests].astype(F32)[:1, :]
        ids = jnp.where(row == column, line, 0.0).sum(1, keepdims=True).astype(jnp.int32)
        ids = jnp.concatenate([ids] * steps, 0)
        total = None
        for high, panel in enumerate(panels):
            flat = panel[0].reshape(4 * share, width)
            ranks = lax.dot_general(
                a_ref[:rows, :], flat, (((1,), (1,)), ((), ())), preferred_element_type=F32
            )
            ranks = jnp.where(owners(ids, ranks.shape, high, share), ranks, 0.0)
            total = ranks if total is None else total + ranks
        part = total[:, :share]
        for i in range(1, 4):
            part = part + total[:, share * i : share * (i + 1)]
        fold = out_ref.shape[1]
        out_ref[k] = jnp.concatenate([part[i * fold : (i + 1) * fold] for i in range(rows // fold)], 1)


def shrink(line, steps, panels, attended):
    replicas, rows, share = len(attended), attended[0].shape[0] - GROUP_REQ, panels[0].shape[2]
    return call(
        line,
        functools.partial(shrink_kernel, steps, len(panels)),
        "shrink",
        (*panels, *attended),
        (),
        [((replicas, rows * share // LANES, LANES), F32)],
        2 * rows * replicas * len(panels) * panels[0].size,
    )[0]


def expand_kernel(steps, replicas, ids_ref, *refs):
    ranks, panels, out_ref = refs[:replicas], refs[replicas:-1], refs[-1]
    _, share, width = panels[0].shape
    ids = jnp.concatenate([ids_ref[...]] * steps, 0)
    total = None
    for k, rank_ref in enumerate(ranks):
        folded = rank_ref[0].astype(BF16).astype(F32)
        part = jnp.concatenate([folded[:, i * share : (i + 1) * share] for i in range(LANES // share)], 0)
        part = jnp.concatenate([part] * 4, 1)
        panel = panels[k]
        spread = [
            jnp.where(owners(ids, part.shape, high, share), part, 0.0).astype(BF16)
            for high in range(panel.shape[0] // 4)
        ]
        term = jnp.dot(
            jnp.concatenate(spread, 1), panel[...].reshape(-1, width), preferred_element_type=F32
        )
        total = term if total is None else total + term
    out_ref[...] = total


def expand(line, steps, ids, ranks, panels):
    rows, width = steps * ids.shape[0], panels[0].shape[2]
    return call(
        line,
        functools.partial(expand_kernel, steps, len(ranks)),
        "expand",
        (ids, *ranks, *panels),
        (),
        [((rows, width), F32)],
        2 * rows * len(panels) * panels[0].size,
    )[0]


def fold_kernel(*refs):
    total = refs[0][0]
    for ref in refs[1:-1]:
        total = total + ref[0].astype(F32)
    refs[-1][...] = total


def fold(line, terms):
    return call(line, fold_kernel, "fold", terms, (), [(terms[0].shape[1:], F32)], 0)[0]


def finish_kernel(spans, lora_ref, *refs):
    refs, out_ref = refs[:-1], refs[-1]
    for n, span in enumerate(spans[:-1]):
        out_ref[span, :] = (refs[n][...] + lora_ref[span, :]).astype(BF16)
    total = lora_ref[spans[-1], :]
    for ref in refs[len(spans) - 1 :]:
        total = total + ref[0].astype(F32)
    out_ref[spans[-1], :] = total.astype(BF16)


def finish(spans, lora, sums, terms):
    operands = [pltpu.with_memory_space_constraint(x, pltpu.VMEM) for x in (lora, *sums, *terms)]
    return pl.pallas_call(
        functools.partial(finish_kernel, spans),
        in_specs=[pl.BlockSpec(memory_space=pltpu.VMEM)] * len(operands),
        out_specs=pl.BlockSpec(memory_space=pltpu.VMEM),
        out_shape=jax.ShapeDtypeStruct(lora.shape, BF16),
        compiler_params=pltpu.CompilerParams(vmem_limit_bytes=VMEM_LIMIT),
        cost_estimate=pl.CostEstimate(flops=4 * lora.size, bytes_accessed=1 << 20, transcendentals=0),
        name="finish",
    )(*operands)


def swap(array, axis, bit, size):
    return lax.ppermute(array, axis, [(i, i ^ bit) for i in range(size)])


def body(
    size,
    replicas,
    queries,
    key_cache,
    value_cache,
    new_keys,
    new_values,
    cache_lengths,
    adapter_ids,
    out_weight,
    shrink_panels,
    expand_panels,
):
    steps, requests, local = queries.shape
    rows = steps * requests
    pairs = size // 2
    stages = size.bit_length() - 2
    plan = SMALL_PLAN if stages == 3 else ((16, tuple(range(stages))),)
    spans, first = [], 0
    for part, _ in plan:
        spans.append(slice(first, first + rows * part // 16))
        first += rows * part // 16

    line = []
    last = len(plan) - 1
    keeps, sends, cames, sums = {}, {}, {}, {}

    def begin(n, after=()):
        order = plan[n][1]
        sends[n] = far(line, spans[n], order[0], operands, after)
        cames[n] = swap(sends[n], "tp", 2 << order[0], size)

    def middle(n, after=()):
        order = plan[n][1]
        if len(order) == 1:
            keep, *rest = near_all(line, spans[n], order[0], operands, cames[n])
            sums[n] = [keep] + [swap(x, "tp", 4 * (h + 1), size) for h, x in enumerate(rest)]
            return
        following = order[1] - (order[1] > order[0])
        keeps[n], send = near(line, spans[n], order[0], following, operands, cames[n], after)
        cames[n] = swap(send, "tp", 2 << order[1], size)

    def end(n):
        order = plan[n][1]
        for i in range(2, len(order)):
            left = order[i] - sum(order[i] > t for t in order[:i])
            keeps[n], send = add(line, left, keeps[n], cames[n])
            cames[n] = swap(send, "tp", 2 << order[i], size)
        if n not in sums:
            sums[n] = [keeps[n], cames[n]]

    picked, cut_keep, cut_send = pick(line, out_weight, shrink_panels, expand_panels, size, replicas)
    weight_other = swap(picked, "tp", 1, size)
    cut_came = swap(cut_send, "tp", 2, size)
    attended, weight_own = attend(
        line, queries, key_cache, value_cache, new_keys, new_values, cache_lengths, adapter_ids, out_weight, size
    )
    attended_other = swap(attended, "tp", 1, size)
    attended_all = [attended] + [swap(attended, "rep", k, replicas) for k in range(1, replicas)]
    operands = (attended, attended_other, weight_own, weight_other)

    begin(0)
    if last:
        begin(2)
    side_keep, side_send = side(line, cut_keep, cut_came, [cames[2]] if last else ())
    panels = far_blocks(sort(line, side_keep, swap(side_send, "tp", 1, size), ()))
    if last:
        begin(1, attended_all[1:])
    shrunk = shrink(line, steps, panels, attended_all)
    came = swap(shrunk, "tp", 2, size)
    middle(0)
    expanding_all = [expanding(line, panels)]
    expanding_all += [swap(expanding_all[0], "rep", k, replicas) for k in range(1, replicas)]
    if last:
        middle(2)
    shrunk = total(line, shrunk, came)
    came = swap(shrunk, "tp", 4, size)
    end(0)
    if last:
        middle(1)
    for bit in range(3, stages + 1):
        shrunk = total(line, shrunk, came)
        came = swap(shrunk, "tp", 1 << bit, size)
    if last:
        sums[0] = [fold(line, sums[0])]
        end(2)
    shrunk = total(line, shrunk, came)
    came = swap(shrunk, "tp", 1, size)
    if last:
        end(1)
    shrunk = total(line, shrunk, came)
    ranks = [shrunk[:1]] + [swap(shrunk[k : k + 1], "rep", k, replicas) for k in range(1, replicas)]
    lora = expand(line, steps, adapter_ids, ranks, expanding_all)
    if last:
        sums[2] = [fold(line, sums[2])]
    ready = [n for n in (0, 2) if n < last or n == 2 and last]
    spans = [spans[n] for n in (*ready, 1 if last else 0)]
    ready = [sums[n][0] for n in ready]
    last = 1 if last else 0
    return finish(spans, lora, ready, sums[last]).reshape(queries.shape)


def solution(mesh):
    return jax.shard_map(
        functools.partial(body, mesh.shape["tp"], mesh.shape["rep"]),
        mesh=mesh,
        in_specs=(
            P(None, "rep", "tp"),
            P("rep", None, None),
            P("rep", None, None),
            P(None, "rep", None),
            P(None, "rep", None),
            P("rep"),
            P("rep", None),
            P("tp", None),
            P("tp", None, None),
            P("tp", None, None),
        ),
        out_specs=P(None, "rep", "tp"),
        check_vma=False,
    )
```

time: 122 us -> 105 us (0.86)
  waiting for transfers between devices: 60.9 us -> 51 us
  starting transfers between devices: 44.3 us -> 37.9 us
    ppermute x39 -> x23, waiting for transfers between devices: 60.9 us -> 51 us  [swap(): return lax.ppermute(array, axis, [(i, i ^ bit) for i in range(size)])]
    ppermute x39 -> x23, starting transfers between devices: 44.3 us -> 37.9 us  [swap(): return lax.ppermute(array, axis, [(i, i ^ bit) for i in range(size)])]
    pallas_call x18 -> x22, Pallas kernels: 15.5 us -> 14.8 us  [call(): pl.pallas_call(run, in_specs=[pl.BlockSpec(memory_space=pltpu.VMEM)] * le...]
  transfers between devices with their start and end apart: 39 -> 23, of which waited for: 17 -> 13; matrix products, arithmetic and copies ran while one was open for 0% -> 0% of each run, Pallas kernels for 11% -> 11%
where the time goes in v3:
time: 105 us
  waiting for transfers between devices  51 us (49%)
  starting transfers between devices  37.9 us (36%)
  Pallas kernels  15.7 us (15%)
    ppermute x23, waiting for transfers between devices, swap(): return lax.ppermute(array, axis, [(i, i ^ bit) for i in range(size)])  51 us
    ppermute x23, starting transfers between devices, swap(): return lax.ppermute(array, axis, [(i, i ^ bit) for i in range(size)])  37.9 us
    pallas_call x22, Pallas kernels, call(): pl.pallas_call(run, in_specs=[pl.BlockSpec(memory_space=pltpu.VMEM)] * le...  14.8 us
  transfers between devices with their start and end apart: 23, of which 13 were waited for; matrix products, arithmetic and copies ran while one was open for 0% of the time, Pallas kernels for 11%

profile of v3, /device:TPU:0, one launch (start us, length us, event | category | flops | bytes accessed | tf_op | source)
XLA Modules:
  0.0 104.9 jit_solution(2689519047036805452)
XLA Ops:
  0.0 2.8 %pick.1 = (bf16[8,512,512]{2,1,0:T(8,128)(2,1)S(1)}, bf16[2,2,4,32,512]{4,3,2,1,0:T(8,128)(2,1)S(1)}, bf16[2,2,4,32,512]{4,3,2,1,0:T(8,128)(2,1)S(1)}) custom-call(bf16[512,8192]{1,0:T(8,128)(2,1)} %refs_7_.1, bf16[1,64,8192]{2,1,0:T(8,128)(2,1)} %refs_1_.1, bf16[1,64,8192]{2,1,0:T(8,128)(2,1)} %refs_2_.2), custom_call_target="tpu_custom_call" | custom-call | bytes 65536 | tf_op jit(solution)/shard_map/pick/pallas_call | solution.py:28
  3.3 3.4 %attention.1 = (bf16[528,512]{1,0:T(8,128)(2,1)S(1)}, bf16[8,512,512]{2,1,0:T(8,128)(2,1)S(1)}) custom-call(s32[1,128]{1,0:T(1,128)S(1)} %bitcast.6, s32[1,128]{1,0:T(1,128)S(1)} %bitcast.5, bf16[4,128,512]{2,1,0:T(8,128)(2,1)} %refs_2_.3, bf16[12,128,1024]{2,1,0:T(8,128)(2,1)} %bitcast.7, bf16[12,128,1024]{2,1,0:T(8,128)(2,1)} %bitcast.8, ...), custom_call_target="tpu_custom_call" | custom-call | flops 268435456 | bytes 65536 | tf_op jit(solution)/shard_map/attention/pallas_call | solution.py:28
  6.8 3.0 %collective-permute-start = (bf16[2,2,4,32,512]{4,3,2,1,0:T(8,128)(2,1)S(1)}, bf16[2,2,4,32,512]{4,3,2,1,0:T(8,128)(2,1)S(1)}, u32[]{:S(2)}, u32[]{:S(2)}) collective-permute-start(bf16[2,2,4,32,512]{4,3,2,1,0:T(8,128)(2,1)S(1)} %get-tuple-element.29), channel_id=1, source_target_pairs={{0,2},{1,3},{2,0},{3,1},{4,6},{5,7},{6,4},{7,5},{8,10},{9,11},{10,... | collective-permute-start | bytes 1572872 | tf_op jit(solution)/shard_map/ppermute | solution.py:457
  12.8 3.0 %collective-permute-start.3 = (bf16[4,96,512]{2,1,0:T(8,128)(2,1)S(1)}, bf16[4,96,512]{2,1,0:T(8,128)(2,1)S(1)}, u32[]{:S(2)}, u32[]{:S(2)}) collective-permute-start(bf16[4,96,512]{2,1,0:T(8,128)(2,1)S(1)} %far.4.refs_2_), channel_id=1, source_target_pairs={{0,4},{1,5},{2,6},{3,7},{4,0},{5,1},{6,2},{7,3},{8,12},{9,13},{10,... | collective-permute-start | bytes 1179656 | tf_op jit(solution)/shard_map/ppermute | solution.py:457
  17.3 5.2 %collective-permute-done.refs_1_ = bf16[2,2,4,32,512]{4,3,2,1,0:T(8,128)(2,1)S(1)} collective-permute-done((bf16[2,2,4,32,512]{4,3,2,1,0:T(8,128)(2,1)S(1)}, bf16[2,2,4,32,512]{4,3,2,1,0:T(8,128)(2,1)S(1)}, u32[]{:S(2)}, u32[]{:S(2)}) %collective-permute-start) | collective-permute-done | bytes 524320 | tf_op jit(solution)/shard_map/ppermute | solution.py:457
  22.5 2.7 %collective-permute-done.3.refs_3_.refs_4_ = bf16[4,96,512]{2,1,0:T(8,128)(2,1)S(1)} collective-permute-done((bf16[4,96,512]{2,1,0:T(8,128)(2,1)S(1)}, bf16[4,96,512]{2,1,0:T(8,128)(2,1)S(1)}, u32[]{:S(2)}, u32[]{:S(2)}) %collective-permute-start.3) | collective-permute-done | bytes 393248 | tf_op jit(solution)/shard_map/ppermute | solution.py:457
  25.3 1.7 %collective-permute-start.8 = (bf16[528,512]{1,0:T(8,128)(2,1)S(1)}, bf16[528,512]{1,0:T(8,128)(2,1)S(1)}, u32[]{:S(2)}, u32[]{:S(2)}) collective-permute-start(bf16[528,512]{1,0:T(8,128)(2,1)S(1)} %get-tuple-element.30.refs_0_.refs_4_), channel_id=1, source_target_pairs={{0,16},{16,0},{1,17},{17,1},{2,18},{18,2},{3,19},{19,3},{4,20},{20... | collective-permute-start | bytes 1622024 | tf_op jit(solution)/shard_map/ppermute | solution.py:457
  27.3 1.8 %collective-permute-start.5 = (bf16[2,4,32,512]{3,2,1,0:T(8,128)(2,1)S(1)}, bf16[2,4,32,512]{3,2,1,0:T(8,128)(2,1)S(1)}, u32[]{:S(2)}, u32[]{:S(2)}) collective-permute-start(bf16[2,4,32,512]{3,2,1,0:T(8,128)(2,1)S(1)} %get-tuple-element.36), channel_id=1, source_target_pairs={{0,4},{1,5},{2,6},{3,7},{4,0},{5,1},{6,2},{7,3},{8,12},{9,13},{10,... | collective-permute-start | bytes 786440 | tf_op jit(solution)/shard_map/ppermute | solution.py:457
  29.1 2.6 %collective-permute-start.6 = (bf16[2,4,32,512]{3,2,1,0:T(8,128)(2,1)S(1)}, bf16[2,4,32,512]{3,2,1,0:T(8,128)(2,1)S(1)}, u32[]{:S(2)}, u32[]{:S(2)}) collective-permute-start(bf16[2,4,32,512]{3,2,1,0:T(8,128)(2,1)S(1)} %get-tuple-element.37), channel_id=1, source_target_pairs={{0,8},{1,9},{2,10},{3,11},{4,12},{5,13},{6,14},{7,15},{8,0},{9,1},... | collective-permute-start | bytes 786440 | tf_op jit(solution)/shard_map/ppermute | solution.py:457
  31.8 8.3 %collective-permute-done.8.refs_5_ = bf16[528,512]{1,0:T(8,128)(2,1)S(1)} collective-permute-done((bf16[528,512]{1,0:T(8,128)(2,1)S(1)}, bf16[528,512]{1,0:T(8,128)(2,1)S(1)}, u32[]{:S(2)}, u32[]{:S(2)}) %collective-permute-start.8) | collective-permute-done | bytes 540704 | tf_op jit(solution)/shard_map/ppermute | solution.py:457
  41.0 1.7 %collective-permute-start.12 = (bf16[4,192,512]{2,1,0:T(8,128)(2,1)S(1)}, bf16[4,192,512]{2,1,0:T(8,128)(2,1)S(1)}, u32[]{:S(2)}, u32[]{:S(2)}) collective-permute-start(bf16[4,192,512]{2,1,0:T(8,128)(2,1)S(1)} %far.5.refs_6_), channel_id=1, source_target_pairs={{0,2},{1,3},{2,0},{3,1},{4,6},{5,7},{6,4},{7,5},{8,10},{9,11},{10,... | collective-permute-start | bytes 2359304 | tf_op jit(solution)/shard_map/ppermute | solution.py:457
  42.8 7.7 %collective-permute-done.6.refs_2_ = bf16[2,4,32,512]{3,2,1,0:T(8,128)(2,1)S(1)} collective-permute-done((bf16[2,4,32,512]{3,2,1,0:T(8,128)(2,1)S(1)}, bf16[2,4,32,512]{3,2,1,0:T(8,128)(2,1)S(1)}, u32[]{:S(2)}, u32[]{:S(2)}) %collective-permute-start.6) | collective-permute-done | bytes 262176 | tf_op jit(solution)/shard_map/ppermute | solution.py:457
  50.4 1.5 %shrink.1.refs_5_.refs_0_ = f32[2,128,128]{2,1,0:T(8,128)S(1)} custom-call(bf16[2,4,32,512]{3,2,1,0:T(8,128)(2,1)S(1)} %get-tuple-element.35.refs_4_.refs_0_, bf16[2,4,32,512]{3,2,1,0:T(8,128)(2,1)S(1)} %collective-permute-done.5.refs_1_, bf16[2,4,32,512]{3,2,1,0:T(8,128)(2,1)S(1)} %collective-permute-done.6.refs_2_, ...), custom_call_target="tpu_custom_call" | custom-call | flops 1073741824 | bytes 65536 | tf_op jit(solution)/shard_map/shrink/pallas_call | solution.py:28
  53.1 5.2 %collective-permute-start.13 = (bf16[2,224,512]{2,1,0:T(8,128)(2,1)S(1)}, bf16[2,224,512]{2,1,0:T(8,128)(2,1)S(1)}, u32[]{:S(2)}, u32[]{:S(2)}) collective-permute-start(bf16[2,224,512]{2,1,0:T(8,128)(2,1)S(1)} %get-tuple-element.41), channel_id=1, source_target_pairs={{0,4},{1,5},{2,6},{3,7},{4,0},{5,1},{6,2},{7,3},{8,12},{9,13},{10,... | collective-permute-start | bytes 1376264 | tf_op jit(solution)/shard_map/ppermute | solution.py:457
  60.6 2.6 %collective-permute-done.9.refs_1_ = f32[2,128,128]{2,1,0:T(8,128)S(1)} collective-permute-done((f32[2,128,128]{2,1,0:T(8,128)S(1)}, f32[2,128,128]{2,1,0:T(8,128)S(1)}, u32[]{:S(2)}, u32[]{:S(2)}) %collective-permute-start.9) | collective-permute-done | bytes 131104 | tf_op jit(solution)/shard_map/ppermute | solution.py:457
  63.3 1.6 %collective-permute-start.11 = (f32[2,128,128]{2,1,0:T(8,128)S(1)}, f32[2,128,128]{2,1,0:T(8,128)S(1)}, u32[]{:S(2)}, u32[]{:S(2)}) collective-permute-start(f32[2,128,128]{2,1,0:T(8,128)S(1)} %total.4.refs_2_.refs_0_), channel_id=1, source_target_pairs={{0,4},{1,5},{2,6},{3,7},{4,0},{5,1},{6,2},{7,3},{8,12},{9,13},{10,... | collective-permute-start | bytes 393224 | tf_op jit(solution)/shard_map/ppermute | solution.py:457
  64.8 4.6 %collective-permute-done.13.refs_1_ = bf16[2,224,512]{2,1,0:T(8,128)(2,1)S(1)} collective-permute-done((bf16[2,224,512]{2,1,0:T(8,128)(2,1)S(1)}, bf16[2,224,512]{2,1,0:T(8,128)(2,1)S(1)}, u32[]{:S(2)}, u32[]{:S(2)}) %collective-permute-start.13) | collective-permute-done | bytes 458784 | tf_op jit(solution)/shard_map/ppermute | solution.py:457
  70.5 1.8 %collective-permute-start.18 = (bf16[2,192,512]{2,1,0:T(8,128)(2,1)S(1)}, bf16[2,192,512]{2,1,0:T(8,128)(2,1)S(1)}, u32[]{:S(2)}, u32[]{:S(2)}) collective-permute-start(bf16[2,192,512]{2,1,0:T(8,128)(2,1)S(1)} %get-tuple-element.47), channel_id=1, source_target_pairs={{0,4},{1,5},{2,6},{3,7},{4,0},{5,1},{6,2},{7,3},{8,12},{9,13},{10,... | collective-permute-start | bytes 1179656 | tf_op jit(solution)/shard_map/ppermute | solution.py:457
  73.6 1.5 %collective-permute-start.15 = (bf16[2,96,512]{2,1,0:T(8,128)(2,1)S(1)}, bf16[2,96,512]{2,1,0:T(8,128)(2,1)S(1)}, u32[]{:S(2)}, u32[]{:S(2)}) collective-permute-start(bf16[2,96,512]{2,1,0:T(8,128)(2,1)S(1)} %get-tuple-element.44), channel_id=1, source_target_pairs={{0,2},{1,3},{2,0},{3,1},{4,6},{5,7},{6,4},{7,5},{8,10},{9,11},{10,... | collective-permute-start | bytes 589832 | tf_op jit(solution)/shard_map/ppermute | solution.py:457
  75.1 1.7 %collective-permute-start.14 = (f32[2,128,128]{2,1,0:T(8,128)S(1)}, f32[2,128,128]{2,1,0:T(8,128)S(1)}, u32[]{:S(2)}, u32[]{:S(2)}) collective-permute-start(f32[2,128,128]{2,1,0:T(8,128)S(1)} %total.5.refs_2_.refs_0_), channel_id=1, source_target_pairs={{0,8},{1,9},{2,10},{3,11},{4,12},{5,13},{6,14},{7,15},{8,0},{9,1},... | collective-permute-start | bytes 393224 | tf_op jit(solution)/shard_map/ppermute | solution.py:457
  78.3 6.5 %collective-permute-done.16.refs_1_ = bf16[1,224,512]{2,1,0:T(8,128)(2,1)S(1)} collective-permute-done((bf16[1,224,512]{2,1,0:T(8,128)(2,1)S(1)}, bf16[1,224,512]{2,1,0:T(8,128)(2,1)S(1)}, u32[]{:S(2)}, u32[]{:S(2)}) %collective-permute-start.16) | collective-permute-done | bytes 229408 | tf_op jit(solution)/shard_map/ppermute | solution.py:457
  87.0 2.9 %collective-permute-start.22 = (bf16[1,192,512]{2,1,0:T(8,128)(2,1)S(1)}, bf16[1,192,512]{2,1,0:T(8,128)(2,1)S(1)}, u32[]{:S(2)}, u32[]{:S(2)}) collective-permute-start(bf16[1,192,512]{2,1,0:T(8,128)(2,1)S(1)} %get-tuple-element.50), channel_id=1, source_target_pairs={{0,8},{1,9},{2,10},{3,11},{4,12},{5,13},{6,14},{7,15},{8,0},{9,1},... | collective-permute-start | bytes 589832 | tf_op jit(solution)/shard_map/ppermute | solution.py:457
  90.0 1.5 %collective-permute-start.19 = (f32[1,128,128]{2,1,0:T(8,128)S(1)}, f32[1,128,128]{2,1,0:T(8,128)S(1)}, u32[]{:S(2)}, u32[]{:S(2)}) collective-permute-start(f32[1,128,128]{2,1,0:T(8,128)S(1)} %get-tuple-element.51), channel_id=1, source_target_pairs={{0,16},{16,0},{1,17},{17,1},{2,18},{18,2},{3,19},{19,3},{4,20},{20... | collective-permute-start | bytes 196616 | tf_op jit(solution)/shard_map/ppermute | solution.py:457
  95.1 8.8 %collective-permute-done.21.refs_1_ = bf16[1,96,512]{2,1,0:T(8,128)(2,1)S(1)} collective-permute-done((bf16[1,96,512]{2,1,0:T(8,128)(2,1)S(1)}, bf16[1,96,512]{2,1,0:T(8,128)(2,1)S(1)}, u32[]{:S(2)}, u32[]{:S(2)}) %collective-permute-start.21) | collective-permute-done | bytes 98336 | tf_op jit(solution)/shard_map/ppermute | solution.py:457
  (51 shorter events, 20.6 us)
Async XLA Ops:
  0.0 3.3 %copy-start.1 = (s32[128]{0:T(128)S(1)}, s32[128]{0:T(128)}, u32[]{:S(2)}) copy-start(s32[128]{0:T(128)} %param.15) | copy-start | bytes 1540
  2.8 8.1 %collective-permute-start.2 = (bf16[8,512,512]{2,1,0:T(8,128)(2,1)S(1)}, bf16[8,512,512]{2,1,0:T(8,128)(2,1)S(1)}, u32[]{:S(2)}, u32[]{:S(2)}) collective-permute-start(bf16[8,512,512]{2,1,0:T(8,128)(2,1)S(1)} %get-tuple-element.32), channel_id=1, source_target_pairs={{0,1},{1,0},{2,3},{3,2},{4,5},{5,4},{6,7},{7,6},{8,9},{9,8},{10,11... | collective-permute-start | bytes 12582920 | tf_op jit(solution)/shard_map/ppermute | solution.py:457
  6.7 4.1 %collective-permute-start.1 = (bf16[528,512]{1,0:T(8,128)(2,1)S(1)}, bf16[528,512]{1,0:T(8,128)(2,1)S(1)}, u32[]{:S(2)}, u32[]{:S(2)}) collective-permute-start(bf16[528,512]{1,0:T(8,128)(2,1)S(1)} %get-tuple-element.30.refs_0_.refs_4_), channel_id=1, source_target_pairs={{0,1},{1,0},{2,3},{3,2},{4,5},{5,4},{6,7},{7,6},{8,9},{9,8},{10,11... | collective-permute-start | bytes 1622024 | tf_op jit(solution)/shard_map/ppermute | solution.py:457
  6.8 15.7 %collective-permute-start = (bf16[2,2,4,32,512]{4,3,2,1,0:T(8,128)(2,1)S(1)}, bf16[2,2,4,32,512]{4,3,2,1,0:T(8,128)(2,1)S(1)}, u32[]{:S(2)}, u32[]{:S(2)}) collective-permute-start(bf16[2,2,4,32,512]{4,3,2,1,0:T(8,128)(2,1)S(1)} %get-tuple-element.29), channel_id=1, source_target_pairs={{0,2},{1,3},{2,0},{3,1},{4,6},{5,7},{6,4},{7,5},{8,10},{9,11},{10,... | collective-permute-start | bytes 1572872 | tf_op jit(solution)/shard_map/ppermute | solution.py:457
  12.8 12.4 %collective-permute-start.3 = (bf16[4,96,512]{2,1,0:T(8,128)(2,1)S(1)}, bf16[4,96,512]{2,1,0:T(8,128)(2,1)S(1)}, u32[]{:S(2)}, u32[]{:S(2)}) collective-permute-start(bf16[4,96,512]{2,1,0:T(8,128)(2,1)S(1)} %far.4.refs_2_), channel_id=1, source_target_pairs={{0,4},{1,5},{2,6},{3,7},{4,0},{5,1},{6,2},{7,3},{8,12},{9,13},{10,... | collective-permute-start | bytes 1179656 | tf_op jit(solution)/shard_map/ppermute | solution.py:457
  15.8 36.2 %collective-permute-start.10 = (bf16[4,224,512]{2,1,0:T(8,128)(2,1)S(1)}, bf16[4,224,512]{2,1,0:T(8,128)(2,1)S(1)}, u32[]{:S(2)}, u32[]{:S(2)}) collective-permute-start(bf16[4,224,512]{2,1,0:T(8,128)(2,1)S(1)} %far.3.refs_4_), channel_id=1, source_target_pairs={{0,2},{1,3},{2,0},{3,1},{4,6},{5,7},{6,4},{7,5},{8,10},{9,11},{10,... | collective-permute-start | bytes 2752520 | tf_op jit(solution)/shard_map/ppermute | solution.py:457
  25.3 2.0 %collective-permute-start.4 = (bf16[2,2,4,32,512]{4,3,2,1,0:T(8,128)(2,1)S(1)}, bf16[2,2,4,32,512]{4,3,2,1,0:T(8,128)(2,1)S(1)}, u32[]{:S(2)}, u32[]{:S(2)}) collective-permute-start(bf16[2,2,4,32,512]{4,3,2,1,0:T(8,128)(2,1)S(1)} %get-tuple-element.34), channel_id=1, source_target_pairs={{0,1},{1,0},{2,3},{3,2},{4,5},{5,4},{6,7},{7,6},{8,9},{9,8},{10,11... | collective-permute-start | bytes 1572872 | tf_op jit(solution)/shard_map/ppermute | solution.py:457
  25.3 14.7 %collective-permute-start.8 = (bf16[528,512]{1,0:T(8,128)(2,1)S(1)}, bf16[528,512]{1,0:T(8,128)(2,1)S(1)}, u32[]{:S(2)}, u32[]{:S(2)}) collective-permute-start(bf16[528,512]{1,0:T(8,128)(2,1)S(1)} %get-tuple-element.30.refs_0_.refs_4_), channel_id=1, source_target_pairs={{0,16},{16,0},{1,17},{17,1},{2,18},{18,2},{3,19},{19,3},{4,20},{20... | collective-permute-start | bytes 1622024 | tf_op jit(solution)/shard_map/ppermute | solution.py:457
  27.3 15.5 %collective-permute-start.5 = (bf16[2,4,32,512]{3,2,1,0:T(8,128)(2,1)S(1)}, bf16[2,4,32,512]{3,2,1,0:T(8,128)(2,1)S(1)}, u32[]{:S(2)}, u32[]{:S(2)}) collective-permute-start(bf16[2,4,32,512]{3,2,1,0:T(8,128)(2,1)S(1)} %get-tuple-element.36), channel_id=1, source_target_pairs={{0,4},{1,5},{2,6},{3,7},{4,0},{5,1},{6,2},{7,3},{8,12},{9,13},{10,... | collective-permute-start | bytes 786440 | tf_op jit(solution)/shard_map/ppermute | solution.py:457
  29.1 21.3 %collective-permute-start.6 = (bf16[2,4,32,512]{3,2,1,0:T(8,128)(2,1)S(1)}, bf16[2,4,32,512]{3,2,1,0:T(8,128)(2,1)S(1)}, u32[]{:S(2)}, u32[]{:S(2)}) collective-permute-start(bf16[2,4,32,512]{3,2,1,0:T(8,128)(2,1)S(1)} %get-tuple-element.37), channel_id=1, source_target_pairs={{0,8},{1,9},{2,10},{3,11},{4,12},{5,13},{6,14},{7,15},{8,0},{9,1},... | collective-permute-start | bytes 786440 | tf_op jit(solution)/shard_map/ppermute | solution.py:457
  31.7 18.7 %collective-permute-start.7 = (bf16[2,4,32,512]{3,2,1,0:T(8,128)(2,1)S(1)}, bf16[2,4,32,512]{3,2,1,0:T(8,128)(2,1)S(1)}, u32[]{:S(2)}, u32[]{:S(2)}) collective-permute-start(bf16[2,4,32,512]{3,2,1,0:T(8,128)(2,1)S(1)} %get-tuple-element.38), channel_id=1, source_target_pairs={{0,12},{1,13},{2,14},{3,15},{4,8},{5,9},{6,10},{7,11},{8,4},{9,5},... | collective-permute-start | bytes 786440 | tf_op jit(solution)/shard_map/ppermute | solution.py:457
  41.0 28.5 %collective-permute-start.12 = (bf16[4,192,512]{2,1,0:T(8,128)(2,1)S(1)}, bf16[4,192,512]{2,1,0:T(8,128)(2,1)S(1)}, u32[]{:S(2)}, u32[]{:S(2)}) collective-permute-start(bf16[4,192,512]{2,1,0:T(8,128)(2,1)S(1)} %far.5.refs_6_), channel_id=1, source_target_pairs={{0,2},{1,3},{2,0},{3,1},{4,6},{5,7},{6,4},{7,5},{8,10},{9,11},{10,... | collective-permute-start | bytes 2359304 | tf_op jit(solution)/shard_map/ppermute | solution.py:457
  53.1 16.3 %collective-permute-start.13 = (bf16[2,224,512]{2,1,0:T(8,128)(2,1)S(1)}, bf16[2,224,512]{2,1,0:T(8,128)(2,1)S(1)}, u32[]{:S(2)}, u32[]{:S(2)}) collective-permute-start(bf16[2,224,512]{2,1,0:T(8,128)(2,1)S(1)} %get-tuple-element.41), channel_id=1, source_target_pairs={{0,4},{1,5},{2,6},{3,7},{4,0},{5,1},{6,2},{7,3},{8,12},{9,13},{10,... | collective-permute-start | bytes 1376264 | tf_op jit(solution)/shard_map/ppermute | solution.py:457
  58.3 5.0 %collective-permute-start.9 = (f32[2,128,128]{2,1,0:T(8,128)S(1)}, f32[2,128,128]{2,1,0:T(8,128)S(1)}, u32[]{:S(2)}, u32[]{:S(2)}) collective-permute-start(f32[2,128,128]{2,1,0:T(8,128)S(1)} %shrink.1.refs_5_.refs_0_), channel_id=1, source_target_pairs={{0,2},{1,3},{2,0},{3,1},{4,6},{5,7},{6,4},{7,5},{8,10},{9,11},{10,... | collective-permute-start | bytes 393224 | tf_op jit(solution)/shard_map/ppermute | solution.py:457
  63.3 11.8 %collective-permute-start.11 = (f32[2,128,128]{2,1,0:T(8,128)S(1)}, f32[2,128,128]{2,1,0:T(8,128)S(1)}, u32[]{:S(2)}, u32[]{:S(2)}) collective-permute-start(f32[2,128,128]{2,1,0:T(8,128)S(1)} %total.4.refs_2_.refs_0_), channel_id=1, source_target_pairs={{0,4},{1,5},{2,6},{3,7},{4,0},{5,1},{6,2},{7,3},{8,12},{9,13},{10,... | collective-permute-start | bytes 393224 | tf_op jit(solution)/shard_map/ppermute | solution.py:457
  70.5 16.5 %collective-permute-start.18 = (bf16[2,192,512]{2,1,0:T(8,128)(2,1)S(1)}, bf16[2,192,512]{2,1,0:T(8,128)(2,1)S(1)}, u32[]{:S(2)}, u32[]{:S(2)}) collective-permute-start(bf16[2,192,512]{2,1,0:T(8,128)(2,1)S(1)} %get-tuple-element.47), channel_id=1, source_target_pairs={{0,4},{1,5},{2,6},{3,7},{4,0},{5,1},{6,2},{7,3},{8,12},{9,13},{10,... | collective-permute-start | bytes 1179656 | tf_op jit(solution)/shard_map/ppermute | solution.py:457
  72.3 12.6 %collective-permute-start.16 = (bf16[1,224,512]{2,1,0:T(8,128)(2,1)S(1)}, bf16[1,224,512]{2,1,0:T(8,128)(2,1)S(1)}, u32[]{:S(2)}, u32[]{:S(2)}) collective-permute-start(bf16[1,224,512]{2,1,0:T(8,128)(2,1)S(1)} %get-tuple-element.45), channel_id=1, source_target_pairs={{0,8},{1,9},{2,10},{3,11},{4,12},{5,13},{6,14},{7,15},{8,0},{9,1},... | collective-permute-start | bytes 688136 | tf_op jit(solution)/shard_map/ppermute | solution.py:457
  73.6 11.3 %collective-permute-start.15 = (bf16[2,96,512]{2,1,0:T(8,128)(2,1)S(1)}, bf16[2,96,512]{2,1,0:T(8,128)(2,1)S(1)}, u32[]{:S(2)}, u32[]{:S(2)}) collective-permute-start(bf16[2,96,512]{2,1,0:T(8,128)(2,1)S(1)} %get-tuple-element.44), channel_id=1, source_target_pairs={{0,2},{1,3},{2,0},{3,1},{4,6},{5,7},{6,4},{7,5},{8,10},{9,11},{10,... | collective-permute-start | bytes 589832 | tf_op jit(solution)/shard_map/ppermute | solution.py:457
  75.1 11.1 %collective-permute-start.14 = (f32[2,128,128]{2,1,0:T(8,128)S(1)}, f32[2,128,128]{2,1,0:T(8,128)S(1)}, u32[]{:S(2)}, u32[]{:S(2)}) collective-permute-start(f32[2,128,128]{2,1,0:T(8,128)S(1)} %total.5.refs_2_.refs_0_), channel_id=1, source_target_pairs={{0,8},{1,9},{2,10},{3,11},{4,12},{5,13},{6,14},{7,15},{8,0},{9,1},... | collective-permute-start | bytes 393224 | tf_op jit(solution)/shard_map/ppermute | solution.py:457
  76.8 16.0 %collective-permute-start.20 = (bf16[16,32,512]{2,1,0:T(8,128)(2,1)S(1)}, bf16[16,32,512]{2,1,0:T(8,128)(2,1)S(1)}, u32[]{:S(2)}, u32[]{:S(2)}) collective-permute-start(bf16[16,32,512]{2,1,0:T(8,128)(2,1)S(1)} %expanding.1.refs_5_.refs_3_), channel_id=1, source_target_pairs={{0,16},{16,0},{1,17},{17,1},{2,18},{18,2},{3,19},{19,3},{4,20},{20... | collective-permute-start | bytes 1572872 | tf_op jit(solution)/shard_map/ppermute | solution.py:457
  86.3 3.7 %collective-permute-start.17 = (f32[2,128,128]{2,1,0:T(8,128)S(1)}, f32[2,128,128]{2,1,0:T(8,128)S(1)}, u32[]{:S(2)}, u32[]{:S(2)}) collective-permute-start(f32[2,128,128]{2,1,0:T(8,128)S(1)} %total.6.refs_2_.refs_0_), channel_id=1, source_target_pairs={{0,1},{1,0},{2,3},{3,2},{4,5},{5,4},{6,7},{7,6},{8,9},{9,8},{10,11... | collective-permute-start | bytes 393224 | tf_op jit(solution)/shard_map/ppermute | solution.py:457
  87.0 16.9 %collective-permute-start.22 = (bf16[1,192,512]{2,1,0:T(8,128)(2,1)S(1)}, bf16[1,192,512]{2,1,0:T(8,128)(2,1)S(1)}, u32[]{:S(2)}, u32[]{:S(2)}) collective-permute-start(bf16[1,192,512]{2,1,0:T(8,128)(2,1)S(1)} %get-tuple-element.50), channel_id=1, source_target_pairs={{0,8},{1,9},{2,10},{3,11},{4,12},{5,13},{6,14},{7,15},{8,0},{9,1},... | collective-permute-start | bytes 589832 | tf_op jit(solution)/shard_map/ppermute | solution.py:457
  90.0 4.3 %collective-permute-start.19 = (f32[1,128,128]{2,1,0:T(8,128)S(1)}, f32[1,128,128]{2,1,0:T(8,128)S(1)}, u32[]{:S(2)}, u32[]{:S(2)}) collective-permute-start(f32[1,128,128]{2,1,0:T(8,128)S(1)} %get-tuple-element.51), channel_id=1, source_target_pairs={{0,16},{16,0},{1,17},{17,1},{2,18},{18,2},{3,19},{19,3},{4,20},{20... | collective-permute-start | bytes 196616 | tf_op jit(solution)/shard_map/ppermute | solution.py:457
  91.5 12.4 %collective-permute-start.21 = (bf16[1,96,512]{2,1,0:T(8,128)(2,1)S(1)}, bf16[1,96,512]{2,1,0:T(8,128)(2,1)S(1)}, u32[]{:S(2)}, u32[]{:S(2)}) collective-permute-start(bf16[1,96,512]{2,1,0:T(8,128)(2,1)S(1)} %get-tuple-element.49), channel_id=1, source_target_pairs={{0,8},{1,9},{2,10},{3,11},{4,12},{5,13},{6,14},{7,15},{8,0},{9,1},... | collective-permute-start | bytes 294920 | tf_op jit(solution)/shard_map/ppermute | solution.py:457
  (1 other events, 3.3 us)

commit v4 on v3

v4 whole, which is shorter than its diff:
```python
import functools

import jax
import jax.numpy as jnp
from jax import lax
from jax.experimental import pallas as pl
from jax.experimental.pallas import tpu as pltpu
from jax.sharding import PartitionSpec as P

HD = 128
LANES = 128
GROUP_REQ = 16
VMEM_LIMIT = 24 << 20
F32 = jnp.float32
BF16 = jnp.bfloat16
PLAN = ((7, (0, 1, 2)), (5, (0, 1, 2)), (1, (0, 1, 2)), (3, (1, 0, 2)))
FIRST_PIECE = 1
RIDE = 2
STEPS = ('far3', 'far0', 'side', 'have3', 'sort', 'have_x', 'far1', 'near0', 'shrink', 'core', 'far2', 'expanding', 'near3', 'near1', 'end0', 'near2', 'end1', 'fold0', 'end3', 'end2', 'fold1', 'ranks', 'expand', 'fold3')
PLAIN_STEPS = ("side", "sort", "shrink", "core", "far0", "near0", "end0", "ranks", "expanding", "expand")
COST = 1


def call(line, kernel, name, vmem, hbm, out, cost, scratch=(), after=()):
    operands = [pltpu.with_memory_space_constraint(x, pltpu.VMEM) for x in vmem]
    operands += [pltpu.with_memory_space_constraint(x, pltpu.HBM) for x in hbm]
    before = [*line, *after]
    count, extra = len(operands), len(before)

    def run(*refs):
        kernel(*refs[:count], *refs[count + extra :])

    results = pl.pallas_call(
        run,
        in_specs=[pl.BlockSpec(memory_space=pltpu.VMEM)] * len(vmem)
        + [pl.BlockSpec(memory_space=pltpu.HBM)] * len(hbm)
        + [pl.BlockSpec(memory_space=pl.ANY)] * extra,
        out_specs=[pl.BlockSpec(memory_space=pltpu.VMEM)] * len(out),
        out_shape=[pltpu.VMEM(shape, dtype) for shape, dtype in out],
        scratch_shapes=scratch,
        compiler_params=pltpu.CompilerParams(vmem_limit_bytes=VMEM_LIMIT),
        cost_estimate=pl.CostEstimate(flops=COST * cost, bytes_accessed=1 << 16, transcendentals=0),
        name=name,
    )(*operands, *before)
    line[:] = [min(results, key=lambda x: x.size)]
    return results


def put_bit(i, position, value):
    low = i & ((1 << position) - 1)
    return ((i >> position) << (position + 1)) | (value << position) | low


def cut_copies(panel_ref, keep_ref, send_ref, panel, place, replica):
    groups, share, width = keep_ref.shape[2:]
    rank = pl.multiple_of(replica * share, share)
    copies = []
    for low, cut_ref in enumerate((keep_ref, keep_ref, send_ref, send_ref)):
        for high in range(groups):
            column = pl.multiple_of((place ^ (4 * high + low)) * width, width)
            copies.append(
                (panel_ref.at[0, pl.ds(rank, share), pl.ds(column, width)], cut_ref.at[low % 2, panel, high])
            )
    return copies


def run_copies(copies, sems):
    copies = [pltpu.make_async_copy(a, b, sems.at[i]) for i, (a, b) in enumerate(copies)]
    for copy in copies:
        copy.start()
    for copy in copies:
        copy.wait()


def cut_kernel(shrink_ref, expand_ref, keep_ref, send_ref, sems):
    place, replica = lax.axis_index("tp"), lax.axis_index("rep")
    copies = cut_copies(shrink_ref, keep_ref, send_ref, 0, place, replica)
    run_copies(copies + cut_copies(expand_ref, keep_ref, send_ref, 1, place, replica), sems)


def cut(line, shrink_panels, expand_panels, size, replicas):
    out = ((2, 2, size // 4, shrink_panels.shape[1] // replicas, shrink_panels.shape[2] // size), BF16)
    return call(
        line,
        cut_kernel,
        "cut",
        (),
        (shrink_panels, expand_panels),
        [out, out],
        0,
        scratch=[pltpu.SemaphoreType.DMA((2 * size,))],
    )


def attention_kernel(
    lengths_ref, ids_ref, q_hbm, kc_hbm, vc_hbm, nk_hbm, nv_hbm, w_hbm, out_ref, own_ref, other_ref, *rest
):
    *piece_refs, q_ref, kc_ref, vc_ref, nk_ref, nv_ref, q_sems, w_sems = rest
    place = lax.axis_index("tp")
    steps, requests, width = q_ref.shape
    heads = width // HD
    cached, fresh = kc_ref.shape[0], nk_ref.shape[0]
    block = own_ref.shape[2]
    size = 2 * own_ref.shape[0]
    group_heads = size * width // kc_hbm.shape[2]
    head = pl.multiple_of(place * heads // group_heads * HD, HD)
    parts = 2
    part = requests // parts
    loads = []
    for n in range(parts):
        span = pl.ds(n * part, part)
        pieces = [(q_hbm.at[:, span, :], q_ref.at[:, span, :])]
        for a, b in ((kc_hbm, kc_ref), (nk_hbm, nk_ref), (vc_hbm, vc_ref), (nv_hbm, nv_ref)):
            pieces.append((a.at[:, span, pl.ds(head, HD)], b.at[:, span, :]))
        loads.append([pltpu.make_async_copy(a, b, q_sems.at[n, i]) for i, (a, b) in enumerate(pieces)])
    pair, mine = place // 2, place % 2
    others = []
    for ref, core in ((other_ref, 1 - mine), (own_ref, mine)):
        for i in range(ref.shape[0]):
            column = pl.multiple_of((2 * (i ^ pair) + core) * block, block)
            others.append((w_hbm.at[:, pl.ds(column, block)], ref.at[i]))
    others = [pltpu.make_async_copy(a, b, w_sems.at[i]) for i, (a, b) in enumerate(others)]
    for copy in [c for load in loads for c in load] + others:
        copy.start()

    group = GROUP_REQ
    rows, columns = steps * heads * group, (cached + fresh) * group
    row = lax.broadcasted_iota(jnp.int32, (rows, columns), 0)
    column = lax.broadcasted_iota(jnp.int32, (rows, columns), 1)
    same = row % group == column % group
    position = column // group
    step = row // (heads * group)
    fresh_ok = jnp.logical_and(position >= cached, position - cached <= step)
    column_position = lax.broadcasted_iota(jnp.int32, (1, columns), 1) // group
    tail = lax.broadcasted_iota(jnp.int32, (group, requests), 0) == 0
    out_ref[steps * requests :, :] = jnp.zeros((group, width), BF16)
    out_ref[steps * requests :, :requests] = jnp.where(tail, ids_ref[...].astype(F32), 0.0).astype(BF16)
    for n in range(parts):
        for copy in loads[n]:
            copy.wait()
        for i in range(n * part // group, (n + 1) * part // group):
            span = slice(i * group, (i + 1) * group)
            query = jnp.concatenate(
                [q_ref[s, span, h * HD : (h + 1) * HD] for s in range(steps) for h in range(heads)], 0
            )
            keys = jnp.concatenate(
                [kc_ref[p, span, :] for p in range(cached)] + [nk_ref[s, span, :] for s in range(fresh)], 0
            )
            values = jnp.concatenate(
                [vc_ref[p, span, :] for p in range(cached)] + [nv_ref[s, span, :] for s in range(fresh)], 0
            )
            scores = lax.dot_general(
                query, keys, (((1,), (1,)), ((), ())), preferred_element_type=F32
            ) * (1.0 / HD**0.5)
            limit = jnp.concatenate([lengths_ref[:, span]] * (cached + fresh), 1)
            cached_ok = column_position < limit
            visible = jnp.logical_and(same, jnp.logical_or(cached_ok, fresh_ok))
            scores = jnp.where(visible, scores, -1e30)
            scaled = jnp.exp(scores - scores.max(-1, keepdims=True))
            weights = (scaled / scaled.sum(-1, keepdims=True)).astype(BF16)
            mixed = jnp.dot(weights, values, preferred_element_type=F32).astype(BF16)
            for s in range(steps):
                for h in range(heads):
                    at = (s * heads + h) * group
                    to = s * requests + i * group
                    out_ref[to : to + group, h * HD : (h + 1) * HD] = mixed[at : at + group, :]
    first = 0
    for piece_ref in piece_refs:
        piece_ref[...] = out_ref[first : first + piece_ref.shape[0], :]
        first += piece_ref.shape[0]
    for copy in others:
        copy.wait()


def attend(line, queries, key_cache, value_cache, new_keys, new_values, cache_lengths, adapter_ids, weight, size, pieces):
    steps, requests, width = queries.shape
    cached = key_cache.shape[1]
    depth, full = weight.shape
    block, pairs = full // size, size // 2
    return call(
        line,
        attention_kernel,
        "attention",
        (cache_lengths.reshape(1, -1), adapter_ids.reshape(1, -1)),
        (queries, key_cache.transpose(1, 0, 2), value_cache.transpose(1, 0, 2), new_keys, new_values, weight),
        [
            ((steps * requests + GROUP_REQ, width), BF16),
            ((pairs, depth, block), BF16),
            ((pairs, depth, block), BF16),
        ]
        + [((piece, width), BF16) for piece in pieces],
        4 * requests * steps * width * (cached + steps) * GROUP_REQ,
        [
            pltpu.VMEM((steps, requests, width), BF16),
            pltpu.VMEM((cached, requests, HD), BF16),
            pltpu.VMEM((cached, requests, HD), BF16),
            pltpu.VMEM((steps, requests, HD), BF16),
            pltpu.VMEM((steps, requests, HD), BF16),
            pltpu.SemaphoreType.DMA((2, 5)),
            pltpu.SemaphoreType.DMA((2 * pairs,)),
        ],
    )


def product(spans, which, a_ref, b_ref, own_ref, other_ref):
    return jnp.dot(a_ref[spans[0], :], own_ref[which], preferred_element_type=F32) + jnp.dot(
        b_ref[spans[1], :], other_ref[which], preferred_element_type=F32
    )


def pack(small, blocks, width):
    part = small.shape[0] // blocks
    fold = part * LANES // width
    return [
        jnp.concatenate([small[i * part + j : i * part + j + fold] for j in range(0, part, fold)], 1)
        for i in range(blocks)
    ]


def unpack(blocks):
    return jnp.concatenate(
        [block[:, j : j + LANES] for block in blocks for j in range(0, block.shape[1], LANES)], 0
    )


def extra_rows(small, blocks, width):
    return 0 if small is None else small.size // (blocks * width)


def pass_small(small_ref, arrived_ref, more_ref, send_ref, rows):
    flat = small_ref[...].reshape(-1, LANES)
    flat = flat + unpack([arrived_ref[i, rows:, :].astype(F32) for i in range(arrived_ref.shape[0])])
    more_ref[...] = flat.reshape(more_ref.shape)
    if send_ref is not None:
        for i, block in enumerate(pack(flat.astype(BF16), send_ref.shape[0], send_ref.shape[2])):
            send_ref[i, rows:, :] = block


def far_kernel(spans, stage, *refs):
    operands, sent_refs, out_ref = refs[:4], refs[4:-1], refs[-1]
    rows = spans[0].stop - spans[0].start
    for i in range(out_ref.shape[0]):
        out_ref[i, :rows, :] = product(spans, put_bit(i, stage, 1), *operands).astype(BF16)
    for sent_ref in sent_refs:
        for i, block in enumerate(pack(sent_ref[...].reshape(-1, LANES), out_ref.shape[0], out_ref.shape[2])):
            out_ref[i, rows:, :] = block


def far(line, spans, stage, operands, sent=None):
    pairs, depth, width = operands[2].shape
    rows = spans[0].stop - spans[0].start
    more = extra_rows(sent, pairs // 2, width)
    return call(
        line,
        functools.partial(far_kernel, spans, stage),
        "far",
        operands if sent is None else (*operands, sent),
        (),
        [((pairs // 2, rows + more, width), BF16)],
        2 * rows * depth * pairs * width,
    )[0]


def near_kernel(spans, stage, following, *refs):
    operands, arrived_ref, refs = refs[:4], refs[4], refs[5:]
    rows = spans[0].stop - spans[0].start
    keep_ref, send_ref = refs[-2:]
    for i in range(keep_ref.shape[0]):
        for value, out_ref in ((1, send_ref), (0, keep_ref)):
            at = put_bit(i, following, value)
            total = product(spans, put_bit(at, stage, 0), *operands) + arrived_ref[at, :rows, :].astype(F32)
            out_ref[i, :rows, :] = total.astype(out_ref.dtype)
    if len(refs) > 2:
        pass_small(refs[0], arrived_ref, refs[1], send_ref, rows)


def near(line, spans, stage, following, operands, arrived, small=None):
    pairs, depth, width = operands[2].shape
    rows = spans[0].stop - spans[0].start
    more = extra_rows(small, pairs // 4, width)
    return call(
        line,
        functools.partial(near_kernel, spans, stage, following),
        "near",
        (*operands, arrived) if small is None else (*operands, arrived, small),
        (),
        ([] if small is None else [(small.shape, F32)])
        + [((pairs // 4, rows, width), F32), ((pairs // 4, rows + more, width), BF16)],
        2 * rows * depth * pairs * width,
    )


def add_kernel(following, keep_ref, arrived_ref, *refs):
    more_ref, send_ref = refs[-2:]
    rows = keep_ref.shape[1]
    for i in range(more_ref.shape[0]):
        for value, out_ref in ((1, send_ref), (0, more_ref)):
            at = put_bit(i, following, value)
            total = keep_ref[at] + arrived_ref[at, :rows, :].astype(F32)
            out_ref[i, :rows, :] = total.astype(out_ref.dtype)
    if len(refs) > 2:
        pass_small(refs[0], arrived_ref, refs[1], send_ref, rows)


def add(line, following, keep, arrived, small=None):
    blocks, rows, width = keep.shape
    more = extra_rows(small, blocks // 2, width)
    return call(
        line,
        functools.partial(add_kernel, following),
        "add",
        (keep, arrived) if small is None else (keep, arrived, small),
        (),
        ([] if small is None else [(small.shape, F32)])
        + [((blocks // 2, rows, width), F32), ((blocks // 2, rows + more, width), BF16)],
        2 * keep.size,
    )


def total_kernel(a_ref, b_ref, *out_refs):
    for out_ref in out_refs:
        out_ref[...] = (a_ref[...] + b_ref[...].astype(F32)).astype(out_ref.dtype)


def total(line, a, b):
    return call(line, total_kernel, "total", (a, b), (), [(a.shape, F32), (a.shape, BF16)], a.size)


def arrive_kernel(rows, small_ref, arrived_ref, *out_refs):
    flat = small_ref[...].reshape(-1, LANES) + unpack([arrived_ref[0, rows:, :].astype(F32)])
    small = flat.reshape(small_ref.shape).astype(BF16)
    for k, out_ref in enumerate(out_refs):
        out_ref[...] = small[k]


def arrive(line, rows, small, arrived):
    out = [(small.shape[1:], BF16)] * small.shape[0]
    return call(line, functools.partial(arrive_kernel, rows), "arrive", (small, arrived), (), out, 0)


def side_kernel(keep_ref, arrived_ref, more_ref, *send_refs):
    for source, ref in enumerate((keep_ref, arrived_ref)):
        more_ref[source] = ref[0]
        for panel, send_ref in enumerate(send_refs):
            send_ref[source] = ref[1, panel]


def side(line, keep, arrived, after):
    part = (keep.shape[:1] + keep.shape[2:], BF16)
    return call(line, side_kernel, "side", (keep, arrived), (), [(keep.shape, BF16), part, part], 0, after=after)


def sort_kernel(keep_ref, *refs):
    arrived_refs, out_refs = refs[:2], refs[2:]
    for high, out_ref in enumerate(out_refs):
        for side in range(2):
            for panel in range(2):
                out_ref[panel, 2 * side] = keep_ref[side, panel, high]
                out_ref[panel, 2 * side + 1] = arrived_refs[panel][side, high]


def sort(line, keep, arrived):
    groups, share, width = keep.shape[2:]
    return call(line, sort_kernel, "sort", (keep, *arrived), (), [((2, 4, share, width), BF16)] * groups, 0)


def far_blocks(blocks):
    size = 4 * len(blocks)
    return [blocks[0]] + [swap(b, "tp", 4 * h, size) for h, b in enumerate(blocks) if h]


def expanding_kernel(*refs):
    out_ref = refs[-1]
    for high, ref in enumerate(refs[:-1]):
        for source in range(4):
            out_ref[4 * high + source] = ref[1, source]


def expanding(line, blocks):
    share, width = blocks[0].shape[2:]
    out = [((4 * len(blocks), share, width), BF16)]
    return call(line, expanding_kernel, "expanding", blocks, (), out, 0)[0]


def owners(ids, shape, high, share):
    owner = 4 * high + lax.broadcasted_iota(jnp.int32, shape, 1) // share
    return owner == (ids ^ lax.axis_index("tp"))


def shrink_kernel(steps, groups, *refs):
    panels, attended, out_refs = refs[:groups], refs[groups:-2], refs[-2:]
    share, width = panels[0].shape[2:]
    for k, a_ref in enumerate(attended):
        rows = a_ref.shape[0] - GROUP_REQ
        requests = rows // steps
        row = lax.broadcasted_iota(jnp.int32, (requests, requests), 0)
        column = lax.broadcasted_iota(jnp.int32, (requests, requests), 1)
        line = a_ref[rows : rows + GROUP_REQ, :requests].astype(F32)[:1, :]
        ids = jnp.where(row == column, line, 0.0).sum(1, keepdims=True).astype(jnp.int32)
        ids = jnp.concatenate([ids] * steps, 0)
        total = None
        for high, panel in enumerate(panels):
            flat = panel[0].reshape(4 * share, width)
            ranks = lax.dot_general(
                a_ref[:rows, :], flat, (((1,), (1,)), ((), ())), preferred_element_type=F32
            )
            ranks = jnp.where(owners(ids, ranks.shape, high, share), ranks, 0.0)
            total = ranks if total is None else total + ranks
        part = total[:, :share]
        for i in range(1, 4):
            part = part + total[:, share * i : share * (i + 1)]
        fold = out_refs[0].shape[1]
        part = jnp.concatenate([part[i * fold : (i + 1) * fold] for i in range(rows // fold)], 1)
        for out_ref in out_refs:
            out_ref[k] = part.astype(out_ref.dtype)


def shrink(line, steps, panels, attended):
    replicas, rows, share = len(attended), attended[0].shape[0] - GROUP_REQ, panels[0].shape[2]
    return call(
        line,
        functools.partial(shrink_kernel, steps, len(panels)),
        "shrink",
        (*panels, *attended),
        (),
        [((replicas, rows * share // LANES, LANES), dtype) for dtype in (F32, BF16)],
        2 * rows * replicas * len(panels) * panels[0].size,
    )


def expand_kernel(steps, replicas, ids_ref, *refs):
    ranks, panels, out_ref = refs[:replicas], refs[replicas:-1], refs[-1]
    _, share, width = panels[0].shape
    ids = jnp.concatenate([ids_ref[...]] * steps, 0)
    total = None
    for k, rank_ref in enumerate(ranks):
        folded = rank_ref[...].astype(F32)
        part = jnp.concatenate([folded[:, i * share : (i + 1) * share] for i in range(LANES // share)], 0)
        part = jnp.concatenate([part] * 4, 1)
        panel = panels[k]
        spread = [
            jnp.where(owners(ids, part.shape, high, share), part, 0.0).astype(BF16)
            for high in range(panel.shape[0] // 4)
        ]
        term = jnp.dot(
            jnp.concatenate(spread, 1), panel[...].reshape(-1, width), preferred_element_type=F32
        )
        total = term if total is None else total + term
    out_ref[...] = total


def expand(line, steps, ids, ranks, panels):
    rows, width = steps * ids.shape[0], panels[0].shape[2]
    return call(
        line,
        functools.partial(expand_kernel, steps, len(ranks)),
        "expand",
        (ids, *ranks, *panels),
        (),
        [((rows, width), F32)],
        2 * rows * len(panels) * panels[0].size,
    )[0]


def fold_kernel(keep_ref, arrived_ref, out_ref):
    out_ref[...] = keep_ref[0] + arrived_ref[0, : keep_ref.shape[1], :].astype(F32)


def fold(line, terms):
    return call(line, fold_kernel, "fold", terms, (), [(terms[0].shape[1:], F32)], 0)[0]


def finish_kernel(spans, folded, lora_ref, *refs):
    refs, out_ref = refs[:-1], refs[-1]
    for n, span in enumerate(spans):
        if n < folded:
            total = refs[n][...]
        else:
            keep_ref, arrived_ref = refs[2 * n - folded : 2 * n - folded + 2]
            total = keep_ref[0] + arrived_ref[0, : keep_ref.shape[1], :].astype(F32)
        out_ref[span, :] = (total + lora_ref[span, :]).astype(BF16)


def finish(spans, lora, sums, terms):
    operands = [pltpu.with_memory_space_constraint(x, pltpu.VMEM) for x in (lora, *sums, *terms)]
    return pl.pallas_call(
        functools.partial(finish_kernel, spans, len(sums)),
        in_specs=[pl.BlockSpec(memory_space=pltpu.VMEM)] * len(operands),
        out_specs=pl.BlockSpec(memory_space=pltpu.VMEM),
        out_shape=jax.ShapeDtypeStruct(lora.shape, BF16),
        compiler_params=pltpu.CompilerParams(vmem_limit_bytes=VMEM_LIMIT),
        cost_estimate=pl.CostEstimate(flops=4 * lora.size, bytes_accessed=1 << 20, transcendentals=0),
        name="finish",
    )(*operands)


def swap(array, axis, bit, size):
    return lax.ppermute(array, axis, [(i, i ^ bit) for i in range(size)])


def body(
    size,
    replicas,
    queries,
    key_cache,
    value_cache,
    new_keys,
    new_values,
    cache_lengths,
    adapter_ids,
    out_weight,
    shrink_panels,
    expand_panels,
):
    steps, requests, local = queries.shape
    rows = steps * requests
    pairs = size // 2
    stages = size.bit_length() - 2
    if stages == 3:
        plan, first_piece, ride, steps_list = PLAN, FIRST_PIECE, RIDE, STEPS
    else:
        plan, first_piece, ride, steps_list = ((16, tuple(range(stages))),), 1, 0, PLAIN_STEPS
    spans, first = [], 0
    for part, _ in plan:
        spans.append(slice(first, first + rows * part // 16))
        first += rows * part // 16

    line = []
    last = len(plan) - 1
    keeps, cames, sums = {}, {}, {}

    def chunk(n):
        piece = 0 if n < first_piece else 1
        start = spans[first_piece].start if piece else 0
        there = slice(spans[n].start - start, spans[n].stop - start)
        return (spans[n], there), (attended, attended_other[piece], weight_own, weight_other)

    def begin(n):
        rows, operands = chunk(n)
        order = plan[n][1]
        block = far(line, rows, order[0], operands, sent if n == ride else None)
        cames[n] = swap(block, "tp", 2 << order[0], size)

    def middle(n):
        nonlocal shrunk
        rows, operands = chunk(n)
        order = plan[n][1]
        following = order[1] - (order[1] > order[0])
        *more, keeps[n], send = near(
            line, rows, order[0], following, operands, cames[n], shrunk if n == ride else None
        )
        shrunk = more[0] if more else shrunk
        cames[n] = swap(send, "tp", 2 << order[1], size)

    def end(n):
        nonlocal shrunk
        order = plan[n][1]
        for i in range(2, len(order)):
            left = order[i] - sum(order[i] > t for t in order[:i])
            *more, keeps[n], send = add(line, left, keeps[n], cames[n], shrunk if n == ride else None)
            shrunk = more[0] if more else shrunk
            cames[n] = swap(send, "tp", 2 << order[i], size)
        sums[n] = [keeps[n], cames[n]]

    cut_keep, cut_send = cut(line, shrink_panels, expand_panels, size, replicas)
    cut_came = swap(cut_send, "tp", 2, size)
    pieces = [spans[first_piece - 1].stop]
    if first_piece < len(plan):
        pieces.append(rows - pieces[0])
    attended, weight_own, picked, *attended_pieces = attend(
        line, queries, key_cache, value_cache, new_keys, new_values, cache_lengths, adapter_ids, out_weight, size, pieces
    )
    weight_other = swap(picked, "tp", 1, size)
    attended_other = [swap(piece, "tp", 1, size) for piece in attended_pieces]
    attended_all = [attended] + [swap(attended, "rep", k, replicas) for k in range(1, replicas)]

    shrunk = sent = panels = ranks = lora = None
    expanding_all = []
    for step in steps_list:
        name, n = (step[:-1], int(step[-1])) if step[-1].isdigit() else (step, 0)
        if name == "side":
            side_keep, *side_send = side(line, cut_keep, cut_came, ())
        elif name == "far":
            begin(n)
        elif name == "sort":
            panels = far_blocks(sort(line, side_keep, [swap(part, "tp", 1, size) for part in side_send]))
        elif name == "shrink":
            shrunk, sent = shrink(line, steps, panels, attended_all)
        elif name == "core":
            shrunk, sent = total(line, shrunk, swap(sent, "tp", 1, size))
        elif name == "ranks":
            rows_there = spans[ride].stop - spans[ride].start
            ranks = arrive(line, rows_there, shrunk, cames[ride])
            ranks = [ranks[0]] + [swap(ranks[k], "rep", k, replicas) for k in range(1, replicas)]
        elif name == "near":
            middle(n)
        elif name == "end":
            end(n)
        elif name == "fold":
            sums[n] = [fold(line, sums[n])]
        elif name == "expanding":
            expanding_all = [expanding(line, panels)]
            expanding_all += [swap(expanding_all[0], "rep", k, replicas) for k in range(1, replicas)]
        elif name == "expand":
            lora = expand(line, steps, adapter_ids, ranks, expanding_all)
        elif name == "have_x":
            line += attended_all[1:]
        elif name == "have_e":
            line += expanding_all[1:]
        elif name == "have":
            line.append(cames[n])
    order = sorted(range(last + 1), key=lambda n: len(sums[n]))
    ready = [sums[n][0] for n in order if len(sums[n]) == 1]
    terms = [x for n in order if len(sums[n]) == 2 for x in sums[n]]
    return finish([spans[n] for n in order], lora, ready, terms).reshape(queries.shape)


def solution(mesh):
    return jax.shard_map(
        functools.partial(body, mesh.shape["tp"], mesh.shape["rep"]),
        mesh=mesh,
        in_specs=(
            P(None, "rep", "tp"),
            P("rep", None, None),
            P("rep", None, None),
            P(None, "rep", None),
            P(None, "rep", None),
            P("rep"),
            P("rep", None),
            P("tp", None),
            P("tp", None, None),
            P("tp", None, None),
        ),
        out_specs=P(None, "rep", "tp"),
        check_vma=False,
    )
```

time: 105 us -> 100 us (0.952)
  starting transfers between devices: 37.9 us -> 33.8 us
  waiting for transfers between devices: 51 us -> 47.9 us
  local copies, waits for them, and re-layouts: 0.13 us -> 1.43 us
    ppermute x23 -> x25, starting transfers between devices: 37.9 us -> 33.8 us  [swap(): return lax.ppermute(array, axis, [(i, i ^ bit) for i in range(size)])]
    ppermute x23 -> x25, waiting for transfers between devices: 51 us -> 47.9 us  [swap(): return lax.ppermute(array, axis, [(i, i ^ bit) for i in range(size)])]
    unnamed x5 -> x7, local copies, waits for them, and re-layouts: 0.12 us -> 1.43 us
    pallas_call x22 -> x24, Pallas kernels: 14.8 us -> 15.7 us  [call(): pl.pallas_call(run, in_specs=[pl.BlockSpec(memory_space=pltpu.VMEM)] * le...]
  transfers between devices with their start and end apart: 23 -> 25, of which waited for: 13 -> 14; matrix products, arithmetic and copies ran while one was open for 0% -> 0% of each run, Pallas kernels for 11% -> 10%
where the time goes in v4:
time: 100 us; the launch traced here: 99.9 us
  waiting for transfers between devices  47.9 us (48%)
  starting transfers between devices  33.8 us (34%)
  Pallas kernels  16.6 us (17%)
  local copies, waits for them, and re-layouts  1.43 us (1%)
    ppermute x25, waiting for transfers between devices, swap(): return lax.ppermute(array, axis, [(i, i ^ bit) for i in range(size)])  47.9 us
    ppermute x25, starting transfers between devices, swap(): return lax.ppermute(array, axis, [(i, i ^ bit) for i in range(size)])  33.8 us
    pallas_call x24, Pallas kernels, call(): pl.pallas_call(run, in_specs=[pl.BlockSpec(memory_space=pltpu.VMEM)] * le...  15.7 us
  transfers between devices with their start and end apart: 25, of which 14 were waited for; matrix products, arithmetic and copies ran while one was open for 0% of the time, Pallas kernels for 10%

profile of v4, /device:TPU:0, one launch (start us, length us, event | category | flops | bytes accessed | tf_op | source)
XLA Modules:
  0.0 99.9 jit_solution(11571160676465469507)
XLA Ops:
  2.8 4.2 %attention.1 = (bf16[528,512]{1,0:T(8,128)(2,1)S(1)}, bf16[8,512,512]{2,1,0:T(8,128)(2,1)S(1)}, bf16[8,512,512]{2,1,0:T(8,128)(2,1)S(1)}, bf16[224,512]{1,0:T(8,128)(2,1)S(1)}, bf16[288,512]{1,0:T(8,128)(2,1)S(1)}) custom-call(s32[1,128]{1,0:T(1,128)S(1)} %bitcast.6, s32[1,128]{1,0:T(1,128)S(1)} %bitcast.5, bf16[4,128,512]{2,1,0:T(8,128)(2,1)} %refs_2_.1, ...), custom_call_target="tpu_custom_call" | custom-call | flops 268435456 | bytes 65536 | tf_op jit(solution)/shard_map/attention/pallas_call | solution.py:33
  8.0 2.6 %collective-permute-start.2 = (bf16[2,2,4,32,512]{4,3,2,1,0:T(8,128)(2,1)S(1)}, bf16[2,2,4,32,512]{4,3,2,1,0:T(8,128)(2,1)S(1)}, u32[]{:S(2)}, u32[]{:S(2)}) collective-permute-start(bf16[2,2,4,32,512]{4,3,2,1,0:T(8,128)(2,1)S(1)} %get-tuple-element.48), channel_id=1, source_target_pairs={{0,2},{1,3},{2,0},{3,1},{4,6},{5,7},{6,4},{7,5},{8,10},{9,11},{10,... | collective-permute-start | bytes 1572872 | tf_op jit(solution)/shard_map/ppermute | solution.py:498
  12.1 2.6 %collective-permute-done.refs_1_ = bf16[288,512]{1,0:T(8,128)(2,1)S(1)} collective-permute-done((bf16[288,512]{1,0:T(8,128)(2,1)S(1)}, bf16[288,512]{1,0:T(8,128)(2,1)S(1)}, u32[]{:S(2)}, u32[]{:S(2)}) %collective-permute-start) | collective-permute-done | bytes 294944 | tf_op jit(solution)/shard_map/ppermute | solution.py:498
  16.7 3.0 %collective-permute-start.11 = (bf16[4,224,512]{2,1,0:T(8,128)(2,1)S(1)}, bf16[4,224,512]{2,1,0:T(8,128)(2,1)S(1)}, u32[]{:S(2)}, u32[]{:S(2)}) collective-permute-start(bf16[4,224,512]{2,1,0:T(8,128)(2,1)S(1)} %far.5.refs_2_), channel_id=1, source_target_pairs={{0,2},{1,3},{2,0},{3,1},{4,6},{5,7},{6,4},{7,5},{8,10},{9,11},{10,... | collective-permute-start | bytes 2752520 | tf_op jit(solution)/shard_map/ppermute | solution.py:498
  19.6 1.6 %collective-permute-start.6 = (bf16[4,96,512]{2,1,0:T(8,128)(2,1)S(1)}, bf16[4,96,512]{2,1,0:T(8,128)(2,1)S(1)}, u32[]{:S(2)}, u32[]{:S(2)}) collective-permute-start(bf16[4,96,512]{2,1,0:T(8,128)(2,1)S(1)} %far.4.refs_4_), channel_id=1, source_target_pairs={{0,4},{1,5},{2,6},{3,7},{4,0},{5,1},{6,2},{7,3},{8,12},{9,13},{10,... | collective-permute-start | bytes 1179656 | tf_op jit(solution)/shard_map/ppermute | solution.py:498
  21.2 2.2 %collective-permute-done.2.refs_1_ = bf16[2,2,4,32,512]{4,3,2,1,0:T(8,128)(2,1)S(1)} collective-permute-done((bf16[2,2,4,32,512]{4,3,2,1,0:T(8,128)(2,1)S(1)}, bf16[2,2,4,32,512]{4,3,2,1,0:T(8,128)(2,1)S(1)}, u32[]{:S(2)}, u32[]{:S(2)}) %collective-permute-start.2) | collective-permute-done | bytes 524320 | tf_op jit(solution)/shard_map/ppermute | solution.py:498
  25.5 5.0 %collective-permute-done.6.refs_4_ = bf16[4,96,512]{2,1,0:T(8,128)(2,1)S(1)} collective-permute-done((bf16[4,96,512]{2,1,0:T(8,128)(2,1)S(1)}, bf16[4,96,512]{2,1,0:T(8,128)(2,1)S(1)}, u32[]{:S(2)}, u32[]{:S(2)}) %collective-permute-start.6) | collective-permute-done | bytes 393248 | tf_op jit(solution)/shard_map/ppermute | solution.py:498
  31.9 1.7 %collective-permute-start.7 = (bf16[2,4,32,512]{3,2,1,0:T(8,128)(2,1)S(1)}, bf16[2,4,32,512]{3,2,1,0:T(8,128)(2,1)S(1)}, u32[]{:S(2)}, u32[]{:S(2)}) collective-permute-start(bf16[2,4,32,512]{3,2,1,0:T(8,128)(2,1)S(1)} %get-tuple-element.54), channel_id=1, source_target_pairs={{0,4},{1,5},{2,6},{3,7},{4,0},{5,1},{6,2},{7,3},{8,12},{9,13},{10,... | collective-permute-start | bytes 786440 | tf_op jit(solution)/shard_map/ppermute | solution.py:498
  33.6 2.6 %collective-permute-start.8 = (bf16[2,4,32,512]{3,2,1,0:T(8,128)(2,1)S(1)}, bf16[2,4,32,512]{3,2,1,0:T(8,128)(2,1)S(1)}, u32[]{:S(2)}, u32[]{:S(2)}) collective-permute-start(bf16[2,4,32,512]{3,2,1,0:T(8,128)(2,1)S(1)} %get-tuple-element.55), channel_id=1, source_target_pairs={{0,8},{1,9},{2,10},{3,11},{4,12},{5,13},{6,14},{7,15},{8,0},{9,1},... | collective-permute-start | bytes 786440 | tf_op jit(solution)/shard_map/ppermute | solution.py:498
  36.3 6.8 %collective-permute-done.11.refs_4_ = bf16[4,224,512]{2,1,0:T(8,128)(2,1)S(1)} collective-permute-done((bf16[4,224,512]{2,1,0:T(8,128)(2,1)S(1)}, bf16[4,224,512]{2,1,0:T(8,128)(2,1)S(1)}, u32[]{:S(2)}, u32[]{:S(2)}) %collective-permute-start.11) | collective-permute-done | bytes 917536 | tf_op jit(solution)/shard_map/ppermute | solution.py:498
  44.2 2.1 %collective-permute-start.14 = (bf16[2,224,512]{2,1,0:T(8,128)(2,1)S(1)}, bf16[2,224,512]{2,1,0:T(8,128)(2,1)S(1)}, u32[]{:S(2)}, u32[]{:S(2)}) collective-permute-start(bf16[2,224,512]{2,1,0:T(8,128)(2,1)S(1)} %get-tuple-element.62), channel_id=1, source_target_pairs={{0,4},{1,5},{2,6},{3,7},{4,0},{5,1},{6,2},{7,3},{8,12},{9,13},{10,... | collective-permute-start | bytes 1376264 | tf_op jit(solution)/shard_map/ppermute | solution.py:498
  46.3 8.7 %collective-permute-done.8.refs_2_ = bf16[2,4,32,512]{3,2,1,0:T(8,128)(2,1)S(1)} collective-permute-done((bf16[2,4,32,512]{3,2,1,0:T(8,128)(2,1)S(1)}, bf16[2,4,32,512]{3,2,1,0:T(8,128)(2,1)S(1)}, u32[]{:S(2)}, u32[]{:S(2)}) %collective-permute-start.8) | collective-permute-done | bytes 262176 | tf_op jit(solution)/shard_map/ppermute | solution.py:498
  55.0 1.5 %shrink.1 = (f32[2,128,128]{2,1,0:T(8,128)S(1)}, bf16[2,128,128]{2,1,0:T(8,128)(2,1)S(1)}) custom-call(bf16[2,4,32,512]{3,2,1,0:T(8,128)(2,1)S(1)} %get-tuple-element.53.refs_4_.refs_0_, bf16[2,4,32,512]{3,2,1,0:T(8,128)(2,1)S(1)} %collective-permute-done.7.refs_1_, bf16[2,4,32,512]{3,2,1,0:T(8,128)(2,1)S(1)} %collective-permute-done.8.refs_2_, ...), custom_call_target="tpu_custom_call" | custom-call | flops 1073741824 | bytes 65536 | tf_op jit(solution)/shard_map/shrink/pallas_call | solution.py:33
  60.4 3.7 %collective-permute-start.19 = (bf16[2,160,512]{2,1,0:T(8,128)(2,1)S(1)}, bf16[2,160,512]{2,1,0:T(8,128)(2,1)S(1)}, u32[]{:S(2)}, u32[]{:S(2)}) collective-permute-start(bf16[2,160,512]{2,1,0:T(8,128)(2,1)S(1)} %get-tuple-element.71), channel_id=1, source_target_pairs={{0,4},{1,5},{2,6},{3,7},{4,0},{5,1},{6,2},{7,3},{8,12},{9,13},{10,... | collective-permute-start | bytes 983048 | tf_op jit(solution)/shard_map/ppermute | solution.py:498
  64.1 1.5 %collective-permute-start.23 = (bf16[16,32,512]{2,1,0:T(8,128)(2,1)S(1)}, bf16[16,32,512]{2,1,0:T(8,128)(2,1)S(1)}, u32[]{:S(2)}, u32[]{:S(2)}) collective-permute-start(bf16[16,32,512]{2,1,0:T(8,128)(2,1)S(1)} %expanding.1.refs_5_.refs_3_), channel_id=1, source_target_pairs={{0,16},{16,0},{1,17},{17,1},{2,18},{18,2},{3,19},{19,3},{4,20},{20... | collective-permute-start | bytes 1572872 | tf_op jit(solution)/shard_map/ppermute | solution.py:498
  65.6 1.5 %collective-permute-start.13 = (bf16[4,48,512]{2,1,0:T(8,128)(2,1)S(1)}, bf16[4,48,512]{2,1,0:T(8,128)(2,1)S(1)}, u32[]{:S(2)}, u32[]{:S(2)}) collective-permute-start(bf16[4,48,512]{2,1,0:T(8,128)(2,1)S(1)} %far.7.refs_4_), channel_id=1, source_target_pairs={{0,2},{1,3},{2,0},{3,1},{4,6},{5,7},{6,4},{7,5},{8,10},{9,11},{10,... | collective-permute-start | bytes 589832 | tf_op jit(solution)/shard_map/ppermute | solution.py:498
  68.9 4.5 %collective-permute-done.13.refs_4_ = bf16[4,48,512]{2,1,0:T(8,128)(2,1)S(1)} collective-permute-done((bf16[4,48,512]{2,1,0:T(8,128)(2,1)S(1)}, bf16[4,48,512]{2,1,0:T(8,128)(2,1)S(1)}, u32[]{:S(2)}, u32[]{:S(2)}) %collective-permute-start.13) | collective-permute-done | bytes 196640 | tf_op jit(solution)/shard_map/ppermute | solution.py:498
  74.3 2.6 %collective-permute-done.19.refs_1_ = bf16[2,160,512]{2,1,0:T(8,128)(2,1)S(1)} collective-permute-done((bf16[2,160,512]{2,1,0:T(8,128)(2,1)S(1)}, bf16[2,160,512]{2,1,0:T(8,128)(2,1)S(1)}, u32[]{:S(2)}, u32[]{:S(2)}) %collective-permute-start.19) | collective-permute-done | bytes 327712 | tf_op jit(solution)/shard_map/ppermute | solution.py:498
  77.5 2.3 %collective-permute-done.18.refs_1_ = bf16[1,224,512]{2,1,0:T(8,128)(2,1)S(1)} collective-permute-done((bf16[1,224,512]{2,1,0:T(8,128)(2,1)S(1)}, bf16[1,224,512]{2,1,0:T(8,128)(2,1)S(1)}, u32[]{:S(2)}, u32[]{:S(2)}) %collective-permute-start.18) | collective-permute-done | bytes 229408 | tf_op jit(solution)/shard_map/ppermute | solution.py:498
  80.0 3.6 %collective-permute-start.20 = (bf16[1,96,512]{2,1,0:T(8,128)(2,1)S(1)}, bf16[1,96,512]{2,1,0:T(8,128)(2,1)S(1)}, u32[]{:S(2)}, u32[]{:S(2)}) collective-permute-start(bf16[1,96,512]{2,1,0:T(8,128)(2,1)S(1)} %get-tuple-element.75), channel_id=1, source_target_pairs={{0,8},{1,9},{2,10},{3,11},{4,12},{5,13},{6,14},{7,15},{8,0},{9,1},... | collective-permute-start | bytes 294920 | tf_op jit(solution)/shard_map/ppermute | solution.py:498
  83.6 6.7 %collective-permute-done.21.refs_1_ = bf16[1,160,512]{2,1,0:T(8,128)(2,1)S(1)} collective-permute-done((bf16[1,160,512]{2,1,0:T(8,128)(2,1)S(1)}, bf16[1,160,512]{2,1,0:T(8,128)(2,1)S(1)}, u32[]{:S(2)}, u32[]{:S(2)}) %collective-permute-start.21) | collective-permute-done | bytes 163872 | tf_op jit(solution)/shard_map/ppermute | solution.py:498
  90.3 1.9 %collective-permute-done.20.refs_1_.refs_4_ = bf16[1,96,512]{2,1,0:T(8,128)(2,1)S(1)} collective-permute-done((bf16[1,96,512]{2,1,0:T(8,128)(2,1)S(1)}, bf16[1,96,512]{2,1,0:T(8,128)(2,1)S(1)}, u32[]{:S(2)}, u32[]{:S(2)}) %collective-permute-start.20) | collective-permute-done | bytes 98336 | tf_op jit(solution)/shard_map/ppermute | solution.py:498
  92.2 4.0 %collective-permute-start.22 = (bf16[128,128]{1,0:T(8,128)(2,1)S(1)}, bf16[128,128]{1,0:T(8,128)(2,1)S(1)}, u32[]{:S(2)}, u32[]{:S(2)}) collective-permute-start(bf16[128,128]{1,0:T(8,128)(2,1)S(1)} %get-tuple-element.79), channel_id=1, source_target_pairs={{0,16},{16,0},{1,17},{17,1},{2,18},{18,2},{3,19},{19,3},{4,20},{20... | collective-permute-start | bytes 98312 | tf_op jit(solution)/shard_map/ppermute | solution.py:498
  96.4 1.8 %collective-permute-done.22.refs_2_ = bf16[128,128]{1,0:T(8,128)(2,1)S(1)} collective-permute-done((bf16[128,128]{1,0:T(8,128)(2,1)S(1)}, bf16[128,128]{1,0:T(8,128)(2,1)S(1)}, u32[]{:S(2)}, u32[]{:S(2)}) %collective-permute-start.22) | collective-permute-done | bytes 32800 | tf_op jit(solution)/shard_map/ppermute | solution.py:498
  (58 shorter events, 20.9 us)
Async XLA Ops:
  7.0 7.7 %collective-permute-start.1 = (bf16[8,512,512]{2,1,0:T(8,128)(2,1)S(1)}, bf16[8,512,512]{2,1,0:T(8,128)(2,1)S(1)}, u32[]{:S(2)}, u32[]{:S(2)}) collective-permute-start(bf16[8,512,512]{2,1,0:T(8,128)(2,1)S(1)} %get-tuple-element.47), channel_id=1, source_target_pairs={{0,1},{1,0},{2,3},{3,2},{4,5},{5,4},{6,7},{7,6},{8,9},{9,8},{10,11... | collective-permute-start | bytes 12582920 | tf_op jit(solution)/shard_map/ppermute | solution.py:498
  7.5 7.2 %collective-permute-start = (bf16[288,512]{1,0:T(8,128)(2,1)S(1)}, bf16[288,512]{1,0:T(8,128)(2,1)S(1)}, u32[]{:S(2)}, u32[]{:S(2)}) collective-permute-start(bf16[288,512]{1,0:T(8,128)(2,1)S(1)} %get-tuple-element.45), channel_id=1, source_target_pairs={{0,1},{1,0},{2,3},{3,2},{4,5},{5,4},{6,7},{7,6},{8,9},{9,8},{10,11... | collective-permute-start | bytes 884744 | tf_op jit(solution)/shard_map/ppermute | solution.py:498
  7.6 7.9 %collective-permute-start.3 = (bf16[224,512]{1,0:T(8,128)(2,1)S(1)}, bf16[224,512]{1,0:T(8,128)(2,1)S(1)}, u32[]{:S(2)}, u32[]{:S(2)}) collective-permute-start(bf16[224,512]{1,0:T(8,128)(2,1)S(1)} %get-tuple-element.49.refs_4_), channel_id=1, source_target_pairs={{0,1},{1,0},{2,3},{3,2},{4,5},{5,4},{6,7},{7,6},{8,9},{9,8},{10,11... | collective-permute-start | bytes 688136 | tf_op jit(solution)/shard_map/ppermute | solution.py:498
  8.0 15.4 %collective-permute-start.2 = (bf16[2,2,4,32,512]{4,3,2,1,0:T(8,128)(2,1)S(1)}, bf16[2,2,4,32,512]{4,3,2,1,0:T(8,128)(2,1)S(1)}, u32[]{:S(2)}, u32[]{:S(2)}) collective-permute-start(bf16[2,2,4,32,512]{4,3,2,1,0:T(8,128)(2,1)S(1)} %get-tuple-element.48), channel_id=1, source_target_pairs={{0,2},{1,3},{2,0},{3,1},{4,6},{5,7},{6,4},{7,5},{8,10},{9,11},{10,... | collective-permute-start | bytes 1572872 | tf_op jit(solution)/shard_map/ppermute | solution.py:498
  10.6 19.9 %collective-permute-start.10 = (bf16[528,512]{1,0:T(8,128)(2,1)S(1)}, bf16[528,512]{1,0:T(8,128)(2,1)S(1)}, u32[]{:S(2)}, u32[]{:S(2)}) collective-permute-start(bf16[528,512]{1,0:T(8,128)(2,1)S(1)} %get-tuple-element.44.refs_0_.refs_4_), channel_id=1, source_target_pairs={{0,16},{16,0},{1,17},{17,1},{2,18},{18,2},{3,19},{19,3},{4,20},{20... | collective-permute-start | bytes 1622024 | tf_op jit(solution)/shard_map/ppermute | solution.py:498
  16.7 26.4 %collective-permute-start.11 = (bf16[4,224,512]{2,1,0:T(8,128)(2,1)S(1)}, bf16[4,224,512]{2,1,0:T(8,128)(2,1)S(1)}, u32[]{:S(2)}, u32[]{:S(2)}) collective-permute-start(bf16[4,224,512]{2,1,0:T(8,128)(2,1)S(1)} %far.5.refs_2_), channel_id=1, source_target_pairs={{0,2},{1,3},{2,0},{3,1},{4,6},{5,7},{6,4},{7,5},{8,10},{9,11},{10,... | collective-permute-start | bytes 2752520 | tf_op jit(solution)/shard_map/ppermute | solution.py:498
  19.6 10.9 %collective-permute-start.6 = (bf16[4,96,512]{2,1,0:T(8,128)(2,1)S(1)}, bf16[4,96,512]{2,1,0:T(8,128)(2,1)S(1)}, u32[]{:S(2)}, u32[]{:S(2)}) collective-permute-start(bf16[4,96,512]{2,1,0:T(8,128)(2,1)S(1)} %far.4.refs_4_), channel_id=1, source_target_pairs={{0,4},{1,5},{2,6},{3,7},{4,0},{5,1},{6,2},{7,3},{8,12},{9,13},{10,... | collective-permute-start | bytes 1179656 | tf_op jit(solution)/shard_map/ppermute | solution.py:498
  23.5 1.6 %collective-permute-start.4 = (bf16[2,4,32,512]{3,2,1,0:T(8,128)(2,1)S(1)}, bf16[2,4,32,512]{3,2,1,0:T(8,128)(2,1)S(1)}, u32[]{:S(2)}, u32[]{:S(2)}) collective-permute-start(bf16[2,4,32,512]{3,2,1,0:T(8,128)(2,1)S(1)} %get-tuple-element.51.refs_3_), channel_id=1, source_target_pairs={{0,1},{1,0},{2,3},{3,2},{4,5},{5,4},{6,7},{7,6},{8,9},{9,8},{10,11... | collective-permute-start | bytes 786440 | tf_op jit(solution)/shard_map/ppermute | solution.py:498
  23.6 1.9 %collective-permute-start.5 = (bf16[2,4,32,512]{3,2,1,0:T(8,128)(2,1)S(1)}, bf16[2,4,32,512]{3,2,1,0:T(8,128)(2,1)S(1)}, u32[]{:S(2)}, u32[]{:S(2)}) collective-permute-start(bf16[2,4,32,512]{3,2,1,0:T(8,128)(2,1)S(1)} %get-tuple-element.52), channel_id=1, source_target_pairs={{0,1},{1,0},{2,3},{3,2},{4,5},{5,4},{6,7},{7,6},{8,9},{9,8},{10,11... | collective-permute-start | bytes 786440 | tf_op jit(solution)/shard_map/ppermute | solution.py:498
  31.4 28.1 %collective-permute-start.15 = (bf16[4,160,512]{2,1,0:T(8,128)(2,1)S(1)}, bf16[4,160,512]{2,1,0:T(8,128)(2,1)S(1)}, u32[]{:S(2)}, u32[]{:S(2)}) collective-permute-start(bf16[4,160,512]{2,1,0:T(8,128)(2,1)S(1)} %far.6.refs_5_), channel_id=1, source_target_pairs={{0,2},{1,3},{2,0},{3,1},{4,6},{5,7},{6,4},{7,5},{8,10},{9,11},{10,... | collective-permute-start | bytes 1966088 | tf_op jit(solution)/shard_map/ppermute | solution.py:498
  31.9 14.4 %collective-permute-start.7 = (bf16[2,4,32,512]{3,2,1,0:T(8,128)(2,1)S(1)}, bf16[2,4,32,512]{3,2,1,0:T(8,128)(2,1)S(1)}, u32[]{:S(2)}, u32[]{:S(2)}) collective-permute-start(bf16[2,4,32,512]{3,2,1,0:T(8,128)(2,1)S(1)} %get-tuple-element.54), channel_id=1, source_target_pairs={{0,4},{1,5},{2,6},{3,7},{4,0},{5,1},{6,2},{7,3},{8,12},{9,13},{10,... | collective-permute-start | bytes 786440 | tf_op jit(solution)/shard_map/ppermute | solution.py:498
  33.6 21.4 %collective-permute-start.8 = (bf16[2,4,32,512]{3,2,1,0:T(8,128)(2,1)S(1)}, bf16[2,4,32,512]{3,2,1,0:T(8,128)(2,1)S(1)}, u32[]{:S(2)}, u32[]{:S(2)}) collective-permute-start(bf16[2,4,32,512]{3,2,1,0:T(8,128)(2,1)S(1)} %get-tuple-element.55), channel_id=1, source_target_pairs={{0,8},{1,9},{2,10},{3,11},{4,12},{5,13},{6,14},{7,15},{8,0},{9,1},... | collective-permute-start | bytes 786440 | tf_op jit(solution)/shard_map/ppermute | solution.py:498
  36.2 18.8 %collective-permute-start.9 = (bf16[2,4,32,512]{3,2,1,0:T(8,128)(2,1)S(1)}, bf16[2,4,32,512]{3,2,1,0:T(8,128)(2,1)S(1)}, u32[]{:S(2)}, u32[]{:S(2)}) collective-permute-start(bf16[2,4,32,512]{3,2,1,0:T(8,128)(2,1)S(1)} %get-tuple-element.56), channel_id=1, source_target_pairs={{0,12},{1,13},{2,14},{3,15},{4,8},{5,9},{6,10},{7,11},{8,4},{9,5},... | collective-permute-start | bytes 786440 | tf_op jit(solution)/shard_map/ppermute | solution.py:498
  44.2 22.9 %collective-permute-start.14 = (bf16[2,224,512]{2,1,0:T(8,128)(2,1)S(1)}, bf16[2,224,512]{2,1,0:T(8,128)(2,1)S(1)}, u32[]{:S(2)}, u32[]{:S(2)}) collective-permute-start(bf16[2,224,512]{2,1,0:T(8,128)(2,1)S(1)} %get-tuple-element.62), channel_id=1, source_target_pairs={{0,4},{1,5},{2,6},{3,7},{4,0},{5,1},{6,2},{7,3},{8,12},{9,13},{10,... | collective-permute-start | bytes 1376264 | tf_op jit(solution)/shard_map/ppermute | solution.py:498
  60.4 16.5 %collective-permute-start.19 = (bf16[2,160,512]{2,1,0:T(8,128)(2,1)S(1)}, bf16[2,160,512]{2,1,0:T(8,128)(2,1)S(1)}, u32[]{:S(2)}, u32[]{:S(2)}) collective-permute-start(bf16[2,160,512]{2,1,0:T(8,128)(2,1)S(1)} %get-tuple-element.71), channel_id=1, source_target_pairs={{0,4},{1,5},{2,6},{3,7},{4,0},{5,1},{6,2},{7,3},{8,12},{9,13},{10,... | collective-permute-start | bytes 983048 | tf_op jit(solution)/shard_map/ppermute | solution.py:498
  64.1 32.3 %collective-permute-start.23 = (bf16[16,32,512]{2,1,0:T(8,128)(2,1)S(1)}, bf16[16,32,512]{2,1,0:T(8,128)(2,1)S(1)}, u32[]{:S(2)}, u32[]{:S(2)}) collective-permute-start(bf16[16,32,512]{2,1,0:T(8,128)(2,1)S(1)} %expanding.1.refs_5_.refs_3_), channel_id=1, source_target_pairs={{0,16},{16,0},{1,17},{17,1},{2,18},{18,2},{3,19},{19,3},{4,20},{20... | collective-permute-start | bytes 1572872 | tf_op jit(solution)/shard_map/ppermute | solution.py:498
  65.6 7.8 %collective-permute-start.13 = (bf16[4,48,512]{2,1,0:T(8,128)(2,1)S(1)}, bf16[4,48,512]{2,1,0:T(8,128)(2,1)S(1)}, u32[]{:S(2)}, u32[]{:S(2)}) collective-permute-start(bf16[4,48,512]{2,1,0:T(8,128)(2,1)S(1)} %far.7.refs_4_), channel_id=1, source_target_pairs={{0,2},{1,3},{2,0},{3,1},{4,6},{5,7},{6,4},{7,5},{8,10},{9,11},{10,... | collective-permute-start | bytes 589832 | tf_op jit(solution)/shard_map/ppermute | solution.py:498
  67.2 12.6 %collective-permute-start.18 = (bf16[1,224,512]{2,1,0:T(8,128)(2,1)S(1)}, bf16[1,224,512]{2,1,0:T(8,128)(2,1)S(1)}, u32[]{:S(2)}, u32[]{:S(2)}) collective-permute-start(bf16[1,224,512]{2,1,0:T(8,128)(2,1)S(1)} %get-tuple-element.70), channel_id=1, source_target_pairs={{0,8},{1,9},{2,10},{3,11},{4,12},{5,13},{6,14},{7,15},{8,0},{9,1},... | collective-permute-start | bytes 688136 | tf_op jit(solution)/shard_map/ppermute | solution.py:498
  68.3 11.5 %collective-permute-start.17 = (bf16[2,96,512]{2,1,0:T(8,128)(2,1)S(1)}, bf16[2,96,512]{2,1,0:T(8,128)(2,1)S(1)}, u32[]{:S(2)}, u32[]{:S(2)}) collective-permute-start(bf16[2,96,512]{2,1,0:T(8,128)(2,1)S(1)} %get-tuple-element.69), channel_id=1, source_target_pairs={{0,2},{1,3},{2,0},{3,1},{4,6},{5,7},{6,4},{7,5},{8,10},{9,11},{10,... | collective-permute-start | bytes 589832 | tf_op jit(solution)/shard_map/ppermute | solution.py:498
  74.2 5.7 %collective-permute-start.16 = (bf16[2,64,512]{2,1,0:T(8,128)(2,1)S(1)}, bf16[2,64,512]{2,1,0:T(8,128)(2,1)S(1)}, u32[]{:S(2)}, u32[]{:S(2)}) collective-permute-start(bf16[2,64,512]{2,1,0:T(8,128)(2,1)S(1)} %get-tuple-element.67), channel_id=1, source_target_pairs={{0,4},{1,5},{2,6},{3,7},{4,0},{5,1},{6,2},{7,3},{8,12},{9,13},{10,... | collective-permute-start | bytes 393224 | tf_op jit(solution)/shard_map/ppermute | solution.py:498
  77.0 13.3 %collective-permute-start.21 = (bf16[1,160,512]{2,1,0:T(8,128)(2,1)S(1)}, bf16[1,160,512]{2,1,0:T(8,128)(2,1)S(1)}, u32[]{:S(2)}, u32[]{:S(2)}) collective-permute-start(bf16[1,160,512]{2,1,0:T(8,128)(2,1)S(1)} %get-tuple-element.76), channel_id=1, source_target_pairs={{0,8},{1,9},{2,10},{3,11},{4,12},{5,13},{6,14},{7,15},{8,0},{9,1},... | collective-permute-start | bytes 491528 | tf_op jit(solution)/shard_map/ppermute | solution.py:498
  80.0 12.3 %collective-permute-start.20 = (bf16[1,96,512]{2,1,0:T(8,128)(2,1)S(1)}, bf16[1,96,512]{2,1,0:T(8,128)(2,1)S(1)}, u32[]{:S(2)}, u32[]{:S(2)}) collective-permute-start(bf16[1,96,512]{2,1,0:T(8,128)(2,1)S(1)} %get-tuple-element.75), channel_id=1, source_target_pairs={{0,8},{1,9},{2,10},{3,11},{4,12},{5,13},{6,14},{7,15},{8,0},{9,1},... | collective-permute-start | bytes 294920 | tf_op jit(solution)/shard_map/ppermute | solution.py:498
  83.5 15.5 %collective-permute-start.24 = (bf16[1,96,512]{2,1,0:T(8,128)(2,1)S(1)}, bf16[1,96,512]{2,1,0:T(8,128)(2,1)S(1)}, u32[]{:S(2)}, u32[]{:S(2)}) collective-permute-start(bf16[1,96,512]{2,1,0:T(8,128)(2,1)S(1)} %get-tuple-element.80), channel_id=1, source_target_pairs={{0,8},{1,9},{2,10},{3,11},{4,12},{5,13},{6,14},{7,15},{8,0},{9,1},... | collective-permute-start | bytes 294920 | tf_op jit(solution)/shard_map/ppermute | solution.py:498
  92.2 5.9 %collective-permute-start.22 = (bf16[128,128]{1,0:T(8,128)(2,1)S(1)}, bf16[128,128]{1,0:T(8,128)(2,1)S(1)}, u32[]{:S(2)}, u32[]{:S(2)}) collective-permute-start(bf16[128,128]{1,0:T(8,128)(2,1)S(1)} %get-tuple-element.79), channel_id=1, source_target_pairs={{0,16},{16,0},{1,17},{17,1},{2,18},{18,2},{3,19},{19,3},{4,20},{20... | collective-permute-start | bytes 98312 | tf_op jit(solution)/shard_map/ppermute | solution.py:498
  (4 other events, 24.7 us)

commit v5 on v4

--- a/solution.py
+++ b/solution.py
@@ -13,12 +13,37 @@
 VMEM_LIMIT = 24 << 20
 F32 = jnp.float32
 BF16 = jnp.bfloat16
-PLAN = ((7, (0, 1, 2)), (5, (0, 1, 2)), (1, (0, 1, 2)), (3, (1, 0, 2)))
-FIRST_PIECE = 1
+PLAN = ((8, (0, 1, 2)), (4, (0, 1, 2)), (1, (0, 1, 2)), (3, (1, 0, 2)))
+FIRST_PIECE = 4
 RIDE = 2
-STEPS = ('far3', 'far0', 'side', 'have3', 'sort', 'have_x', 'far1', 'near0', 'shrink', 'core', 'far2', 'expanding', 'near3', 'near1', 'end0', 'near2', 'end1', 'fold0', 'end3', 'end2', 'fold1', 'ranks', 'expand', 'fold3')
-PLAIN_STEPS = ("side", "sort", "shrink", "core", "far0", "near0", "end0", "ranks", "expanding", "expand")
-COST = 1
+STEPS = (
+    "side",
+    "far3",
+    "far0",
+    "sort",
+    "have_x",
+    "far1",
+    "have3",
+    "near0",
+    "shrink",
+    "core",
+    "cross",
+    "expanding",
+    "far2",
+    "near3",
+    "near1",
+    "end0",
+    "near2",
+    "end1",
+    "fold0",
+    "end3",
+    "end2",
+    "fold1",
+    "ranks",
+    "expand",
+    "fold3",
+)
+PLAIN_STEPS = ("side", "sort", "shrink", "core", "cross", "far0", "near0", "end0", "ranks", "expanding", "expand")
 
 
 def call(line, kernel, name, vmem, hbm, out, cost, scratch=(), after=()):
@@ -39,7 +64,7 @@
         out_shape=[pltpu.VMEM(shape, dtype) for shape, dtype in out],
         scratch_shapes=scratch,
         compiler_params=pltpu.CompilerParams(vmem_limit_bytes=VMEM_LIMIT),
-        cost_estimate=pl.CostEstimate(flops=COST * cost, bytes_accessed=1 << 16, transcendentals=0),
+        cost_estimate=pl.CostEstimate(flops=cost, bytes_accessed=1 << 16, transcendentals=0),
         name=name,
     )(*operands, *before)
     line[:] = [min(results, key=lambda x: x.size)]
@@ -72,28 +97,36 @@
         copy.wait()
 
 
-def cut_kernel(shrink_ref, expand_ref, keep_ref, send_ref, sems):
+def pick_kernel(w_ref, shrink_ref, expand_ref, pick_ref, keep_ref, send_ref, sems):
     place, replica = lax.axis_index("tp"), lax.axis_index("rep")
-    copies = cut_copies(shrink_ref, keep_ref, send_ref, 0, place, replica)
-    run_copies(copies + cut_copies(expand_ref, keep_ref, send_ref, 1, place, replica), sems)
-
-
-def cut(line, shrink_panels, expand_panels, size, replicas):
-    out = ((2, 2, size // 4, shrink_panels.shape[1] // replicas, shrink_panels.shape[2] // size), BF16)
+    pairs, _, width = pick_ref.shape
+    copies = []
+    for i in range(pairs):
+        column = pl.multiple_of((2 * (i ^ (place // 2)) + 1 - place % 2) * width, width)
+        copies.append((w_ref.at[:, pl.ds(column, width)], pick_ref.at[i]))
+    copies += cut_copies(shrink_ref, keep_ref, send_ref, 0, place, replica)
+    copies += cut_copies(expand_ref, keep_ref, send_ref, 1, place, replica)
+    run_copies(copies, sems)
+
+
+def pick(line, weight, shrink_panels, expand_panels, size, replicas):
+    depth, full = weight.shape
+    pairs, width = size // 2, full // size
+    cut = ((2, 2, size // 4, shrink_panels.shape[1] // replicas, width), BF16)
     return call(
         line,
-        cut_kernel,
-        "cut",
+        pick_kernel,
+        "pick",
         (),
-        (shrink_panels, expand_panels),
-        [out, out],
+        (weight, shrink_panels, expand_panels),
+        [((pairs, depth, width), BF16), cut, cut],
         0,
-        scratch=[pltpu.SemaphoreType.DMA((2 * size,))],
+        scratch=[pltpu.SemaphoreType.DMA((pairs + 2 * size,))],
     )
 
 
 def attention_kernel(
-    lengths_ref, ids_ref, q_hbm, kc_hbm, vc_hbm, nk_hbm, nv_hbm, w_hbm, out_ref, own_ref, other_ref, *rest
+    lengths_ref, ids_ref, q_hbm, kc_hbm, vc_hbm, nk_hbm, nv_hbm, w_hbm, out_ref, own_ref, *rest
 ):
     *piece_refs, q_ref, kc_ref, vc_ref, nk_ref, nv_ref, q_sems, w_sems = rest
     place = lax.axis_index("tp")
@@ -115,10 +148,9 @@
         loads.append([pltpu.make_async_copy(a, b, q_sems.at[n, i]) for i, (a, b) in enumerate(pieces)])
     pair, mine = place // 2, place % 2
     others = []
-    for ref, core in ((other_ref, 1 - mine), (own_ref, mine)):
-        for i in range(ref.shape[0]):
-            column = pl.multiple_of((2 * (i ^ pair) + core) * block, block)
-            others.append((w_hbm.at[:, pl.ds(column, block)], ref.at[i]))
+    for i in range(own_ref.shape[0]):
+        column = pl.multiple_of((2 * (i ^ pair) + mine) * block, block)
+        others.append((w_hbm.at[:, pl.ds(column, block)], own_ref.at[i]))
     others = [pltpu.make_async_copy(a, b, w_sems.at[i]) for i, (a, b) in enumerate(others)]
     for copy in [c for load in loads for c in load] + others:
         copy.start()
@@ -186,7 +218,6 @@
         [
             ((steps * requests + GROUP_REQ, width), BF16),
             ((pairs, depth, block), BF16),
-            ((pairs, depth, block), BF16),
         ]
         + [((piece, width), BF16) for piece in pieces],
         4 * requests * steps * width * (cached + steps) * GROUP_REQ,
@@ -197,7 +228,7 @@
             pltpu.VMEM((steps, requests, HD), BF16),
             pltpu.VMEM((steps, requests, HD), BF16),
             pltpu.SemaphoreType.DMA((2, 5)),
-            pltpu.SemaphoreType.DMA((2 * pairs,)),
+            pltpu.SemaphoreType.DMA((pairs,)),
         ],
     )
 
@@ -317,13 +348,27 @@
     )
 
 
-def total_kernel(a_ref, b_ref, *out_refs):
-    for out_ref in out_refs:
-        out_ref[...] = (a_ref[...] + b_ref[...].astype(F32)).astype(out_ref.dtype)
+def total_kernel(a_ref, b_ref, out_ref, *sent_refs):
+    out_ref[...] = a_ref[...] + b_ref[...].astype(F32)
+    for k, sent_ref in enumerate(sent_refs):
+        sent_ref[...] = out_ref[k + 1].astype(BF16)
 
 
 def total(line, a, b):
-    return call(line, total_kernel, "total", (a, b), (), [(a.shape, F32), (a.shape, BF16)], a.size)
+    out = [(a.shape, F32)] + [(a.shape[1:], BF16)] * (a.shape[0] - 1)
+    return call(line, total_kernel, "total", (a, b), (), out, a.size)
+
+
+def cross_kernel(a_ref, *refs):
+    arrived_refs, (out_ref, sent_ref) = refs[:-2], refs[-2:]
+    out_ref[0] = a_ref[0]
+    for k, ref in enumerate(arrived_refs):
+        out_ref[k + 1] = ref[...].astype(F32)
+    sent_ref[...] = out_ref[...].astype(BF16)
+
+
+def cross(line, a, arrived):
+    return call(line, cross_kernel, "cross", (a, *arrived), (), [(a.shape, F32), (a.shape, BF16)], 0)
 
 
 def arrive_kernel(rows, small_ref, arrived_ref, *out_refs):
@@ -562,15 +607,15 @@
             cames[n] = swap(send, "tp", 2 << order[i], size)
         sums[n] = [keeps[n], cames[n]]
 
-    cut_keep, cut_send = cut(line, shrink_panels, expand_panels, size, replicas)
+    picked, cut_keep, cut_send = pick(line, out_weight, shrink_panels, expand_panels, size, replicas)
+    weight_other = swap(picked, "tp", 1, size)
     cut_came = swap(cut_send, "tp", 2, size)
     pieces = [spans[first_piece - 1].stop]
     if first_piece < len(plan):
         pieces.append(rows - pieces[0])
-    attended, weight_own, picked, *attended_pieces = attend(
+    attended, weight_own, *attended_pieces = attend(
         line, queries, key_cache, value_cache, new_keys, new_values, cache_lengths, adapter_ids, out_weight, size, pieces
     )
-    weight_other = swap(picked, "tp", 1, size)
     attended_other = [swap(piece, "tp", 1, size) for piece in attended_pieces]
     attended_all = [attended] + [swap(attended, "rep", k, replicas) for k in range(1, replicas)]
 
@@ -587,11 +632,13 @@
         elif name == "shrink":
             shrunk, sent = shrink(line, steps, panels, attended_all)
         elif name == "core":
-            shrunk, sent = total(line, shrunk, swap(sent, "tp", 1, size))
+            shrunk, *parts = total(line, shrunk, swap(sent, "tp", 1, size))
+            parts = [swap(part, "rep", k + 1, replicas) for k, part in enumerate(parts)]
+        elif name == "cross":
+            shrunk, sent = cross(line, shrunk, parts)
         elif name == "ranks":
             rows_there = spans[ride].stop - spans[ride].start
             ranks = arrive(line, rows_there, shrunk, cames[ride])
-            ranks = [ranks[0]] + [swap(ranks[k], "rep", k, replicas) for k in range(1, replicas)]
         elif name == "near":
             middle(n)
         elif name == "end":

time: 100 us -> 95.3 us (0.953)
  starting transfers between devices: 33.8 us -> 29.5 us
  local copies, waits for them, and re-layouts: 1.43 us -> 0.12 us
    ppermute x25 -> x24, starting transfers between devices: 33.8 us -> 29.5 us  [swap(): return lax.ppermute(array, axis, [(i, i ^ bit) for i in range(size)])]
    unnamed x7 -> x5, local copies, waits for them, and re-layouts: 1.43 us -> 0.12 us
    pallas_call x24 -> x25, Pallas kernels: 15.7 us -> 16.2 us  [call(): pl.pallas_call(run, in_specs=[pl.BlockSpec(memory_space=pltpu.VMEM)] * le...]
    ppermute x25 -> x24, waiting for transfers between devices: 47.9 us -> 48.2 us  [swap(): return lax.ppermute(array, axis, [(i, i ^ bit) for i in range(size)])]
  transfers between devices with their start and end apart: 25 -> 24, of which waited for: 14 -> 14; matrix products, arithmetic and copies ran while one was open for 0% -> 0% of each run, Pallas kernels for 10% -> 12%
where the time goes in v5:
time: 95.3 us; the launch traced here: 95.2 us
  waiting for transfers between devices  48.2 us (51%)
  starting transfers between devices  29.5 us (31%)
  Pallas kernels  17.1 us (18%)
    ppermute x24, waiting for transfers between devices, swap(): return lax.ppermute(array, axis, [(i, i ^ bit) for i in range(size)])  48.2 us
    ppermute x24, starting transfers between devices, swap(): return lax.ppermute(array, axis, [(i, i ^ bit) for i in range(size)])  29.5 us
    pallas_call x25, Pallas kernels, call(): pl.pallas_call(run, in_specs=[pl.BlockSpec(memory_space=pltpu.VMEM)] * le...  16.2 us
  transfers between devices with their start and end apart: 24, of which 14 were waited for; matrix products, arithmetic and copies ran while one was open for 0% of the time, Pallas kernels for 12%

profile of v5, /device:TPU:0, one launch (start us, length us, event | category | flops | bytes accessed | tf_op | source)
XLA Modules:
  0.0 95.2 jit_solution(5834227197437970957)
XLA Ops:
  0.0 2.8 %pick.1 = (bf16[8,512,512]{2,1,0:T(8,128)(2,1)S(1)}, bf16[2,2,4,32,512]{4,3,2,1,0:T(8,128)(2,1)S(1)}, bf16[2,2,4,32,512]{4,3,2,1,0:T(8,128)(2,1)S(1)}) custom-call(bf16[512,8192]{1,0:T(8,128)(2,1)} %refs_7_.1, bf16[1,64,8192]{2,1,0:T(8,128)(2,1)} %refs_1_.1, bf16[1,64,8192]{2,1,0:T(8,128)(2,1)} %refs_2_.2), custom_call_target="tpu_custom_call" | custom-call | bytes 65536 | tf_op jit(solution)/shard_map/pick/pallas_call | solution.py:58
  3.3 2.6 %collective-permute-start.2 = (bf16[2,2,4,32,512]{4,3,2,1,0:T(8,128)(2,1)S(1)}, bf16[2,2,4,32,512]{4,3,2,1,0:T(8,128)(2,1)S(1)}, u32[]{:S(2)}, u32[]{:S(2)}) collective-permute-start(bf16[2,2,4,32,512]{4,3,2,1,0:T(8,128)(2,1)S(1)} %get-tuple-element.49), channel_id=1, source_target_pairs={{0,2},{1,3},{2,0},{3,1},{4,6},{5,7},{6,4},{7,5},{8,10},{9,11},{10,... | collective-permute-start | bytes 1572872 | tf_op jit(solution)/shard_map/ppermute | solution.py:543
  5.9 3.4 %attention.1 = (bf16[528,512]{1,0:T(8,128)(2,1)S(1)}, bf16[8,512,512]{2,1,0:T(8,128)(2,1)S(1)}, bf16[512,512]{1,0:T(8,128)(2,1)S(1)}) custom-call(s32[1,128]{1,0:T(1,128)S(1)} %bitcast.6, s32[1,128]{1,0:T(1,128)S(1)} %bitcast.5, bf16[4,128,512]{2,1,0:T(8,128)(2,1)} %refs_2_.3, bf16[12,128,1024]{2,1,0:T(8,128)(2,1)} %bitcast.7, ...), custom_call_target="tpu_custom_call" | custom-call | flops 268435456 | bytes 65536 | tf_op jit(solution)/shard_map/attention/pallas_call | solution.py:58
  9.5 8.9 %collective-permute-done.2.refs_1_ = bf16[2,2,4,32,512]{4,3,2,1,0:T(8,128)(2,1)S(1)} collective-permute-done((bf16[2,2,4,32,512]{4,3,2,1,0:T(8,128)(2,1)S(1)}, bf16[2,2,4,32,512]{4,3,2,1,0:T(8,128)(2,1)S(1)}, u32[]{:S(2)}, u32[]{:S(2)}) %collective-permute-start.2) | collective-permute-done | bytes 524320 | tf_op jit(solution)/shard_map/ppermute | solution.py:543
  19.3 1.2 %far.5.refs_3_ = bf16[4,256,512]{2,1,0:T(8,128)(2,1)S(1)} custom-call(bf16[528,512]{1,0:T(8,128)(2,1)S(1)} %get-tuple-element.45.refs_0_.refs_4_, bf16[512,512]{1,0:T(8,128)(2,1)S(1)} %collective-permute-done.refs_1_, bf16[8,512,512]{2,1,0:T(8,128)(2,1)S(1)} %get-tuple-element.47.refs_2_, bf16[8,512,512]{2,1,0:T(8,128)(2,1)S(1)} %collective-permute-done.1.refs_3_, ...), custom_call_target="tpu_custom_call" | custom-call | flops 1073741824 | bytes 65536 | tf_op jit(solution)/shard_map/far/pallas_call | solution.py:58
  20.5 1.8 %collective-permute-start.9 = (bf16[4,256,512]{2,1,0:T(8,128)(2,1)S(1)}, bf16[4,256,512]{2,1,0:T(8,128)(2,1)S(1)}, u32[]{:S(2)}, u32[]{:S(2)}) collective-permute-start(bf16[4,256,512]{2,1,0:T(8,128)(2,1)S(1)} %far.5.refs_3_), channel_id=1, source_target_pairs={{0,2},{1,3},{2,0},{3,1},{4,6},{5,7},{6,4},{7,5},{8,10},{9,11},{10,... | collective-permute-start | bytes 3145736 | tf_op jit(solution)/shard_map/ppermute | solution.py:543
  22.4 1.5 %collective-permute-start.8 = (bf16[528,512]{1,0:T(8,128)(2,1)S(1)}, bf16[528,512]{1,0:T(8,128)(2,1)S(1)}, u32[]{:S(2)}, u32[]{:S(2)}) collective-permute-start(bf16[528,512]{1,0:T(8,128)(2,1)S(1)} %get-tuple-element.45.refs_0_.refs_4_), channel_id=1, source_target_pairs={{0,16},{16,0},{1,17},{17,1},{2,18},{18,2},{3,19},{19,3},{4,20},{20... | collective-permute-start | bytes 1622024 | tf_op jit(solution)/shard_map/ppermute | solution.py:543
  23.9 1.6 %collective-permute-start.10 = (bf16[4,96,512]{2,1,0:T(8,128)(2,1)S(1)}, bf16[4,96,512]{2,1,0:T(8,128)(2,1)S(1)}, u32[]{:S(2)}, u32[]{:S(2)}) collective-permute-start(bf16[4,96,512]{2,1,0:T(8,128)(2,1)S(1)} %far.4.refs_4_), channel_id=1, source_target_pairs={{0,4},{1,5},{2,6},{3,7},{4,0},{5,1},{6,2},{7,3},{8,12},{9,13},{10,... | collective-permute-start | bytes 1179656 | tf_op jit(solution)/shard_map/ppermute | solution.py:543
  27.9 2.6 %collective-permute-start.6 = (bf16[2,4,32,512]{3,2,1,0:T(8,128)(2,1)S(1)}, bf16[2,4,32,512]{3,2,1,0:T(8,128)(2,1)S(1)}, u32[]{:S(2)}, u32[]{:S(2)}) collective-permute-start(bf16[2,4,32,512]{3,2,1,0:T(8,128)(2,1)S(1)} %get-tuple-element.55), channel_id=1, source_target_pairs={{0,8},{1,9},{2,10},{3,11},{4,12},{5,13},{6,14},{7,15},{8,0},{9,1},... | collective-permute-start | bytes 786440 | tf_op jit(solution)/shard_map/ppermute | solution.py:543
  30.5 5.4 %collective-permute-done.8.refs_5_ = bf16[528,512]{1,0:T(8,128)(2,1)S(1)} collective-permute-done((bf16[528,512]{1,0:T(8,128)(2,1)S(1)}, bf16[528,512]{1,0:T(8,128)(2,1)S(1)}, u32[]{:S(2)}, u32[]{:S(2)}) %collective-permute-start.8) | collective-permute-done | bytes 540704 | tf_op jit(solution)/shard_map/ppermute | solution.py:543
  35.9 3.6 %collective-permute-start.7 = (bf16[2,4,32,512]{3,2,1,0:T(8,128)(2,1)S(1)}, bf16[2,4,32,512]{3,2,1,0:T(8,128)(2,1)S(1)}, u32[]{:S(2)}, u32[]{:S(2)}) collective-permute-start(bf16[2,4,32,512]{3,2,1,0:T(8,128)(2,1)S(1)} %get-tuple-element.56), channel_id=1, source_target_pairs={{0,12},{1,13},{2,14},{3,15},{4,8},{5,9},{6,10},{7,11},{8,4},{9,5},... | collective-permute-start | bytes 786440 | tf_op jit(solution)/shard_map/ppermute | solution.py:543
  40.2 1.3 %collective-permute-done.10.refs_6_.refs_4_ = bf16[4,96,512]{2,1,0:T(8,128)(2,1)S(1)} collective-permute-done((bf16[4,96,512]{2,1,0:T(8,128)(2,1)S(1)}, bf16[4,96,512]{2,1,0:T(8,128)(2,1)S(1)}, u32[]{:S(2)}, u32[]{:S(2)}) %collective-permute-start.10) | collective-permute-done | bytes 393248 | tf_op jit(solution)/shard_map/ppermute | solution.py:543
  42.0 4.6 %collective-permute-done.9.refs_4_ = bf16[4,256,512]{2,1,0:T(8,128)(2,1)S(1)} collective-permute-done((bf16[4,256,512]{2,1,0:T(8,128)(2,1)S(1)}, bf16[4,256,512]{2,1,0:T(8,128)(2,1)S(1)}, u32[]{:S(2)}, u32[]{:S(2)}) %collective-permute-start.9) | collective-permute-done | bytes 1048608 | tf_op jit(solution)/shard_map/ppermute | solution.py:543
  47.9 1.9 %collective-permute-start.14 = (bf16[2,256,512]{2,1,0:T(8,128)(2,1)S(1)}, bf16[2,256,512]{2,1,0:T(8,128)(2,1)S(1)}, u32[]{:S(2)}, u32[]{:S(2)}) collective-permute-start(bf16[2,256,512]{2,1,0:T(8,128)(2,1)S(1)} %get-tuple-element.64), channel_id=1, source_target_pairs={{0,4},{1,5},{2,6},{3,7},{4,0},{5,1},{6,2},{7,3},{8,12},{9,13},{10,... | collective-permute-start | bytes 1572872 | tf_op jit(solution)/shard_map/ppermute | solution.py:543
  49.8 5.0 %collective-permute-done.7.refs_3_ = bf16[2,4,32,512]{3,2,1,0:T(8,128)(2,1)S(1)} collective-permute-done((bf16[2,4,32,512]{3,2,1,0:T(8,128)(2,1)S(1)}, bf16[2,4,32,512]{3,2,1,0:T(8,128)(2,1)S(1)}, u32[]{:S(2)}, u32[]{:S(2)}) %collective-permute-start.7) | collective-permute-done | bytes 262176 | tf_op jit(solution)/shard_map/ppermute | solution.py:543
  54.8 1.5 %shrink.1 = (f32[2,128,128]{2,1,0:T(8,128)S(1)}, bf16[2,128,128]{2,1,0:T(8,128)(2,1)S(1)}) custom-call(bf16[2,4,32,512]{3,2,1,0:T(8,128)(2,1)S(1)} %get-tuple-element.53.refs_4_.refs_0_, bf16[2,4,32,512]{3,2,1,0:T(8,128)(2,1)S(1)} %collective-permute-done.5.refs_1_, bf16[2,4,32,512]{3,2,1,0:T(8,128)(2,1)S(1)} %collective-permute-done.6.refs_2_, ...), custom_call_target="tpu_custom_call" | custom-call | flops 1073741824 | bytes 65536 | tf_op jit(solution)/shard_map/shrink/pallas_call | solution.py:58
  58.1 3.6 %collective-permute-done.12.refs_1_ = bf16[128,128]{1,0:T(8,128)(2,1)S(1)} collective-permute-done((bf16[128,128]{1,0:T(8,128)(2,1)S(1)}, bf16[128,128]{1,0:T(8,128)(2,1)S(1)}, u32[]{:S(2)}, u32[]{:S(2)}) %collective-permute-start.12) | collective-permute-done | bytes 32800 | tf_op jit(solution)/shard_map/ppermute | solution.py:543
  64.5 2.3 %collective-permute-start.19 = (bf16[2,128,512]{2,1,0:T(8,128)(2,1)S(1)}, bf16[2,128,512]{2,1,0:T(8,128)(2,1)S(1)}, u32[]{:S(2)}, u32[]{:S(2)}) collective-permute-start(bf16[2,128,512]{2,1,0:T(8,128)(2,1)S(1)} %get-tuple-element.73), channel_id=1, source_target_pairs={{0,4},{1,5},{2,6},{3,7},{4,0},{5,1},{6,2},{7,3},{8,12},{9,13},{10,... | collective-permute-start | bytes 786440 | tf_op jit(solution)/shard_map/ppermute | solution.py:543
  67.8 1.5 %collective-permute-start.17 = (bf16[2,96,512]{2,1,0:T(8,128)(2,1)S(1)}, bf16[2,96,512]{2,1,0:T(8,128)(2,1)S(1)}, u32[]{:S(2)}, u32[]{:S(2)}) collective-permute-start(bf16[2,96,512]{2,1,0:T(8,128)(2,1)S(1)} %get-tuple-element.71), channel_id=1, source_target_pairs={{0,2},{1,3},{2,0},{3,1},{4,6},{5,7},{6,4},{7,5},{8,10},{9,11},{10,... | collective-permute-start | bytes 589832 | tf_op jit(solution)/shard_map/ppermute | solution.py:543
  70.1 2.0 %collective-permute-start.16 = (bf16[2,64,512]{2,1,0:T(8,128)(2,1)S(1)}, bf16[2,64,512]{2,1,0:T(8,128)(2,1)S(1)}, u32[]{:S(2)}, u32[]{:S(2)}) collective-permute-start(bf16[2,64,512]{2,1,0:T(8,128)(2,1)S(1)} %get-tuple-element.69), channel_id=1, source_target_pairs={{0,4},{1,5},{2,6},{3,7},{4,0},{5,1},{6,2},{7,3},{8,12},{9,13},{10,... | collective-permute-start | bytes 393224 | tf_op jit(solution)/shard_map/ppermute | solution.py:543
  72.2 7.5 %collective-permute-done.19.refs_1_ = bf16[2,128,512]{2,1,0:T(8,128)(2,1)S(1)} collective-permute-done((bf16[2,128,512]{2,1,0:T(8,128)(2,1)S(1)}, bf16[2,128,512]{2,1,0:T(8,128)(2,1)S(1)}, u32[]{:S(2)}, u32[]{:S(2)}) %collective-permute-start.19) | collective-permute-done | bytes 262176 | tf_op jit(solution)/shard_map/ppermute | solution.py:543
  79.9 1.4 %collective-permute-done.16.refs_1_ = bf16[2,64,512]{2,1,0:T(8,128)(2,1)S(1)} collective-permute-done((bf16[2,64,512]{2,1,0:T(8,128)(2,1)S(1)}, bf16[2,64,512]{2,1,0:T(8,128)(2,1)S(1)}, u32[]{:S(2)}, u32[]{:S(2)}) %collective-permute-start.16) | collective-permute-done | bytes 131104 | tf_op jit(solution)/shard_map/ppermute | solution.py:543
  81.4 3.9 %collective-permute-start.20 = (bf16[1,96,512]{2,1,0:T(8,128)(2,1)S(1)}, bf16[1,96,512]{2,1,0:T(8,128)(2,1)S(1)}, u32[]{:S(2)}, u32[]{:S(2)}) collective-permute-start(bf16[1,96,512]{2,1,0:T(8,128)(2,1)S(1)} %get-tuple-element.77), channel_id=1, source_target_pairs={{0,8},{1,9},{2,10},{3,11},{4,12},{5,13},{6,14},{7,15},{8,0},{9,1},... | collective-permute-start | bytes 294920 | tf_op jit(solution)/shard_map/ppermute | solution.py:543
  85.5 6.6 %collective-permute-done.21.refs_1_ = bf16[1,128,512]{2,1,0:T(8,128)(2,1)S(1)} collective-permute-done((bf16[1,128,512]{2,1,0:T(8,128)(2,1)S(1)}, bf16[1,128,512]{2,1,0:T(8,128)(2,1)S(1)}, u32[]{:S(2)}, u32[]{:S(2)}) %collective-permute-start.21) | collective-permute-done | bytes 131104 | tf_op jit(solution)/shard_map/ppermute | solution.py:543
  (55 shorter events, 16.3 us)
Async XLA Ops:
  2.8 15.7 %collective-permute-start.1 = (bf16[8,512,512]{2,1,0:T(8,128)(2,1)S(1)}, bf16[8,512,512]{2,1,0:T(8,128)(2,1)S(1)}, u32[]{:S(2)}, u32[]{:S(2)}) collective-permute-start(bf16[8,512,512]{2,1,0:T(8,128)(2,1)S(1)} %get-tuple-element.48), channel_id=1, source_target_pairs={{0,1},{1,0},{2,3},{3,2},{4,5},{5,4},{6,7},{7,6},{8,9},{9,8},{10,11... | collective-permute-start | bytes 12582920 | tf_op jit(solution)/shard_map/ppermute | solution.py:543
  3.3 15.1 %collective-permute-start.2 = (bf16[2,2,4,32,512]{4,3,2,1,0:T(8,128)(2,1)S(1)}, bf16[2,2,4,32,512]{4,3,2,1,0:T(8,128)(2,1)S(1)}, u32[]{:S(2)}, u32[]{:S(2)}) collective-permute-start(bf16[2,2,4,32,512]{4,3,2,1,0:T(8,128)(2,1)S(1)} %get-tuple-element.49), channel_id=1, source_target_pairs={{0,2},{1,3},{2,0},{3,1},{4,6},{5,7},{6,4},{7,5},{8,10},{9,11},{10,... | collective-permute-start | bytes 1572872 | tf_op jit(solution)/shard_map/ppermute | solution.py:543
  9.3 9.2 %collective-permute-start = (bf16[512,512]{1,0:T(8,128)(2,1)S(1)}, bf16[512,512]{1,0:T(8,128)(2,1)S(1)}, u32[]{:S(2)}, u32[]{:S(2)}) collective-permute-start(bf16[512,512]{1,0:T(8,128)(2,1)S(1)} %get-tuple-element.46.refs_2_), channel_id=1, source_target_pairs={{0,1},{1,0},{2,3},{3,2},{4,5},{5,4},{6,7},{7,6},{8,9},{9,8},{10,11... | collective-permute-start | bytes 1572872 | tf_op jit(solution)/shard_map/ppermute | solution.py:543
  20.5 26.1 %collective-permute-start.9 = (bf16[4,256,512]{2,1,0:T(8,128)(2,1)S(1)}, bf16[4,256,512]{2,1,0:T(8,128)(2,1)S(1)}, u32[]{:S(2)}, u32[]{:S(2)}) collective-permute-start(bf16[4,256,512]{2,1,0:T(8,128)(2,1)S(1)} %far.5.refs_3_), channel_id=1, source_target_pairs={{0,2},{1,3},{2,0},{3,1},{4,6},{5,7},{6,4},{7,5},{8,10},{9,11},{10,... | collective-permute-start | bytes 3145736 | tf_op jit(solution)/shard_map/ppermute | solution.py:543
  22.4 13.6 %collective-permute-start.8 = (bf16[528,512]{1,0:T(8,128)(2,1)S(1)}, bf16[528,512]{1,0:T(8,128)(2,1)S(1)}, u32[]{:S(2)}, u32[]{:S(2)}) collective-permute-start(bf16[528,512]{1,0:T(8,128)(2,1)S(1)} %get-tuple-element.45.refs_0_.refs_4_), channel_id=1, source_target_pairs={{0,16},{16,0},{1,17},{17,1},{2,18},{18,2},{3,19},{19,3},{4,20},{20... | collective-permute-start | bytes 1622024 | tf_op jit(solution)/shard_map/ppermute | solution.py:543
  23.9 17.7 %collective-permute-start.10 = (bf16[4,96,512]{2,1,0:T(8,128)(2,1)S(1)}, bf16[4,96,512]{2,1,0:T(8,128)(2,1)S(1)}, u32[]{:S(2)}, u32[]{:S(2)}) collective-permute-start(bf16[4,96,512]{2,1,0:T(8,128)(2,1)S(1)} %far.4.refs_4_), channel_id=1, source_target_pairs={{0,4},{1,5},{2,6},{3,7},{4,0},{5,1},{6,2},{7,3},{8,12},{9,13},{10,... | collective-permute-start | bytes 1179656 | tf_op jit(solution)/shard_map/ppermute | solution.py:543
  25.4 1.5 %collective-permute-start.3 = (bf16[2,4,32,512]{3,2,1,0:T(8,128)(2,1)S(1)}, bf16[2,4,32,512]{3,2,1,0:T(8,128)(2,1)S(1)}, u32[]{:S(2)}, u32[]{:S(2)}) collective-permute-start(bf16[2,4,32,512]{3,2,1,0:T(8,128)(2,1)S(1)} %get-tuple-element.51.refs_4_), channel_id=1, source_target_pairs={{0,1},{1,0},{2,3},{3,2},{4,5},{5,4},{6,7},{7,6},{8,9},{9,8},{10,11... | collective-permute-start | bytes 786440 | tf_op jit(solution)/shard_map/ppermute | solution.py:543
  25.4 1.9 %collective-permute-start.4 = (bf16[2,4,32,512]{3,2,1,0:T(8,128)(2,1)S(1)}, bf16[2,4,32,512]{3,2,1,0:T(8,128)(2,1)S(1)}, u32[]{:S(2)}, u32[]{:S(2)}) collective-permute-start(bf16[2,4,32,512]{3,2,1,0:T(8,128)(2,1)S(1)} %get-tuple-element.52), channel_id=1, source_target_pairs={{0,1},{1,0},{2,3},{3,2},{4,5},{5,4},{6,7},{7,6},{8,9},{9,8},{10,11... | collective-permute-start | bytes 786440 | tf_op jit(solution)/shard_map/ppermute | solution.py:543
  27.4 22.4 %collective-permute-start.5 = (bf16[2,4,32,512]{3,2,1,0:T(8,128)(2,1)S(1)}, bf16[2,4,32,512]{3,2,1,0:T(8,128)(2,1)S(1)}, u32[]{:S(2)}, u32[]{:S(2)}) collective-permute-start(bf16[2,4,32,512]{3,2,1,0:T(8,128)(2,1)S(1)} %get-tuple-element.54), channel_id=1, source_target_pairs={{0,4},{1,5},{2,6},{3,7},{4,0},{5,1},{6,2},{7,3},{8,12},{9,13},{10,... | collective-permute-start | bytes 786440 | tf_op jit(solution)/shard_map/ppermute | solution.py:543
  27.9 21.9 %collective-permute-start.6 = (bf16[2,4,32,512]{3,2,1,0:T(8,128)(2,1)S(1)}, bf16[2,4,32,512]{3,2,1,0:T(8,128)(2,1)S(1)}, u32[]{:S(2)}, u32[]{:S(2)}) collective-permute-start(bf16[2,4,32,512]{3,2,1,0:T(8,128)(2,1)S(1)} %get-tuple-element.55), channel_id=1, source_target_pairs={{0,8},{1,9},{2,10},{3,11},{4,12},{5,13},{6,14},{7,15},{8,0},{9,1},... | collective-permute-start | bytes 786440 | tf_op jit(solution)/shard_map/ppermute | solution.py:543
  35.9 18.9 %collective-permute-start.7 = (bf16[2,4,32,512]{3,2,1,0:T(8,128)(2,1)S(1)}, bf16[2,4,32,512]{3,2,1,0:T(8,128)(2,1)S(1)}, u32[]{:S(2)}, u32[]{:S(2)}) collective-permute-start(bf16[2,4,32,512]{3,2,1,0:T(8,128)(2,1)S(1)} %get-tuple-element.56), channel_id=1, source_target_pairs={{0,12},{1,13},{2,14},{3,15},{4,8},{5,9},{6,10},{7,11},{8,4},{9,5},... | collective-permute-start | bytes 786440 | tf_op jit(solution)/shard_map/ppermute | solution.py:543
  41.5 22.2 %collective-permute-start.15 = (bf16[4,128,512]{2,1,0:T(8,128)(2,1)S(1)}, bf16[4,128,512]{2,1,0:T(8,128)(2,1)S(1)}, u32[]{:S(2)}, u32[]{:S(2)}) collective-permute-start(bf16[4,128,512]{2,1,0:T(8,128)(2,1)S(1)} %far.6.refs_5_), channel_id=1, source_target_pairs={{0,2},{1,3},{2,0},{3,1},{4,6},{5,7},{6,4},{7,5},{8,10},{9,11},{10,... | collective-permute-start | bytes 1572872 | tf_op jit(solution)/shard_map/ppermute | solution.py:543
  47.9 18.9 %collective-permute-start.14 = (bf16[2,256,512]{2,1,0:T(8,128)(2,1)S(1)}, bf16[2,256,512]{2,1,0:T(8,128)(2,1)S(1)}, u32[]{:S(2)}, u32[]{:S(2)}) collective-permute-start(bf16[2,256,512]{2,1,0:T(8,128)(2,1)S(1)} %get-tuple-element.64), channel_id=1, source_target_pairs={{0,4},{1,5},{2,6},{3,7},{4,0},{5,1},{6,2},{7,3},{8,12},{9,13},{10,... | collective-permute-start | bytes 1572872 | tf_op jit(solution)/shard_map/ppermute | solution.py:543
  56.4 1.3 %collective-permute-start.11 = (bf16[2,128,128]{2,1,0:T(8,128)(2,1)S(1)}, bf16[2,128,128]{2,1,0:T(8,128)(2,1)S(1)}, u32[]{:S(2)}, u32[]{:S(2)}) collective-permute-start(bf16[2,128,128]{2,1,0:T(8,128)(2,1)S(1)} %get-tuple-element.59), channel_id=1, source_target_pairs={{0,1},{1,0},{2,3},{3,2},{4,5},{5,4},{6,7},{7,6},{8,9},{9,8},{10,11... | collective-permute-start | bytes 196616 | tf_op jit(solution)/shard_map/ppermute | solution.py:543
  57.7 4.0 %collective-permute-start.12 = (bf16[128,128]{1,0:T(8,128)(2,1)S(1)}, bf16[128,128]{1,0:T(8,128)(2,1)S(1)}, u32[]{:S(2)}, u32[]{:S(2)}) collective-permute-start(bf16[128,128]{1,0:T(8,128)(2,1)S(1)} %get-tuple-element.61.refs_2_), channel_id=1, source_target_pairs={{0,16},{16,0},{1,17},{17,1},{2,18},{18,2},{3,19},{19,3},{4,20},{20... | collective-permute-start | bytes 98312 | tf_op jit(solution)/shard_map/ppermute | solution.py:543
  61.7 31.5 %collective-permute-start.22 = (bf16[16,32,512]{2,1,0:T(8,128)(2,1)S(1)}, bf16[16,32,512]{2,1,0:T(8,128)(2,1)S(1)}, u32[]{:S(2)}, u32[]{:S(2)}) collective-permute-start(bf16[16,32,512]{2,1,0:T(8,128)(2,1)S(1)} %expanding.1.refs_5_.refs_3_), channel_id=1, source_target_pairs={{0,16},{16,0},{1,17},{17,1},{2,18},{18,2},{3,19},{19,3},{4,20},{20... | collective-permute-start | bytes 1572872 | tf_op jit(solution)/shard_map/ppermute | solution.py:543
  62.9 6.4 %collective-permute-start.13 = (bf16[4,48,512]{2,1,0:T(8,128)(2,1)S(1)}, bf16[4,48,512]{2,1,0:T(8,128)(2,1)S(1)}, u32[]{:S(2)}, u32[]{:S(2)}) collective-permute-start(bf16[4,48,512]{2,1,0:T(8,128)(2,1)S(1)} %far.7.refs_5_), channel_id=1, source_target_pairs={{0,2},{1,3},{2,0},{3,1},{4,6},{5,7},{6,4},{7,5},{8,10},{9,11},{10,... | collective-permute-start | bytes 589832 | tf_op jit(solution)/shard_map/ppermute | solution.py:543
  64.5 15.2 %collective-permute-start.19 = (bf16[2,128,512]{2,1,0:T(8,128)(2,1)S(1)}, bf16[2,128,512]{2,1,0:T(8,128)(2,1)S(1)}, u32[]{:S(2)}, u32[]{:S(2)}) collective-permute-start(bf16[2,128,512]{2,1,0:T(8,128)(2,1)S(1)} %get-tuple-element.73), channel_id=1, source_target_pairs={{0,4},{1,5},{2,6},{3,7},{4,0},{5,1},{6,2},{7,3},{8,12},{9,13},{10,... | collective-permute-start | bytes 786440 | tf_op jit(solution)/shard_map/ppermute | solution.py:543
  66.9 12.9 %collective-permute-start.18 = (bf16[1,256,512]{2,1,0:T(8,128)(2,1)S(1)}, bf16[1,256,512]{2,1,0:T(8,128)(2,1)S(1)}, u32[]{:S(2)}, u32[]{:S(2)}) collective-permute-start(bf16[1,256,512]{2,1,0:T(8,128)(2,1)S(1)} %get-tuple-element.72), channel_id=1, source_target_pairs={{0,8},{1,9},{2,10},{3,11},{4,12},{5,13},{6,14},{7,15},{8,0},{9,1},... | collective-permute-start | bytes 786440 | tf_op jit(solution)/shard_map/ppermute | solution.py:543
  67.8 12.0 %collective-permute-start.17 = (bf16[2,96,512]{2,1,0:T(8,128)(2,1)S(1)}, bf16[2,96,512]{2,1,0:T(8,128)(2,1)S(1)}, u32[]{:S(2)}, u32[]{:S(2)}) collective-permute-start(bf16[2,96,512]{2,1,0:T(8,128)(2,1)S(1)} %get-tuple-element.71), channel_id=1, source_target_pairs={{0,2},{1,3},{2,0},{3,1},{4,6},{5,7},{6,4},{7,5},{8,10},{9,11},{10,... | collective-permute-start | bytes 589832 | tf_op jit(solution)/shard_map/ppermute | solution.py:543
  70.1 11.2 %collective-permute-start.16 = (bf16[2,64,512]{2,1,0:T(8,128)(2,1)S(1)}, bf16[2,64,512]{2,1,0:T(8,128)(2,1)S(1)}, u32[]{:S(2)}, u32[]{:S(2)}) collective-permute-start(bf16[2,64,512]{2,1,0:T(8,128)(2,1)S(1)} %get-tuple-element.69), channel_id=1, source_target_pairs={{0,4},{1,5},{2,6},{3,7},{4,0},{5,1},{6,2},{7,3},{8,12},{9,13},{10,... | collective-permute-start | bytes 393224 | tf_op jit(solution)/shard_map/ppermute | solution.py:543
  79.7 12.4 %collective-permute-start.21 = (bf16[1,128,512]{2,1,0:T(8,128)(2,1)S(1)}, bf16[1,128,512]{2,1,0:T(8,128)(2,1)S(1)}, u32[]{:S(2)}, u32[]{:S(2)}) collective-permute-start(bf16[1,128,512]{2,1,0:T(8,128)(2,1)S(1)} %get-tuple-element.78), channel_id=1, source_target_pairs={{0,8},{1,9},{2,10},{3,11},{4,12},{5,13},{6,14},{7,15},{8,0},{9,1},... | collective-permute-start | bytes 393224 | tf_op jit(solution)/shard_map/ppermute | solution.py:543
  81.4 11.8 %collective-permute-start.20 = (bf16[1,96,512]{2,1,0:T(8,128)(2,1)S(1)}, bf16[1,96,512]{2,1,0:T(8,128)(2,1)S(1)}, u32[]{:S(2)}, u32[]{:S(2)}) collective-permute-start(bf16[1,96,512]{2,1,0:T(8,128)(2,1)S(1)} %get-tuple-element.77), channel_id=1, source_target_pairs={{0,8},{1,9},{2,10},{3,11},{4,12},{5,13},{6,14},{7,15},{8,0},{9,1},... | collective-permute-start | bytes 294920 | tf_op jit(solution)/shard_map/ppermute | solution.py:543
  85.3 8.9 %collective-permute-start.23 = (bf16[1,96,512]{2,1,0:T(8,128)(2,1)S(1)}, bf16[1,96,512]{2,1,0:T(8,128)(2,1)S(1)}, u32[]{:S(2)}, u32[]{:S(2)}) collective-permute-start(bf16[1,96,512]{2,1,0:T(8,128)(2,1)S(1)} %get-tuple-element.82), channel_id=1, source_target_pairs={{0,8},{1,9},{2,10},{3,11},{4,12},{5,13},{6,14},{7,15},{8,0},{9,1},... | collective-permute-start | bytes 294920 | tf_op jit(solution)/shard_map/ppermute | solution.py:543
  (2 other events, 11.8 us)

commit v6 on v5

--- a/solution.py
+++ b/solution.py
@@ -30,9 +30,9 @@
     "cross",
     "expanding",
     "far2",
-    "near3",
     "near1",
     "end0",
+    "near3",
     "near2",
     "end1",
     "fold0",

time: 95.3 us -> 94.5 us (level)
  no operation moved by 1% of the time
where the time goes in v6:
time: 94.5 us; the launch traced here: 94.3 us
  waiting for transfers between devices  47.4 us (50%)
  starting transfers between devices  29.6 us (31%)
  Pallas kernels  17.1 us (18%)
    ppermute x24, waiting for transfers between devices, swap(): return lax.ppermute(array, axis, [(i, i ^ bit) for i in range(size)])  47.4 us
    ppermute x24, starting transfers between devices, swap(): return lax.ppermute(array, axis, [(i, i ^ bit) for i in range(size)])  29.6 us
    pallas_call x25, Pallas kernels, call(): pl.pallas_call(run, in_specs=[pl.BlockSpec(memory_space=pltpu.VMEM)] * le...  16.2 us
  transfers between devices with their start and end apart: 24, of which 14 were waited for; matrix products, arithmetic and copies ran while one was open for 0% of the time, Pallas kernels for 12%

profile of v6, /device:TPU:0, one launch (start us, length us, event | category | flops | bytes accessed | tf_op | source)
XLA Modules:
  0.0 94.3 jit_solution(2851992638935434045)
XLA Ops:
  0.0 2.8 %pick.1 = (bf16[8,512,512]{2,1,0:T(8,128)(2,1)S(1)}, bf16[2,2,4,32,512]{4,3,2,1,0:T(8,128)(2,1)S(1)}, bf16[2,2,4,32,512]{4,3,2,1,0:T(8,128)(2,1)S(1)}) custom-call(bf16[512,8192]{1,0:T(8,128)(2,1)} %refs_7_.1, bf16[1,64,8192]{2,1,0:T(8,128)(2,1)} %refs_1_.1, bf16[1,64,8192]{2,1,0:T(8,128)(2,1)} %refs_2_.2), custom_call_target="tpu_custom_call" | custom-call | bytes 65536 | tf_op jit(solution)/shard_map/pick/pallas_call | solution.py:58
  3.3 2.6 %collective-permute-start.2 = (bf16[2,2,4,32,512]{4,3,2,1,0:T(8,128)(2,1)S(1)}, bf16[2,2,4,32,512]{4,3,2,1,0:T(8,128)(2,1)S(1)}, u32[]{:S(2)}, u32[]{:S(2)}) collective-permute-start(bf16[2,2,4,32,512]{4,3,2,1,0:T(8,128)(2,1)S(1)} %get-tuple-element.49), channel_id=1, source_target_pairs={{0,2},{1,3},{2,0},{3,1},{4,6},{5,7},{6,4},{7,5},{8,10},{9,11},{10,... | collective-permute-start | bytes 1572872 | tf_op jit(solution)/shard_map/ppermute | solution.py:543
  5.9 3.4 %attention.1 = (bf16[528,512]{1,0:T(8,128)(2,1)S(1)}, bf16[8,512,512]{2,1,0:T(8,128)(2,1)S(1)}, bf16[512,512]{1,0:T(8,128)(2,1)S(1)}) custom-call(s32[1,128]{1,0:T(1,128)S(1)} %bitcast.6, s32[1,128]{1,0:T(1,128)S(1)} %bitcast.5, bf16[4,128,512]{2,1,0:T(8,128)(2,1)} %refs_2_.3, bf16[12,128,1024]{2,1,0:T(8,128)(2,1)} %bitcast.7, ...), custom_call_target="tpu_custom_call" | custom-call | flops 268435456 | bytes 65536 | tf_op jit(solution)/shard_map/attention/pallas_call | solution.py:58
  9.5 8.9 %collective-permute-done.2.refs_1_ = bf16[2,2,4,32,512]{4,3,2,1,0:T(8,128)(2,1)S(1)} collective-permute-done((bf16[2,2,4,32,512]{4,3,2,1,0:T(8,128)(2,1)S(1)}, bf16[2,2,4,32,512]{4,3,2,1,0:T(8,128)(2,1)S(1)}, u32[]{:S(2)}, u32[]{:S(2)}) %collective-permute-start.2) | collective-permute-done | bytes 524320 | tf_op jit(solution)/shard_map/ppermute | solution.py:543
  19.3 1.2 %far.5.refs_3_ = bf16[4,256,512]{2,1,0:T(8,128)(2,1)S(1)} custom-call(bf16[528,512]{1,0:T(8,128)(2,1)S(1)} %get-tuple-element.45.refs_0_.refs_4_, bf16[512,512]{1,0:T(8,128)(2,1)S(1)} %collective-permute-done.refs_1_, bf16[8,512,512]{2,1,0:T(8,128)(2,1)S(1)} %get-tuple-element.47.refs_2_, bf16[8,512,512]{2,1,0:T(8,128)(2,1)S(1)} %collective-permute-done.1.refs_3_, ...), custom_call_target="tpu_custom_call" | custom-call | flops 1073741824 | bytes 65536 | tf_op jit(solution)/shard_map/far/pallas_call | solution.py:58
  20.5 1.8 %collective-permute-start.9 = (bf16[4,256,512]{2,1,0:T(8,128)(2,1)S(1)}, bf16[4,256,512]{2,1,0:T(8,128)(2,1)S(1)}, u32[]{:S(2)}, u32[]{:S(2)}) collective-permute-start(bf16[4,256,512]{2,1,0:T(8,128)(2,1)S(1)} %far.5.refs_3_), channel_id=1, source_target_pairs={{0,2},{1,3},{2,0},{3,1},{4,6},{5,7},{6,4},{7,5},{8,10},{9,11},{10,... | collective-permute-start | bytes 3145736 | tf_op jit(solution)/shard_map/ppermute | solution.py:543
  22.4 1.5 %collective-permute-start.8 = (bf16[528,512]{1,0:T(8,128)(2,1)S(1)}, bf16[528,512]{1,0:T(8,128)(2,1)S(1)}, u32[]{:S(2)}, u32[]{:S(2)}) collective-permute-start(bf16[528,512]{1,0:T(8,128)(2,1)S(1)} %get-tuple-element.45.refs_0_.refs_4_), channel_id=1, source_target_pairs={{0,16},{16,0},{1,17},{17,1},{2,18},{18,2},{3,19},{19,3},{4,20},{20... | collective-permute-start | bytes 1622024 | tf_op jit(solution)/shard_map/ppermute | solution.py:543
  23.9 1.6 %collective-permute-start.10 = (bf16[4,96,512]{2,1,0:T(8,128)(2,1)S(1)}, bf16[4,96,512]{2,1,0:T(8,128)(2,1)S(1)}, u32[]{:S(2)}, u32[]{:S(2)}) collective-permute-start(bf16[4,96,512]{2,1,0:T(8,128)(2,1)S(1)} %far.4.refs_4_), channel_id=1, source_target_pairs={{0,4},{1,5},{2,6},{3,7},{4,0},{5,1},{6,2},{7,3},{8,12},{9,13},{10,... | collective-permute-start | bytes 1179656 | tf_op jit(solution)/shard_map/ppermute | solution.py:543
  27.9 2.6 %collective-permute-start.6 = (bf16[2,4,32,512]{3,2,1,0:T(8,128)(2,1)S(1)}, bf16[2,4,32,512]{3,2,1,0:T(8,128)(2,1)S(1)}, u32[]{:S(2)}, u32[]{:S(2)}) collective-permute-start(bf16[2,4,32,512]{3,2,1,0:T(8,128)(2,1)S(1)} %get-tuple-element.55), channel_id=1, source_target_pairs={{0,8},{1,9},{2,10},{3,11},{4,12},{5,13},{6,14},{7,15},{8,0},{9,1},... | collective-permute-start | bytes 786440 | tf_op jit(solution)/shard_map/ppermute | solution.py:543
  30.5 5.4 %collective-permute-done.8.refs_5_ = bf16[528,512]{1,0:T(8,128)(2,1)S(1)} collective-permute-done((bf16[528,512]{1,0:T(8,128)(2,1)S(1)}, bf16[528,512]{1,0:T(8,128)(2,1)S(1)}, u32[]{:S(2)}, u32[]{:S(2)}) %collective-permute-start.8) | collective-permute-done | bytes 540704 | tf_op jit(solution)/shard_map/ppermute | solution.py:543
  35.9 3.6 %collective-permute-start.7 = (bf16[2,4,32,512]{3,2,1,0:T(8,128)(2,1)S(1)}, bf16[2,4,32,512]{3,2,1,0:T(8,128)(2,1)S(1)}, u32[]{:S(2)}, u32[]{:S(2)}) collective-permute-start(bf16[2,4,32,512]{3,2,1,0:T(8,128)(2,1)S(1)} %get-tuple-element.56), channel_id=1, source_target_pairs={{0,12},{1,13},{2,14},{3,15},{4,8},{5,9},{6,10},{7,11},{8,4},{9,5},... | collective-permute-start | bytes 786440 | tf_op jit(solution)/shard_map/ppermute | solution.py:543
  40.2 1.3 %collective-permute-done.10.refs_6_.refs_4_ = bf16[4,96,512]{2,1,0:T(8,128)(2,1)S(1)} collective-permute-done((bf16[4,96,512]{2,1,0:T(8,128)(2,1)S(1)}, bf16[4,96,512]{2,1,0:T(8,128)(2,1)S(1)}, u32[]{:S(2)}, u32[]{:S(2)}) %collective-permute-start.10) | collective-permute-done | bytes 393248 | tf_op jit(solution)/shard_map/ppermute | solution.py:543
  42.0 4.6 %collective-permute-done.9.refs_4_ = bf16[4,256,512]{2,1,0:T(8,128)(2,1)S(1)} collective-permute-done((bf16[4,256,512]{2,1,0:T(8,128)(2,1)S(1)}, bf16[4,256,512]{2,1,0:T(8,128)(2,1)S(1)}, u32[]{:S(2)}, u32[]{:S(2)}) %collective-permute-start.9) | collective-permute-done | bytes 1048608 | tf_op jit(solution)/shard_map/ppermute | solution.py:543
  47.9 1.9 %collective-permute-start.14 = (bf16[2,256,512]{2,1,0:T(8,128)(2,1)S(1)}, bf16[2,256,512]{2,1,0:T(8,128)(2,1)S(1)}, u32[]{:S(2)}, u32[]{:S(2)}) collective-permute-start(bf16[2,256,512]{2,1,0:T(8,128)(2,1)S(1)} %get-tuple-element.64), channel_id=1, source_target_pairs={{0,4},{1,5},{2,6},{3,7},{4,0},{5,1},{6,2},{7,3},{8,12},{9,13},{10,... | collective-permute-start | bytes 1572872 | tf_op jit(solution)/shard_map/ppermute | solution.py:543
  49.8 5.0 %collective-permute-done.7.refs_3_ = bf16[2,4,32,512]{3,2,1,0:T(8,128)(2,1)S(1)} collective-permute-done((bf16[2,4,32,512]{3,2,1,0:T(8,128)(2,1)S(1)}, bf16[2,4,32,512]{3,2,1,0:T(8,128)(2,1)S(1)}, u32[]{:S(2)}, u32[]{:S(2)}) %collective-permute-start.7) | collective-permute-done | bytes 262176 | tf_op jit(solution)/shard_map/ppermute | solution.py:543
  54.8 1.5 %shrink.1 = (f32[2,128,128]{2,1,0:T(8,128)S(1)}, bf16[2,128,128]{2,1,0:T(8,128)(2,1)S(1)}) custom-call(bf16[2,4,32,512]{3,2,1,0:T(8,128)(2,1)S(1)} %get-tuple-element.53.refs_4_.refs_0_, bf16[2,4,32,512]{3,2,1,0:T(8,128)(2,1)S(1)} %collective-permute-done.5.refs_1_, bf16[2,4,32,512]{3,2,1,0:T(8,128)(2,1)S(1)} %collective-permute-done.6.refs_2_, ...), custom_call_target="tpu_custom_call" | custom-call | flops 1073741824 | bytes 65536 | tf_op jit(solution)/shard_map/shrink/pallas_call | solution.py:58
  58.1 3.6 %collective-permute-done.12.refs_1_ = bf16[128,128]{1,0:T(8,128)(2,1)S(1)} collective-permute-done((bf16[128,128]{1,0:T(8,128)(2,1)S(1)}, bf16[128,128]{1,0:T(8,128)(2,1)S(1)}, u32[]{:S(2)}, u32[]{:S(2)}) %collective-permute-start.12) | collective-permute-done | bytes 32800 | tf_op jit(solution)/shard_map/ppermute | solution.py:543
  63.7 2.3 %collective-permute-start.19 = (bf16[2,128,512]{2,1,0:T(8,128)(2,1)S(1)}, bf16[2,128,512]{2,1,0:T(8,128)(2,1)S(1)}, u32[]{:S(2)}, u32[]{:S(2)}) collective-permute-start(bf16[2,128,512]{2,1,0:T(8,128)(2,1)S(1)} %get-tuple-element.73), channel_id=1, source_target_pairs={{0,4},{1,5},{2,6},{3,7},{4,0},{5,1},{6,2},{7,3},{8,12},{9,13},{10,... | collective-permute-start | bytes 786440 | tf_op jit(solution)/shard_map/ppermute | solution.py:543
  67.8 1.6 %collective-permute-start.17 = (bf16[2,96,512]{2,1,0:T(8,128)(2,1)S(1)}, bf16[2,96,512]{2,1,0:T(8,128)(2,1)S(1)}, u32[]{:S(2)}, u32[]{:S(2)}) collective-permute-start(bf16[2,96,512]{2,1,0:T(8,128)(2,1)S(1)} %get-tuple-element.71), channel_id=1, source_target_pairs={{0,2},{1,3},{2,0},{3,1},{4,6},{5,7},{6,4},{7,5},{8,10},{9,11},{10,... | collective-permute-start | bytes 589832 | tf_op jit(solution)/shard_map/ppermute | solution.py:543
  70.2 2.0 %collective-permute-start.16 = (bf16[2,64,512]{2,1,0:T(8,128)(2,1)S(1)}, bf16[2,64,512]{2,1,0:T(8,128)(2,1)S(1)}, u32[]{:S(2)}, u32[]{:S(2)}) collective-permute-start(bf16[2,64,512]{2,1,0:T(8,128)(2,1)S(1)} %get-tuple-element.69), channel_id=1, source_target_pairs={{0,4},{1,5},{2,6},{3,7},{4,0},{5,1},{6,2},{7,3},{8,12},{9,13},{10,... | collective-permute-start | bytes 393224 | tf_op jit(solution)/shard_map/ppermute | solution.py:543
  72.2 6.6 %collective-permute-done.19.refs_1_ = bf16[2,128,512]{2,1,0:T(8,128)(2,1)S(1)} collective-permute-done((bf16[2,128,512]{2,1,0:T(8,128)(2,1)S(1)}, bf16[2,128,512]{2,1,0:T(8,128)(2,1)S(1)}, u32[]{:S(2)}, u32[]{:S(2)}) %collective-permute-start.19) | collective-permute-done | bytes 262176 | tf_op jit(solution)/shard_map/ppermute | solution.py:543
  79.1 1.4 %collective-permute-done.16.refs_1_ = bf16[2,64,512]{2,1,0:T(8,128)(2,1)S(1)} collective-permute-done((bf16[2,64,512]{2,1,0:T(8,128)(2,1)S(1)}, bf16[2,64,512]{2,1,0:T(8,128)(2,1)S(1)}, u32[]{:S(2)}, u32[]{:S(2)}) %collective-permute-start.16) | collective-permute-done | bytes 131104 | tf_op jit(solution)/shard_map/ppermute | solution.py:543
  80.6 3.9 %collective-permute-start.20 = (bf16[1,96,512]{2,1,0:T(8,128)(2,1)S(1)}, bf16[1,96,512]{2,1,0:T(8,128)(2,1)S(1)}, u32[]{:S(2)}, u32[]{:S(2)}) collective-permute-start(bf16[1,96,512]{2,1,0:T(8,128)(2,1)S(1)} %get-tuple-element.77), channel_id=1, source_target_pairs={{0,8},{1,9},{2,10},{3,11},{4,12},{5,13},{6,14},{7,15},{8,0},{9,1},... | collective-permute-start | bytes 294920 | tf_op jit(solution)/shard_map/ppermute | solution.py:543
  84.7 6.6 %collective-permute-done.21.refs_1_ = bf16[1,128,512]{2,1,0:T(8,128)(2,1)S(1)} collective-permute-done((bf16[1,128,512]{2,1,0:T(8,128)(2,1)S(1)}, bf16[1,128,512]{2,1,0:T(8,128)(2,1)S(1)}, u32[]{:S(2)}, u32[]{:S(2)}) %collective-permute-start.21) | collective-permute-done | bytes 131104 | tf_op jit(solution)/shard_map/ppermute | solution.py:543
  (55 shorter events, 16.3 us)
Async XLA Ops:
  2.8 15.7 %collective-permute-start.1 = (bf16[8,512,512]{2,1,0:T(8,128)(2,1)S(1)}, bf16[8,512,512]{2,1,0:T(8,128)(2,1)S(1)}, u32[]{:S(2)}, u32[]{:S(2)}) collective-permute-start(bf16[8,512,512]{2,1,0:T(8,128)(2,1)S(1)} %get-tuple-element.48), channel_id=1, source_target_pairs={{0,1},{1,0},{2,3},{3,2},{4,5},{5,4},{6,7},{7,6},{8,9},{9,8},{10,11... | collective-permute-start | bytes 12582920 | tf_op jit(solution)/shard_map/ppermute | solution.py:543
  3.3 15.1 %collective-permute-start.2 = (bf16[2,2,4,32,512]{4,3,2,1,0:T(8,128)(2,1)S(1)}, bf16[2,2,4,32,512]{4,3,2,1,0:T(8,128)(2,1)S(1)}, u32[]{:S(2)}, u32[]{:S(2)}) collective-permute-start(bf16[2,2,4,32,512]{4,3,2,1,0:T(8,128)(2,1)S(1)} %get-tuple-element.49), channel_id=1, source_target_pairs={{0,2},{1,3},{2,0},{3,1},{4,6},{5,7},{6,4},{7,5},{8,10},{9,11},{10,... | collective-permute-start | bytes 1572872 | tf_op jit(solution)/shard_map/ppermute | solution.py:543
  9.3 9.2 %collective-permute-start = (bf16[512,512]{1,0:T(8,128)(2,1)S(1)}, bf16[512,512]{1,0:T(8,128)(2,1)S(1)}, u32[]{:S(2)}, u32[]{:S(2)}) collective-permute-start(bf16[512,512]{1,0:T(8,128)(2,1)S(1)} %get-tuple-element.46.refs_2_), channel_id=1, source_target_pairs={{0,1},{1,0},{2,3},{3,2},{4,5},{5,4},{6,7},{7,6},{8,9},{9,8},{10,11... | collective-permute-start | bytes 1572872 | tf_op jit(solution)/shard_map/ppermute | solution.py:543
  20.5 26.1 %collective-permute-start.9 = (bf16[4,256,512]{2,1,0:T(8,128)(2,1)S(1)}, bf16[4,256,512]{2,1,0:T(8,128)(2,1)S(1)}, u32[]{:S(2)}, u32[]{:S(2)}) collective-permute-start(bf16[4,256,512]{2,1,0:T(8,128)(2,1)S(1)} %far.5.refs_3_), channel_id=1, source_target_pairs={{0,2},{1,3},{2,0},{3,1},{4,6},{5,7},{6,4},{7,5},{8,10},{9,11},{10,... | collective-permute-start | bytes 3145736 | tf_op jit(solution)/shard_map/ppermute | solution.py:543
  22.4 13.6 %collective-permute-start.8 = (bf16[528,512]{1,0:T(8,128)(2,1)S(1)}, bf16[528,512]{1,0:T(8,128)(2,1)S(1)}, u32[]{:S(2)}, u32[]{:S(2)}) collective-permute-start(bf16[528,512]{1,0:T(8,128)(2,1)S(1)} %get-tuple-element.45.refs_0_.refs_4_), channel_id=1, source_target_pairs={{0,16},{16,0},{1,17},{17,1},{2,18},{18,2},{3,19},{19,3},{4,20},{20... | collective-permute-start | bytes 1622024 | tf_op jit(solution)/shard_map/ppermute | solution.py:543
  23.9 17.7 %collective-permute-start.10 = (bf16[4,96,512]{2,1,0:T(8,128)(2,1)S(1)}, bf16[4,96,512]{2,1,0:T(8,128)(2,1)S(1)}, u32[]{:S(2)}, u32[]{:S(2)}) collective-permute-start(bf16[4,96,512]{2,1,0:T(8,128)(2,1)S(1)} %far.4.refs_4_), channel_id=1, source_target_pairs={{0,4},{1,5},{2,6},{3,7},{4,0},{5,1},{6,2},{7,3},{8,12},{9,13},{10,... | collective-permute-start | bytes 1179656 | tf_op jit(solution)/shard_map/ppermute | solution.py:543
  25.4 1.5 %collective-permute-start.3 = (bf16[2,4,32,512]{3,2,1,0:T(8,128)(2,1)S(1)}, bf16[2,4,32,512]{3,2,1,0:T(8,128)(2,1)S(1)}, u32[]{:S(2)}, u32[]{:S(2)}) collective-permute-start(bf16[2,4,32,512]{3,2,1,0:T(8,128)(2,1)S(1)} %get-tuple-element.51.refs_4_), channel_id=1, source_target_pairs={{0,1},{1,0},{2,3},{3,2},{4,5},{5,4},{6,7},{7,6},{8,9},{9,8},{10,11... | collective-permute-start | bytes 786440 | tf_op jit(solution)/shard_map/ppermute | solution.py:543
  25.4 1.9 %collective-permute-start.4 = (bf16[2,4,32,512]{3,2,1,0:T(8,128)(2,1)S(1)}, bf16[2,4,32,512]{3,2,1,0:T(8,128)(2,1)S(1)}, u32[]{:S(2)}, u32[]{:S(2)}) collective-permute-start(bf16[2,4,32,512]{3,2,1,0:T(8,128)(2,1)S(1)} %get-tuple-element.52), channel_id=1, source_target_pairs={{0,1},{1,0},{2,3},{3,2},{4,5},{5,4},{6,7},{7,6},{8,9},{9,8},{10,11... | collective-permute-start | bytes 786440 | tf_op jit(solution)/shard_map/ppermute | solution.py:543
  27.4 22.4 %collective-permute-start.5 = (bf16[2,4,32,512]{3,2,1,0:T(8,128)(2,1)S(1)}, bf16[2,4,32,512]{3,2,1,0:T(8,128)(2,1)S(1)}, u32[]{:S(2)}, u32[]{:S(2)}) collective-permute-start(bf16[2,4,32,512]{3,2,1,0:T(8,128)(2,1)S(1)} %get-tuple-element.54), channel_id=1, source_target_pairs={{0,4},{1,5},{2,6},{3,7},{4,0},{5,1},{6,2},{7,3},{8,12},{9,13},{10,... | collective-permute-start | bytes 786440 | tf_op jit(solution)/shard_map/ppermute | solution.py:543
  27.9 21.9 %collective-permute-start.6 = (bf16[2,4,32,512]{3,2,1,0:T(8,128)(2,1)S(1)}, bf16[2,4,32,512]{3,2,1,0:T(8,128)(2,1)S(1)}, u32[]{:S(2)}, u32[]{:S(2)}) collective-permute-start(bf16[2,4,32,512]{3,2,1,0:T(8,128)(2,1)S(1)} %get-tuple-element.55), channel_id=1, source_target_pairs={{0,8},{1,9},{2,10},{3,11},{4,12},{5,13},{6,14},{7,15},{8,0},{9,1},... | collective-permute-start | bytes 786440 | tf_op jit(solution)/shard_map/ppermute | solution.py:543
  35.9 18.9 %collective-permute-start.7 = (bf16[2,4,32,512]{3,2,1,0:T(8,128)(2,1)S(1)}, bf16[2,4,32,512]{3,2,1,0:T(8,128)(2,1)S(1)}, u32[]{:S(2)}, u32[]{:S(2)}) collective-permute-start(bf16[2,4,32,512]{3,2,1,0:T(8,128)(2,1)S(1)} %get-tuple-element.56), channel_id=1, source_target_pairs={{0,12},{1,13},{2,14},{3,15},{4,8},{5,9},{6,10},{7,11},{8,4},{9,5},... | collective-permute-start | bytes 786440 | tf_op jit(solution)/shard_map/ppermute | solution.py:543
  41.5 21.4 %collective-permute-start.15 = (bf16[4,128,512]{2,1,0:T(8,128)(2,1)S(1)}, bf16[4,128,512]{2,1,0:T(8,128)(2,1)S(1)}, u32[]{:S(2)}, u32[]{:S(2)}) collective-permute-start(bf16[4,128,512]{2,1,0:T(8,128)(2,1)S(1)} %far.6.refs_5_), channel_id=1, source_target_pairs={{0,2},{1,3},{2,0},{3,1},{4,6},{5,7},{6,4},{7,5},{8,10},{9,11},{10,... | collective-permute-start | bytes 1572872 | tf_op jit(solution)/shard_map/ppermute | solution.py:543
  47.9 18.1 %collective-permute-start.14 = (bf16[2,256,512]{2,1,0:T(8,128)(2,1)S(1)}, bf16[2,256,512]{2,1,0:T(8,128)(2,1)S(1)}, u32[]{:S(2)}, u32[]{:S(2)}) collective-permute-start(bf16[2,256,512]{2,1,0:T(8,128)(2,1)S(1)} %get-tuple-element.64), channel_id=1, source_target_pairs={{0,4},{1,5},{2,6},{3,7},{4,0},{5,1},{6,2},{7,3},{8,12},{9,13},{10,... | collective-permute-start | bytes 1572872 | tf_op jit(solution)/shard_map/ppermute | solution.py:543
  56.4 1.3 %collective-permute-start.11 = (bf16[2,128,128]{2,1,0:T(8,128)(2,1)S(1)}, bf16[2,128,128]{2,1,0:T(8,128)(2,1)S(1)}, u32[]{:S(2)}, u32[]{:S(2)}) collective-permute-start(bf16[2,128,128]{2,1,0:T(8,128)(2,1)S(1)} %get-tuple-element.59), channel_id=1, source_target_pairs={{0,1},{1,0},{2,3},{3,2},{4,5},{5,4},{6,7},{7,6},{8,9},{9,8},{10,11... | collective-permute-start | bytes 196616 | tf_op jit(solution)/shard_map/ppermute | solution.py:543
  57.7 4.0 %collective-permute-start.12 = (bf16[128,128]{1,0:T(8,128)(2,1)S(1)}, bf16[128,128]{1,0:T(8,128)(2,1)S(1)}, u32[]{:S(2)}, u32[]{:S(2)}) collective-permute-start(bf16[128,128]{1,0:T(8,128)(2,1)S(1)} %get-tuple-element.61.refs_2_), channel_id=1, source_target_pairs={{0,16},{16,0},{1,17},{17,1},{2,18},{18,2},{3,19},{19,3},{4,20},{20... | collective-permute-start | bytes 98312 | tf_op jit(solution)/shard_map/ppermute | solution.py:543
  61.7 30.7 %collective-permute-start.22 = (bf16[16,32,512]{2,1,0:T(8,128)(2,1)S(1)}, bf16[16,32,512]{2,1,0:T(8,128)(2,1)S(1)}, u32[]{:S(2)}, u32[]{:S(2)}) collective-permute-start(bf16[16,32,512]{2,1,0:T(8,128)(2,1)S(1)} %expanding.1.refs_5_.refs_3_), channel_id=1, source_target_pairs={{0,16},{16,0},{1,17},{17,1},{2,18},{18,2},{3,19},{19,3},{4,20},{20... | collective-permute-start | bytes 1572872 | tf_op jit(solution)/shard_map/ppermute | solution.py:543
  62.9 6.5 %collective-permute-start.13 = (bf16[4,48,512]{2,1,0:T(8,128)(2,1)S(1)}, bf16[4,48,512]{2,1,0:T(8,128)(2,1)S(1)}, u32[]{:S(2)}, u32[]{:S(2)}) collective-permute-start(bf16[4,48,512]{2,1,0:T(8,128)(2,1)S(1)} %far.7.refs_5_), channel_id=1, source_target_pairs={{0,2},{1,3},{2,0},{3,1},{4,6},{5,7},{6,4},{7,5},{8,10},{9,11},{10,... | collective-permute-start | bytes 589832 | tf_op jit(solution)/shard_map/ppermute | solution.py:543
  63.7 15.2 %collective-permute-start.19 = (bf16[2,128,512]{2,1,0:T(8,128)(2,1)S(1)}, bf16[2,128,512]{2,1,0:T(8,128)(2,1)S(1)}, u32[]{:S(2)}, u32[]{:S(2)}) collective-permute-start(bf16[2,128,512]{2,1,0:T(8,128)(2,1)S(1)} %get-tuple-element.73), channel_id=1, source_target_pairs={{0,4},{1,5},{2,6},{3,7},{4,0},{5,1},{6,2},{7,3},{8,12},{9,13},{10,... | collective-permute-start | bytes 786440 | tf_op jit(solution)/shard_map/ppermute | solution.py:543
  66.1 12.9 %collective-permute-start.18 = (bf16[1,256,512]{2,1,0:T(8,128)(2,1)S(1)}, bf16[1,256,512]{2,1,0:T(8,128)(2,1)S(1)}, u32[]{:S(2)}, u32[]{:S(2)}) collective-permute-start(bf16[1,256,512]{2,1,0:T(8,128)(2,1)S(1)} %get-tuple-element.72), channel_id=1, source_target_pairs={{0,8},{1,9},{2,10},{3,11},{4,12},{5,13},{6,14},{7,15},{8,0},{9,1},... | collective-permute-start | bytes 786440 | tf_op jit(solution)/shard_map/ppermute | solution.py:543
  67.8 11.2 %collective-permute-start.17 = (bf16[2,96,512]{2,1,0:T(8,128)(2,1)S(1)}, bf16[2,96,512]{2,1,0:T(8,128)(2,1)S(1)}, u32[]{:S(2)}, u32[]{:S(2)}) collective-permute-start(bf16[2,96,512]{2,1,0:T(8,128)(2,1)S(1)} %get-tuple-element.71), channel_id=1, source_target_pairs={{0,2},{1,3},{2,0},{3,1},{4,6},{5,7},{6,4},{7,5},{8,10},{9,11},{10,... | collective-permute-start | bytes 589832 | tf_op jit(solution)/shard_map/ppermute | solution.py:543
  70.2 10.3 %collective-permute-start.16 = (bf16[2,64,512]{2,1,0:T(8,128)(2,1)S(1)}, bf16[2,64,512]{2,1,0:T(8,128)(2,1)S(1)}, u32[]{:S(2)}, u32[]{:S(2)}) collective-permute-start(bf16[2,64,512]{2,1,0:T(8,128)(2,1)S(1)} %get-tuple-element.69), channel_id=1, source_target_pairs={{0,4},{1,5},{2,6},{3,7},{4,0},{5,1},{6,2},{7,3},{8,12},{9,13},{10,... | collective-permute-start | bytes 393224 | tf_op jit(solution)/shard_map/ppermute | solution.py:543
  78.9 12.4 %collective-permute-start.21 = (bf16[1,128,512]{2,1,0:T(8,128)(2,1)S(1)}, bf16[1,128,512]{2,1,0:T(8,128)(2,1)S(1)}, u32[]{:S(2)}, u32[]{:S(2)}) collective-permute-start(bf16[1,128,512]{2,1,0:T(8,128)(2,1)S(1)} %get-tuple-element.78), channel_id=1, source_target_pairs={{0,8},{1,9},{2,10},{3,11},{4,12},{5,13},{6,14},{7,15},{8,0},{9,1},... | collective-permute-start | bytes 393224 | tf_op jit(solution)/shard_map/ppermute | solution.py:543
  80.6 11.8 %collective-permute-start.20 = (bf16[1,96,512]{2,1,0:T(8,128)(2,1)S(1)}, bf16[1,96,512]{2,1,0:T(8,128)(2,1)S(1)}, u32[]{:S(2)}, u32[]{:S(2)}) collective-permute-start(bf16[1,96,512]{2,1,0:T(8,128)(2,1)S(1)} %get-tuple-element.77), channel_id=1, source_target_pairs={{0,8},{1,9},{2,10},{3,11},{4,12},{5,13},{6,14},{7,15},{8,0},{9,1},... | collective-permute-start | bytes 294920 | tf_op jit(solution)/shard_map/ppermute | solution.py:543
  84.5 8.9 %collective-permute-start.23 = (bf16[1,96,512]{2,1,0:T(8,128)(2,1)S(1)}, bf16[1,96,512]{2,1,0:T(8,128)(2,1)S(1)}, u32[]{:S(2)}, u32[]{:S(2)}) collective-permute-start(bf16[1,96,512]{2,1,0:T(8,128)(2,1)S(1)} %get-tuple-element.82), channel_id=1, source_target_pairs={{0,8},{1,9},{2,10},{3,11},{4,12},{5,13},{6,14},{7,15},{8,0},{9,1},... | collective-permute-start | bytes 294920 | tf_op jit(solution)/shard_map/ppermute | solution.py:543
  (2 other events, 11.8 us)

commit v7 on v6

--- a/solution.py
+++ b/solution.py
@@ -34,13 +34,13 @@
     "end0",
     "near3",
     "near2",
+    "end2",
     "end1",
     "fold0",
     "end3",
-    "end2",
-    "fold1",
     "ranks",
     "expand",
+    "fold1",
     "fold3",
 )
 PLAIN_STEPS = ("side", "sort", "shrink", "core", "cross", "far0", "near0", "end0", "ranks", "expanding", "expand")

time: 94.5 us -> 96.4 us (1.020)
  starting transfers between devices: 29.6 us -> 31.2 us
    ppermute x24, starting transfers between devices: 29.6 us -> 31.2 us  [swap(): return lax.ppermute(array, axis, [(i, i ^ bit) for i in range(size)])]
  transfers between devices with their start and end apart: 24 -> 24, of which waited for: 14 -> 13; matrix products, arithmetic and copies ran while one was open for 0% -> 0% of each run, Pallas kernels for 12% -> 12%
where the time goes in v7:
time: 96.4 us; the launch traced here: 96.3 us
  waiting for transfers between devices  47.7 us (49%)
  starting transfers between devices  31.2 us (32%)
  Pallas kernels  17.1 us (18%)
    ppermute x24, waiting for transfers between devices, swap(): return lax.ppermute(array, axis, [(i, i ^ bit) for i in range(size)])  47.7 us
    ppermute x24, starting transfers between devices, swap(): return lax.ppermute(array, axis, [(i, i ^ bit) for i in range(size)])  31.2 us
    pallas_call x25, Pallas kernels, call(): pl.pallas_call(run, in_specs=[pl.BlockSpec(memory_space=pltpu.VMEM)] * le...  16.2 us
  transfers between devices with their start and end apart: 24, of which 13 were waited for; matrix products, arithmetic and copies ran while one was open for 0% of the time, Pallas kernels for 12%

profile of v7, /device:TPU:0, one launch (start us, length us, event | category | flops | bytes accessed | tf_op | source)
XLA Modules:
  0.0 96.3 jit_solution(3174664691356405614)
XLA Ops:
  0.0 2.8 %pick.1 = (bf16[8,512,512]{2,1,0:T(8,128)(2,1)S(1)}, bf16[2,2,4,32,512]{4,3,2,1,0:T(8,128)(2,1)S(1)}, bf16[2,2,4,32,512]{4,3,2,1,0:T(8,128)(2,1)S(1)}) custom-call(bf16[512,8192]{1,0:T(8,128)(2,1)} %refs_7_.1, bf16[1,64,8192]{2,1,0:T(8,128)(2,1)} %refs_1_.1, bf16[1,64,8192]{2,1,0:T(8,128)(2,1)} %refs_2_.2), custom_call_target="tpu_custom_call" | custom-call | bytes 65536 | tf_op jit(solution)/shard_map/pick/pallas_call | solution.py:58
  3.3 2.6 %collective-permute-start.2 = (bf16[2,2,4,32,512]{4,3,2,1,0:T(8,128)(2,1)S(1)}, bf16[2,2,4,32,512]{4,3,2,1,0:T(8,128)(2,1)S(1)}, u32[]{:S(2)}, u32[]{:S(2)}) collective-permute-start(bf16[2,2,4,32,512]{4,3,2,1,0:T(8,128)(2,1)S(1)} %get-tuple-element.49), channel_id=1, source_target_pairs={{0,2},{1,3},{2,0},{3,1},{4,6},{5,7},{6,4},{7,5},{8,10},{9,11},{10,... | collective-permute-start | bytes 1572872 | tf_op jit(solution)/shard_map/ppermute | solution.py:543
  5.9 3.4 %attention.1 = (bf16[528,512]{1,0:T(8,128)(2,1)S(1)}, bf16[8,512,512]{2,1,0:T(8,128)(2,1)S(1)}, bf16[512,512]{1,0:T(8,128)(2,1)S(1)}) custom-call(s32[1,128]{1,0:T(1,128)S(1)} %bitcast.6, s32[1,128]{1,0:T(1,128)S(1)} %bitcast.5, bf16[4,128,512]{2,1,0:T(8,128)(2,1)} %refs_2_.3, bf16[12,128,1024]{2,1,0:T(8,128)(2,1)} %bitcast.7, ...), custom_call_target="tpu_custom_call" | custom-call | flops 268435456 | bytes 65536 | tf_op jit(solution)/shard_map/attention/pallas_call | solution.py:58
  9.5 8.9 %collective-permute-done.2.refs_1_ = bf16[2,2,4,32,512]{4,3,2,1,0:T(8,128)(2,1)S(1)} collective-permute-done((bf16[2,2,4,32,512]{4,3,2,1,0:T(8,128)(2,1)S(1)}, bf16[2,2,4,32,512]{4,3,2,1,0:T(8,128)(2,1)S(1)}, u32[]{:S(2)}, u32[]{:S(2)}) %collective-permute-start.2) | collective-permute-done | bytes 524320 | tf_op jit(solution)/shard_map/ppermute | solution.py:543
  20.5 1.8 %collective-permute-start.9 = (bf16[4,256,512]{2,1,0:T(8,128)(2,1)S(1)}, bf16[4,256,512]{2,1,0:T(8,128)(2,1)S(1)}, u32[]{:S(2)}, u32[]{:S(2)}) collective-permute-start(bf16[4,256,512]{2,1,0:T(8,128)(2,1)S(1)} %far.5.refs_3_), channel_id=1, source_target_pairs={{0,2},{1,3},{2,0},{3,1},{4,6},{5,7},{6,4},{7,5},{8,10},{9,11},{10,... | collective-permute-start | bytes 3145736 | tf_op jit(solution)/shard_map/ppermute | solution.py:543
  22.4 1.5 %collective-permute-start.8 = (bf16[528,512]{1,0:T(8,128)(2,1)S(1)}, bf16[528,512]{1,0:T(8,128)(2,1)S(1)}, u32[]{:S(2)}, u32[]{:S(2)}) collective-permute-start(bf16[528,512]{1,0:T(8,128)(2,1)S(1)} %get-tuple-element.45.refs_0_.refs_4_), channel_id=1, source_target_pairs={{0,16},{16,0},{1,17},{17,1},{2,18},{18,2},{3,19},{19,3},{4,20},{20... | collective-permute-start | bytes 1622024 | tf_op jit(solution)/shard_map/ppermute | solution.py:543
  23.9 1.6 %collective-permute-start.10 = (bf16[4,96,512]{2,1,0:T(8,128)(2,1)S(1)}, bf16[4,96,512]{2,1,0:T(8,128)(2,1)S(1)}, u32[]{:S(2)}, u32[]{:S(2)}) collective-permute-start(bf16[4,96,512]{2,1,0:T(8,128)(2,1)S(1)} %far.4.refs_4_), channel_id=1, source_target_pairs={{0,4},{1,5},{2,6},{3,7},{4,0},{5,1},{6,2},{7,3},{8,12},{9,13},{10,... | collective-permute-start | bytes 1179656 | tf_op jit(solution)/shard_map/ppermute | solution.py:543
  27.9 2.6 %collective-permute-start.6 = (bf16[2,4,32,512]{3,2,1,0:T(8,128)(2,1)S(1)}, bf16[2,4,32,512]{3,2,1,0:T(8,128)(2,1)S(1)}, u32[]{:S(2)}, u32[]{:S(2)}) collective-permute-start(bf16[2,4,32,512]{3,2,1,0:T(8,128)(2,1)S(1)} %get-tuple-element.55), channel_id=1, source_target_pairs={{0,8},{1,9},{2,10},{3,11},{4,12},{5,13},{6,14},{7,15},{8,0},{9,1},... | collective-permute-start | bytes 786440 | tf_op jit(solution)/shard_map/ppermute | solution.py:543
  30.5 5.4 %collective-permute-done.8.refs_5_ = bf16[528,512]{1,0:T(8,128)(2,1)S(1)} collective-permute-done((bf16[528,512]{1,0:T(8,128)(2,1)S(1)}, bf16[528,512]{1,0:T(8,128)(2,1)S(1)}, u32[]{:S(2)}, u32[]{:S(2)}) %collective-permute-start.8) | collective-permute-done | bytes 540704 | tf_op jit(solution)/shard_map/ppermute | solution.py:543
  35.9 3.6 %collective-permute-start.7 = (bf16[2,4,32,512]{3,2,1,0:T(8,128)(2,1)S(1)}, bf16[2,4,32,512]{3,2,1,0:T(8,128)(2,1)S(1)}, u32[]{:S(2)}, u32[]{:S(2)}) collective-permute-start(bf16[2,4,32,512]{3,2,1,0:T(8,128)(2,1)S(1)} %get-tuple-element.56), channel_id=1, source_target_pairs={{0,12},{1,13},{2,14},{3,15},{4,8},{5,9},{6,10},{7,11},{8,4},{9,5},... | collective-permute-start | bytes 786440 | tf_op jit(solution)/shard_map/ppermute | solution.py:543
  40.2 1.3 %collective-permute-done.10.refs_6_.refs_4_ = bf16[4,96,512]{2,1,0:T(8,128)(2,1)S(1)} collective-permute-done((bf16[4,96,512]{2,1,0:T(8,128)(2,1)S(1)}, bf16[4,96,512]{2,1,0:T(8,128)(2,1)S(1)}, u32[]{:S(2)}, u32[]{:S(2)}) %collective-permute-start.10) | collective-permute-done | bytes 393248 | tf_op jit(solution)/shard_map/ppermute | solution.py:543
  42.0 4.6 %collective-permute-done.9.refs_4_ = bf16[4,256,512]{2,1,0:T(8,128)(2,1)S(1)} collective-permute-done((bf16[4,256,512]{2,1,0:T(8,128)(2,1)S(1)}, bf16[4,256,512]{2,1,0:T(8,128)(2,1)S(1)}, u32[]{:S(2)}, u32[]{:S(2)}) %collective-permute-start.9) | collective-permute-done | bytes 1048608 | tf_op jit(solution)/shard_map/ppermute | solution.py:543
  47.9 1.9 %collective-permute-start.14 = (bf16[2,256,512]{2,1,0:T(8,128)(2,1)S(1)}, bf16[2,256,512]{2,1,0:T(8,128)(2,1)S(1)}, u32[]{:S(2)}, u32[]{:S(2)}) collective-permute-start(bf16[2,256,512]{2,1,0:T(8,128)(2,1)S(1)} %get-tuple-element.64), channel_id=1, source_target_pairs={{0,4},{1,5},{2,6},{3,7},{4,0},{5,1},{6,2},{7,3},{8,12},{9,13},{10,... | collective-permute-start | bytes 1572872 | tf_op jit(solution)/shard_map/ppermute | solution.py:543
  49.8 5.0 %collective-permute-done.7.refs_3_ = bf16[2,4,32,512]{3,2,1,0:T(8,128)(2,1)S(1)} collective-permute-done((bf16[2,4,32,512]{3,2,1,0:T(8,128)(2,1)S(1)}, bf16[2,4,32,512]{3,2,1,0:T(8,128)(2,1)S(1)}, u32[]{:S(2)}, u32[]{:S(2)}) %collective-permute-start.7) | collective-permute-done | bytes 262176 | tf_op jit(solution)/shard_map/ppermute | solution.py:543
  54.8 1.5 %shrink.1 = (f32[2,128,128]{2,1,0:T(8,128)S(1)}, bf16[2,128,128]{2,1,0:T(8,128)(2,1)S(1)}) custom-call(bf16[2,4,32,512]{3,2,1,0:T(8,128)(2,1)S(1)} %get-tuple-element.53.refs_4_.refs_0_, bf16[2,4,32,512]{3,2,1,0:T(8,128)(2,1)S(1)} %collective-permute-done.5.refs_1_, bf16[2,4,32,512]{3,2,1,0:T(8,128)(2,1)S(1)} %collective-permute-done.6.refs_2_, ...), custom_call_target="tpu_custom_call" | custom-call | flops 1073741824 | bytes 65536 | tf_op jit(solution)/shard_map/shrink/pallas_call | solution.py:58
  58.1 3.6 %collective-permute-done.12.refs_1_ = bf16[128,128]{1,0:T(8,128)(2,1)S(1)} collective-permute-done((bf16[128,128]{1,0:T(8,128)(2,1)S(1)}, bf16[128,128]{1,0:T(8,128)(2,1)S(1)}, u32[]{:S(2)}, u32[]{:S(2)}) %collective-permute-start.12) | collective-permute-done | bytes 32800 | tf_op jit(solution)/shard_map/ppermute | solution.py:543
  63.7 2.3 %collective-permute-start.20 = (bf16[2,128,512]{2,1,0:T(8,128)(2,1)S(1)}, bf16[2,128,512]{2,1,0:T(8,128)(2,1)S(1)}, u32[]{:S(2)}, u32[]{:S(2)}) collective-permute-start(bf16[2,128,512]{2,1,0:T(8,128)(2,1)S(1)} %get-tuple-element.75), channel_id=1, source_target_pairs={{0,4},{1,5},{2,6},{3,7},{4,0},{5,1},{6,2},{7,3},{8,12},{9,13},{10,... | collective-permute-start | bytes 786440 | tf_op jit(solution)/shard_map/ppermute | solution.py:543
  67.8 1.6 %collective-permute-start.18 = (bf16[2,96,512]{2,1,0:T(8,128)(2,1)S(1)}, bf16[2,96,512]{2,1,0:T(8,128)(2,1)S(1)}, u32[]{:S(2)}, u32[]{:S(2)}) collective-permute-start(bf16[2,96,512]{2,1,0:T(8,128)(2,1)S(1)} %get-tuple-element.73), channel_id=1, source_target_pairs={{0,2},{1,3},{2,0},{3,1},{4,6},{5,7},{6,4},{7,5},{8,10},{9,11},{10,... | collective-permute-start | bytes 589832 | tf_op jit(solution)/shard_map/ppermute | solution.py:543
  70.2 2.0 %collective-permute-start.16 = (bf16[2,64,512]{2,1,0:T(8,128)(2,1)S(1)}, bf16[2,64,512]{2,1,0:T(8,128)(2,1)S(1)}, u32[]{:S(2)}, u32[]{:S(2)}) collective-permute-start(bf16[2,64,512]{2,1,0:T(8,128)(2,1)S(1)} %get-tuple-element.69), channel_id=1, source_target_pairs={{0,4},{1,5},{2,6},{3,7},{4,0},{5,1},{6,2},{7,3},{8,12},{9,13},{10,... | collective-permute-start | bytes 393224 | tf_op jit(solution)/shard_map/ppermute | solution.py:543
  72.2 7.4 %collective-permute-done.16.refs_1_ = bf16[2,64,512]{2,1,0:T(8,128)(2,1)S(1)} collective-permute-done((bf16[2,64,512]{2,1,0:T(8,128)(2,1)S(1)}, bf16[2,64,512]{2,1,0:T(8,128)(2,1)S(1)}, u32[]{:S(2)}, u32[]{:S(2)}) %collective-permute-start.16) | collective-permute-done | bytes 131104 | tf_op jit(solution)/shard_map/ppermute | solution.py:543
  79.7 2.7 %collective-permute-start.17 = (bf16[1,96,512]{2,1,0:T(8,128)(2,1)S(1)}, bf16[1,96,512]{2,1,0:T(8,128)(2,1)S(1)}, u32[]{:S(2)}, u32[]{:S(2)}) collective-permute-start(bf16[1,96,512]{2,1,0:T(8,128)(2,1)S(1)} %get-tuple-element.72), channel_id=1, source_target_pairs={{0,8},{1,9},{2,10},{3,11},{4,12},{5,13},{6,14},{7,15},{8,0},{9,1},... | collective-permute-start | bytes 294920 | tf_op jit(solution)/shard_map/ppermute | solution.py:543
  82.9 2.7 %collective-permute-start.23 = (bf16[1,96,512]{2,1,0:T(8,128)(2,1)S(1)}, bf16[1,96,512]{2,1,0:T(8,128)(2,1)S(1)}, u32[]{:S(2)}, u32[]{:S(2)}) collective-permute-start(bf16[1,96,512]{2,1,0:T(8,128)(2,1)S(1)} %get-tuple-element.82), channel_id=1, source_target_pairs={{0,8},{1,9},{2,10},{3,11},{4,12},{5,13},{6,14},{7,15},{8,0},{9,1},... | collective-permute-start | bytes 294920 | tf_op jit(solution)/shard_map/ppermute | solution.py:543
  85.7 5.9 %collective-permute-done.17.refs_1_.refs_4_ = bf16[1,96,512]{2,1,0:T(8,128)(2,1)S(1)} collective-permute-done((bf16[1,96,512]{2,1,0:T(8,128)(2,1)S(1)}, bf16[1,96,512]{2,1,0:T(8,128)(2,1)S(1)}, u32[]{:S(2)}, u32[]{:S(2)}) %collective-permute-start.17) | collective-permute-done | bytes 98336 | tf_op jit(solution)/shard_map/ppermute | solution.py:543
  92.4 1.9 %collective-permute-done.22.refs_1_ = bf16[1,128,512]{2,1,0:T(8,128)(2,1)S(1)} collective-permute-done((bf16[1,128,512]{2,1,0:T(8,128)(2,1)S(1)}, bf16[1,128,512]{2,1,0:T(8,128)(2,1)S(1)}, u32[]{:S(2)}, u32[]{:S(2)}) %collective-permute-start.22) | collective-permute-done | bytes 131104 | tf_op jit(solution)/shard_map/ppermute | solution.py:543
  (55 shorter events, 17.6 us)
Async XLA Ops:
  2.8 15.7 %collective-permute-start.1 = (bf16[8,512,512]{2,1,0:T(8,128)(2,1)S(1)}, bf16[8,512,512]{2,1,0:T(8,128)(2,1)S(1)}, u32[]{:S(2)}, u32[]{:S(2)}) collective-permute-start(bf16[8,512,512]{2,1,0:T(8,128)(2,1)S(1)} %get-tuple-element.48), channel_id=1, source_target_pairs={{0,1},{1,0},{2,3},{3,2},{4,5},{5,4},{6,7},{7,6},{8,9},{9,8},{10,11... | collective-permute-start | bytes 12582920 | tf_op jit(solution)/shard_map/ppermute | solution.py:543
  3.3 15.1 %collective-permute-start.2 = (bf16[2,2,4,32,512]{4,3,2,1,0:T(8,128)(2,1)S(1)}, bf16[2,2,4,32,512]{4,3,2,1,0:T(8,128)(2,1)S(1)}, u32[]{:S(2)}, u32[]{:S(2)}) collective-permute-start(bf16[2,2,4,32,512]{4,3,2,1,0:T(8,128)(2,1)S(1)} %get-tuple-element.49), channel_id=1, source_target_pairs={{0,2},{1,3},{2,0},{3,1},{4,6},{5,7},{6,4},{7,5},{8,10},{9,11},{10,... | collective-permute-start | bytes 1572872 | tf_op jit(solution)/shard_map/ppermute | solution.py:543
  9.3 9.2 %collective-permute-start = (bf16[512,512]{1,0:T(8,128)(2,1)S(1)}, bf16[512,512]{1,0:T(8,128)(2,1)S(1)}, u32[]{:S(2)}, u32[]{:S(2)}) collective-permute-start(bf16[512,512]{1,0:T(8,128)(2,1)S(1)} %get-tuple-element.46.refs_2_), channel_id=1, source_target_pairs={{0,1},{1,0},{2,3},{3,2},{4,5},{5,4},{6,7},{7,6},{8,9},{9,8},{10,11... | collective-permute-start | bytes 1572872 | tf_op jit(solution)/shard_map/ppermute | solution.py:543
  20.5 26.1 %collective-permute-start.9 = (bf16[4,256,512]{2,1,0:T(8,128)(2,1)S(1)}, bf16[4,256,512]{2,1,0:T(8,128)(2,1)S(1)}, u32[]{:S(2)}, u32[]{:S(2)}) collective-permute-start(bf16[4,256,512]{2,1,0:T(8,128)(2,1)S(1)} %far.5.refs_3_), channel_id=1, source_target_pairs={{0,2},{1,3},{2,0},{3,1},{4,6},{5,7},{6,4},{7,5},{8,10},{9,11},{10,... | collective-permute-start | bytes 3145736 | tf_op jit(solution)/shard_map/ppermute | solution.py:543
  22.4 13.6 %collective-permute-start.8 = (bf16[528,512]{1,0:T(8,128)(2,1)S(1)}, bf16[528,512]{1,0:T(8,128)(2,1)S(1)}, u32[]{:S(2)}, u32[]{:S(2)}) collective-permute-start(bf16[528,512]{1,0:T(8,128)(2,1)S(1)} %get-tuple-element.45.refs_0_.refs_4_), channel_id=1, source_target_pairs={{0,16},{16,0},{1,17},{17,1},{2,18},{18,2},{3,19},{19,3},{4,20},{20... | collective-permute-start | bytes 1622024 | tf_op jit(solution)/shard_map/ppermute | solution.py:543
  23.9 17.7 %collective-permute-start.10 = (bf16[4,96,512]{2,1,0:T(8,128)(2,1)S(1)}, bf16[4,96,512]{2,1,0:T(8,128)(2,1)S(1)}, u32[]{:S(2)}, u32[]{:S(2)}) collective-permute-start(bf16[4,96,512]{2,1,0:T(8,128)(2,1)S(1)} %far.4.refs_4_), channel_id=1, source_target_pairs={{0,4},{1,5},{2,6},{3,7},{4,0},{5,1},{6,2},{7,3},{8,12},{9,13},{10,... | collective-permute-start | bytes 1179656 | tf_op jit(solution)/shard_map/ppermute | solution.py:543
  25.4 1.5 %collective-permute-start.3 = (bf16[2,4,32,512]{3,2,1,0:T(8,128)(2,1)S(1)}, bf16[2,4,32,512]{3,2,1,0:T(8,128)(2,1)S(1)}, u32[]{:S(2)}, u32[]{:S(2)}) collective-permute-start(bf16[2,4,32,512]{3,2,1,0:T(8,128)(2,1)S(1)} %get-tuple-element.51.refs_4_), channel_id=1, source_target_pairs={{0,1},{1,0},{2,3},{3,2},{4,5},{5,4},{6,7},{7,6},{8,9},{9,8},{10,11... | collective-permute-start | bytes 786440 | tf_op jit(solution)/shard_map/ppermute | solution.py:543
  25.4 1.9 %collective-permute-start.4 = (bf16[2,4,32,512]{3,2,1,0:T(8,128)(2,1)S(1)}, bf16[2,4,32,512]{3,2,1,0:T(8,128)(2,1)S(1)}, u32[]{:S(2)}, u32[]{:S(2)}) collective-permute-start(bf16[2,4,32,512]{3,2,1,0:T(8,128)(2,1)S(1)} %get-tuple-element.52), channel_id=1, source_target_pairs={{0,1},{1,0},{2,3},{3,2},{4,5},{5,4},{6,7},{7,6},{8,9},{9,8},{10,11... | collective-permute-start | bytes 786440 | tf_op jit(solution)/shard_map/ppermute | solution.py:543
  27.4 22.4 %collective-permute-start.5 = (bf16[2,4,32,512]{3,2,1,0:T(8,128)(2,1)S(1)}, bf16[2,4,32,512]{3,2,1,0:T(8,128)(2,1)S(1)}, u32[]{:S(2)}, u32[]{:S(2)}) collective-permute-start(bf16[2,4,32,512]{3,2,1,0:T(8,128)(2,1)S(1)} %get-tuple-element.54), channel_id=1, source_target_pairs={{0,4},{1,5},{2,6},{3,7},{4,0},{5,1},{6,2},{7,3},{8,12},{9,13},{10,... | collective-permute-start | bytes 786440 | tf_op jit(solution)/shard_map/ppermute | solution.py:543
  27.9 21.9 %collective-permute-start.6 = (bf16[2,4,32,512]{3,2,1,0:T(8,128)(2,1)S(1)}, bf16[2,4,32,512]{3,2,1,0:T(8,128)(2,1)S(1)}, u32[]{:S(2)}, u32[]{:S(2)}) collective-permute-start(bf16[2,4,32,512]{3,2,1,0:T(8,128)(2,1)S(1)} %get-tuple-element.55), channel_id=1, source_target_pairs={{0,8},{1,9},{2,10},{3,11},{4,12},{5,13},{6,14},{7,15},{8,0},{9,1},... | collective-permute-start | bytes 786440 | tf_op jit(solution)/shard_map/ppermute | solution.py:543
  35.9 18.9 %collective-permute-start.7 = (bf16[2,4,32,512]{3,2,1,0:T(8,128)(2,1)S(1)}, bf16[2,4,32,512]{3,2,1,0:T(8,128)(2,1)S(1)}, u32[]{:S(2)}, u32[]{:S(2)}) collective-permute-start(bf16[2,4,32,512]{3,2,1,0:T(8,128)(2,1)S(1)} %get-tuple-element.56), channel_id=1, source_target_pairs={{0,12},{1,13},{2,14},{3,15},{4,8},{5,9},{6,10},{7,11},{8,4},{9,5},... | collective-permute-start | bytes 786440 | tf_op jit(solution)/shard_map/ppermute | solution.py:543
  41.5 21.4 %collective-permute-start.15 = (bf16[4,128,512]{2,1,0:T(8,128)(2,1)S(1)}, bf16[4,128,512]{2,1,0:T(8,128)(2,1)S(1)}, u32[]{:S(2)}, u32[]{:S(2)}) collective-permute-start(bf16[4,128,512]{2,1,0:T(8,128)(2,1)S(1)} %far.6.refs_5_), channel_id=1, source_target_pairs={{0,2},{1,3},{2,0},{3,1},{4,6},{5,7},{6,4},{7,5},{8,10},{9,11},{10,... | collective-permute-start | bytes 1572872 | tf_op jit(solution)/shard_map/ppermute | solution.py:543
  47.9 18.1 %collective-permute-start.14 = (bf16[2,256,512]{2,1,0:T(8,128)(2,1)S(1)}, bf16[2,256,512]{2,1,0:T(8,128)(2,1)S(1)}, u32[]{:S(2)}, u32[]{:S(2)}) collective-permute-start(bf16[2,256,512]{2,1,0:T(8,128)(2,1)S(1)} %get-tuple-element.64), channel_id=1, source_target_pairs={{0,4},{1,5},{2,6},{3,7},{4,0},{5,1},{6,2},{7,3},{8,12},{9,13},{10,... | collective-permute-start | bytes 1572872 | tf_op jit(solution)/shard_map/ppermute | solution.py:543
  56.4 1.3 %collective-permute-start.11 = (bf16[2,128,128]{2,1,0:T(8,128)(2,1)S(1)}, bf16[2,128,128]{2,1,0:T(8,128)(2,1)S(1)}, u32[]{:S(2)}, u32[]{:S(2)}) collective-permute-start(bf16[2,128,128]{2,1,0:T(8,128)(2,1)S(1)} %get-tuple-element.59), channel_id=1, source_target_pairs={{0,1},{1,0},{2,3},{3,2},{4,5},{5,4},{6,7},{7,6},{8,9},{9,8},{10,11... | collective-permute-start | bytes 196616 | tf_op jit(solution)/shard_map/ppermute | solution.py:543
  57.7 4.0 %collective-permute-start.12 = (bf16[128,128]{1,0:T(8,128)(2,1)S(1)}, bf16[128,128]{1,0:T(8,128)(2,1)S(1)}, u32[]{:S(2)}, u32[]{:S(2)}) collective-permute-start(bf16[128,128]{1,0:T(8,128)(2,1)S(1)} %get-tuple-element.61.refs_2_), channel_id=1, source_target_pairs={{0,16},{16,0},{1,17},{17,1},{2,18},{18,2},{3,19},{19,3},{4,20},{20... | collective-permute-start | bytes 98312 | tf_op jit(solution)/shard_map/ppermute | solution.py:543
  61.7 29.8 %collective-permute-start.21 = (bf16[16,32,512]{2,1,0:T(8,128)(2,1)S(1)}, bf16[16,32,512]{2,1,0:T(8,128)(2,1)S(1)}, u32[]{:S(2)}, u32[]{:S(2)}) collective-permute-start(bf16[16,32,512]{2,1,0:T(8,128)(2,1)S(1)} %expanding.1.refs_5_.refs_3_), channel_id=1, source_target_pairs={{0,16},{16,0},{1,17},{17,1},{2,18},{18,2},{3,19},{19,3},{4,20},{20... | collective-permute-start | bytes 1572872 | tf_op jit(solution)/shard_map/ppermute | solution.py:543
  62.9 6.5 %collective-permute-start.13 = (bf16[4,48,512]{2,1,0:T(8,128)(2,1)S(1)}, bf16[4,48,512]{2,1,0:T(8,128)(2,1)S(1)}, u32[]{:S(2)}, u32[]{:S(2)}) collective-permute-start(bf16[4,48,512]{2,1,0:T(8,128)(2,1)S(1)} %far.7.refs_5_), channel_id=1, source_target_pairs={{0,2},{1,3},{2,0},{3,1},{4,6},{5,7},{6,4},{7,5},{8,10},{9,11},{10,... | collective-permute-start | bytes 589832 | tf_op jit(solution)/shard_map/ppermute | solution.py:543
  63.7 18.7 %collective-permute-start.20 = (bf16[2,128,512]{2,1,0:T(8,128)(2,1)S(1)}, bf16[2,128,512]{2,1,0:T(8,128)(2,1)S(1)}, u32[]{:S(2)}, u32[]{:S(2)}) collective-permute-start(bf16[2,128,512]{2,1,0:T(8,128)(2,1)S(1)} %get-tuple-element.75), channel_id=1, source_target_pairs={{0,4},{1,5},{2,6},{3,7},{4,0},{5,1},{6,2},{7,3},{8,12},{9,13},{10,... | collective-permute-start | bytes 786440 | tf_op jit(solution)/shard_map/ppermute | solution.py:543
  66.1 16.7 %collective-permute-start.19 = (bf16[1,256,512]{2,1,0:T(8,128)(2,1)S(1)}, bf16[1,256,512]{2,1,0:T(8,128)(2,1)S(1)}, u32[]{:S(2)}, u32[]{:S(2)}) collective-permute-start(bf16[1,256,512]{2,1,0:T(8,128)(2,1)S(1)} %get-tuple-element.74), channel_id=1, source_target_pairs={{0,8},{1,9},{2,10},{3,11},{4,12},{5,13},{6,14},{7,15},{8,0},{9,1},... | collective-permute-start | bytes 786440 | tf_op jit(solution)/shard_map/ppermute | solution.py:543
  67.8 15.0 %collective-permute-start.18 = (bf16[2,96,512]{2,1,0:T(8,128)(2,1)S(1)}, bf16[2,96,512]{2,1,0:T(8,128)(2,1)S(1)}, u32[]{:S(2)}, u32[]{:S(2)}) collective-permute-start(bf16[2,96,512]{2,1,0:T(8,128)(2,1)S(1)} %get-tuple-element.73), channel_id=1, source_target_pairs={{0,2},{1,3},{2,0},{3,1},{4,6},{5,7},{6,4},{7,5},{8,10},{9,11},{10,... | collective-permute-start | bytes 589832 | tf_op jit(solution)/shard_map/ppermute | solution.py:543
  70.2 9.4 %collective-permute-start.16 = (bf16[2,64,512]{2,1,0:T(8,128)(2,1)S(1)}, bf16[2,64,512]{2,1,0:T(8,128)(2,1)S(1)}, u32[]{:S(2)}, u32[]{:S(2)}) collective-permute-start(bf16[2,64,512]{2,1,0:T(8,128)(2,1)S(1)} %get-tuple-element.69), channel_id=1, source_target_pairs={{0,4},{1,5},{2,6},{3,7},{4,0},{5,1},{6,2},{7,3},{8,12},{9,13},{10,... | collective-permute-start | bytes 393224 | tf_op jit(solution)/shard_map/ppermute | solution.py:543
  79.7 11.9 %collective-permute-start.17 = (bf16[1,96,512]{2,1,0:T(8,128)(2,1)S(1)}, bf16[1,96,512]{2,1,0:T(8,128)(2,1)S(1)}, u32[]{:S(2)}, u32[]{:S(2)}) collective-permute-start(bf16[1,96,512]{2,1,0:T(8,128)(2,1)S(1)} %get-tuple-element.72), channel_id=1, source_target_pairs={{0,8},{1,9},{2,10},{3,11},{4,12},{5,13},{6,14},{7,15},{8,0},{9,1},... | collective-permute-start | bytes 294920 | tf_op jit(solution)/shard_map/ppermute | solution.py:543
  82.4 11.9 %collective-permute-start.22 = (bf16[1,128,512]{2,1,0:T(8,128)(2,1)S(1)}, bf16[1,128,512]{2,1,0:T(8,128)(2,1)S(1)}, u32[]{:S(2)}, u32[]{:S(2)}) collective-permute-start(bf16[1,128,512]{2,1,0:T(8,128)(2,1)S(1)} %get-tuple-element.81), channel_id=1, source_target_pairs={{0,8},{1,9},{2,10},{3,11},{4,12},{5,13},{6,14},{7,15},{8,0},{9,1},... | collective-permute-start | bytes 393224 | tf_op jit(solution)/shard_map/ppermute | solution.py:543
  82.9 12.5 %collective-permute-start.23 = (bf16[1,96,512]{2,1,0:T(8,128)(2,1)S(1)}, bf16[1,96,512]{2,1,0:T(8,128)(2,1)S(1)}, u32[]{:S(2)}, u32[]{:S(2)}) collective-permute-start(bf16[1,96,512]{2,1,0:T(8,128)(2,1)S(1)} %get-tuple-element.82), channel_id=1, source_target_pairs={{0,8},{1,9},{2,10},{3,11},{4,12},{5,13},{6,14},{7,15},{8,0},{9,1},... | collective-permute-start | bytes 294920 | tf_op jit(solution)/shard_map/ppermute | solution.py:543
  (2 other events, 11.8 us)
